TPU v7x, 256 devices: a whole 4x4x8 slice. The times are simulated.
256 devices in a mesh: face: 4 (over z_hi), blk: 64 (over x, y, z_lo, core).
Axes of the slice: x: 4, y: 4, z: 8 (z_hi: 4, z_lo: 2; z = z_hi * 2 + z_lo), core: 2. Of those that a mesh axis runs over, the one named last changes fastest.
Arguments:
- state: float32 [256, 16, 4, 8, 4, 360], P(('face', 'blk')), may hold values from -6 to 6
- jacobian: float32 [256, 16, 4, 8, 4], P(('face', 'blk')), may hold values from 0.5 to 2
- metric_xx: float32 [256, 16, 4, 8, 4], P(('face', 'blk')), may hold values from 0.5 to 2
- metric_yy: float32 [256, 16, 4, 8, 4], P(('face', 'blk')), may hold values from 0.5 to 2
- metric_xy: float32 [256, 16, 4, 8, 4], P(('face', 'blk')), may hold values from -0.3 to 0.3
Outputs:
- smoothed: float32 [256, 16, 4, 8, 4, 360], P(('face', 'blk'))
All inputs are finite; a program needn't handle non-finite values.
Results may differ from a plain program's by a relative error of at most 0.0001.
Values sent between devices are 32-bit elements; how exact they have to be, the bound alone decides.
No kernel may reach another device: no remote copies, remote signals or barrier semaphores. Data moves between devices by JAX's collectives and lax.ppermute only.
A program may use at most 64 MiB of HBM per device.

v0:
```python
import math

import jax
import jax.numpy as jnp
import numpy as np
from jax import lax
from jax.experimental import pallas as pl
from jax.experimental.pallas import tpu as pltpu
from jax.sharding import PartitionSpec as P

PY = 8
EX = 16
FL = 360
LANES = 384
PTS = 128
HALO = 3
WIDE = EX + 2 * HALO
GROUPS = 3 * HALO + 1
LINE = 25
RIM = 8 * GROUPS
SENT = RIM + 8
REST = 17
TAIL = LANES - FL
AXES = ("face", "blk")
VISCOSITY = 1e-4
F32 = jnp.float32
BF16 = jnp.bfloat16


def gll_tables():
    root = 1.0 / math.sqrt(5.0)
    points = np.array([-1.0, -root, root, 1.0])
    weights = np.array([1.0 / 6.0, 5.0 / 6.0, 5.0 / 6.0, 1.0 / 6.0])
    scales = np.array(
        [np.prod([points[t] - points[o] for o in range(4) if o != t]) for t in range(4)]
    )
    derivative = np.zeros((4, 4))
    for t in range(4):
        for s in range(4):
            if t != s:
                derivative[t, s] = scales[t] / (scales[s] * (points[t] - points[s]))
        derivative[t, t] = -np.sum(derivative[t])
    return weights, derivative


def tables():
    derivative = gll_tables()[1]
    d_x = np.kron(derivative, np.eye(32))
    d_y = np.kron(np.eye(32), derivative)
    share = np.eye(PTS)
    for r in range(PTS):
        if r % 4 == 3 and r % 32 != 31:
            share[r, r + 1] = 1.0
            share[r + 1, r] = 1.0
    left = (-share @ np.concatenate([d_x.T, d_y.T], axis=1)).astype(np.float32)
    ends = np.concatenate([np.r_[32 * i : 32 * i + 4, 32 * i + 28 : 32 * i + 32] for i in range(4)])
    rim = np.zeros((16, 64), np.float32)
    rim[0:4] = left[0::32][:, np.concatenate([ends, PTS + ends])]
    rim[4:8] = left[31::32][:, np.concatenate([ends, PTS + ends])]
    diff = np.stack([d_x, d_y]).astype(np.float32)
    spread_rim = np.zeros((32 * GROUPS, RIM), np.float32)
    spread = np.zeros((32 * GROUPS, 176), np.float32)
    for g in range(GROUPS):
        for ey in range(8):
            for j in range(4):
                k = 3 * ey + j
                row = 32 * g + 4 * ey + j
                if k < 4:
                    spread_rim[row, 8 * g + k] = 1.0
                elif k > 20:
                    spread_rim[row, 8 * g + k - 17] = 1.0
                else:
                    spread[row, REST * g + k - 4] = 1.0

    def pair(a):
        high = a.astype(jnp.bfloat16)
        return np.stack([high, (a - high.astype(np.float32)).astype(jnp.bfloat16)])

    return (
        pair(left),
        pair(rim),
        diff,
        diff[:, ends][:, :, ends],
        spread_rim.astype(jnp.bfloat16),
        spread.astype(jnp.bfloat16),
    )


def halves(value):
    high = value.astype(BF16)
    low = (value - high.astype(F32)).astype(BF16)
    return high, low


def dot(a, b):
    return jnp.dot(a, b, preferred_element_type=F32)


def product(a_hi, a_lo, b):
    b_hi, b_lo = halves(b)
    return dot(a_hi, b_hi) + (dot(a_hi, b_lo) + dot(a_lo, b_hi))


def applied(m_twice, m_lo, value):
    v_hi, v_lo = halves(value)
    return dot(m_twice, jnp.concatenate([v_hi, v_lo], axis=0)) + dot(m_lo, v_hi)


def moved_rows(choice, value):
    a = value.astype(BF16)
    rest = value - a.astype(F32)
    b = rest.astype(BF16)
    c = (rest - b.astype(F32)).astype(BF16)
    return (dot(choice, c) + dot(choice, b)) + dot(choice, a)


def fluxes(diff_ref, fxx, fxy, fyy):
    d_x = diff_ref[0]
    d_y = diff_ref[1]
    return jnp.concatenate([fxx * d_x + fxy * d_y, fxy * d_x + fyy * d_y], axis=0)


def form(left_ref, diff_ref, f):
    return product(left_ref[0], left_ref[1], fluxes(diff_ref, *f))


def geometry(jac_ref, xx_ref, yy_ref, xy_ref):
    ends, inner = (float(w) for w in gll_tables()[0][0:2])
    row = lax.broadcasted_iota(jnp.int32, (PTS, EX), 0)
    along = jnp.where((row < 32) | (row >= 96), ends, inner)
    weight = jac_ref[...] * (along * jnp.where((row % 4 == 0) | (row % 4 == 3), ends, inner))
    f = (weight * xx_ref[...], weight * xy_ref[...], weight * yy_ref[...])
    up = jnp.concatenate([weight[1:], weight[:1]], axis=0)
    down = jnp.concatenate([weight[-1:], weight[:-1]], axis=0)
    mass = weight + jnp.where((row % 4 == 3) & (row % 32 != 31), up, 0.0)
    mass = mass + jnp.where((row % 4 == 0) & (row % 32 != 0), down, 0.0)
    return f, mass


def column(f, c):
    return [t[:, c : c + 1] for t in f]


def fetch(sources, buffers, sems):
    copies = [pltpu.make_async_copy(s, d, sems.at[k]) for k, (s, d) in enumerate(zip(sources, buffers))]
    for copy in copies:
        copy.start()
    return copies


def either(even, a, b):
    return jnp.where(even, a, b)


def side_columns(want_west, u_ref, f, mass, left_ref, diff_ref, rim_out_ref, layers_ref, q_ref, m_ref):
    lane = lax.broadcasted_iota(jnp.int32, (PTS, PTS), 1)
    raw, part = {}, {}
    for k in range(HALO + 1):
        m = form(left_ref, diff_ref, column(f, k))
        m_ref[jnp.where(want_west, k, EX - HALO - 1 + k)] = m
        m_hi, m_lo = halves(m)
        q = product(m_hi, m_lo, u_ref[k].reshape(PTS, FL))
        for i in range(4):
            raw[k, i] = q[32 * i : 32 * i + 32]
            part[k, i] = mass[32 * i : 32 * i + 32, k : k + 1]
    for values in (raw, part):
        for k in range(HALO):
            values[k, 3] = values[k + 1, 0] = values[k, 3] + values[k + 1, 0]
    for k in range(HALO + 1):
        c = jnp.where(want_west, k, EX - HALO - 1 + k)
        for i in range(4):
            q_ref[c, i, :, 0:FL] = raw[k, i]
            q_ref[c, i, :, FL:LANES] = jnp.broadcast_to(part[k, i], (32, TAIL))
    sub = lax.broadcasted_iota(jnp.int32, (8, LANES), 0)
    for g in range(GROUPS):
        k, i = (g // 3, g % 3) if g < GROUPS - 1 else (HALO - 1, 3)
        row = either(want_west, raw[k, i], raw[k + 1, i])
        tail = jnp.broadcast_to(either(want_west, part[k, i], part[k + 1, i]), (32, TAIL))
        for lanes, value in ((slice(0, FL), row), (slice(FL, LANES), tail)):
            rim_out_ref[8 * g : 8 * g + 8, lanes] = jnp.where(sub[:, lanes] < 4, value[0:8], value[24:32])
            layers_ref[32 * g : 32 * g + 32, lanes] = value
    x = jnp.zeros((PTS, PTS), F32)
    for t in range(3):
        for k in range(HALO):
            x = jnp.where(lane == HALO * t + k, either(want_west, f[t][:, k : k + 1], f[t][:, k + 1 : k + 2]), x)
    x = jnp.transpose(x)
    rim_out_ref[RIM:SENT, 0:PTS] = x[0:8]
    rim_out_ref[RIM:SENT, PTS : 2 * PTS] = x[8:16]
    rim_out_ref[RIM:SENT, 2 * PTS :] = jnp.zeros((8, PTS), F32)


def gather_rest(layers_ref, out_ref):
    for g in range(GROUPS):
        for ey in range(1, 7):
            size = 3 if ey < 6 else 2
            to = REST * g + 3 * (ey - 1)
            at = 32 * g + 4 * ey + 1
            out_ref[to : to + size, :] = layers_ref[at : at + size, :]
    out_ref[REST * GROUPS :, :] = jnp.zeros((6, LANES), F32)


def nearest(want_west, t):
    return either(want_west, t[:, 0 : HALO + 1], t[:, EX - HALO - 1 : EX])


def first_kernel(flags_ref, u_hbm, jac_hbm, xx_hbm, yy_hbm, xy_hbm, left_hbm, diff_hbm, rim_out_ref, layers_ref, other_ref, f_ref, mass_ref, left_ref, diff_ref, q_ref, m_ref, u_ref, jac_ref, xx_ref, yy_ref, xy_ref, sems):
    want_west = flags_ref[2] != 0
    size = HALO + 1
    here = jnp.where(want_west, 0, EX - size)
    there = jnp.where(want_west, EX - size, 0)
    copies = fetch(
        (jac_hbm, xx_hbm, yy_hbm, xy_hbm, left_hbm, diff_hbm, u_hbm.at[0, pl.ds(here, size)], u_hbm.at[0, pl.ds(there, size)]),
        (jac_ref, xx_ref, yy_ref, xy_ref, left_ref, diff_ref, u_ref, other_ref),
        sems,
    )
    for copy in copies[:6]:
        copy.wait()
    f, mass = geometry(jac_ref, xx_ref, yy_ref, xy_ref)
    for t in range(3):
        f_ref[t] = f[t]
    mass_ref[...] = mass
    copies[6].wait()
    side_columns(want_west, u_ref, [nearest(want_west, t) for t in f], nearest(want_west, mass), left_ref, diff_ref, rim_out_ref, layers_ref, q_ref, m_ref)
    copies[7].wait()


def other_kernel(flags_ref, u_ref, f_ref, mass_ref, left_ref, diff_ref, q_in, m_in, rim_out_ref, layers_ref, q_ref, m_ref):
    del q_in, m_in
    want_west = flags_ref[2] == 0
    f = [nearest(want_west, f_ref[t]) for t in range(3)]
    side_columns(want_west, u_ref, f, nearest(want_west, mass_ref[...]), left_ref, diff_ref, rim_out_ref, layers_ref, q_ref, m_ref)


def rest_kernel(first_ref, other_ref, one_ref, two_ref):
    gather_rest(first_ref, one_ref)
    gather_rest(other_ref, two_ref)


def end_rows(f):
    return [jnp.concatenate([t[32 * i + a : 32 * i + a + 4] for i in range(4) for a in (0, 28)], axis=0) for t in f]


def rows_kernel(u_hbm, rim_hbm, near_hbm, f_ref, mass_ref, e_ref, south_ref, north_ref, low_ref, high_ref, rim_ref, near_ref, sems):
    copies = fetch(
        (rim_hbm, near_hbm, u_hbm.at[0, :, :, 0], u_hbm.at[0, :, :, 7]), (rim_ref, near_ref, low_ref, high_ref), sems
    )
    for copy in copies[:2]:
        copy.wait()
    f = end_rows([f_ref[t] for t in range(3)])
    for c in range(EX):
        e_ref[c] = form(rim_ref, near_ref, column(f, c))[0:8]
    for copy in copies[2:]:
        copy.wait()
    res = {}
    for c in range(0, EX, 4):
        tiles = [ref[c + k, i] for k in range(4) for i in range(4) for ref in (low_ref, high_ref)]
        r = rim_product([e_ref[c + k] for k in range(4)], jnp.concatenate(tiles, axis=0))
        for k in range(4):
            res[c + k] = r[8 * k : 8 * k + 8]
    mass = mass_ref[...]
    for side, (out, at) in enumerate(((south_ref, 0), (north_ref, 31))):
        for c in range(EX):
            for i in range(4 if c == EX - 1 else 3):
                row = 3 * c + i
                value = res[c][4 * side + i : 4 * side + i + 1]
                part = mass[32 * i + at : 32 * i + at + 1, c : c + 1]
                if i == 0 and c > 0:
                    value = value + res[c - 1][4 * side + 3 : 4 * side + 4]
                    part = part + mass[96 + at : 97 + at, c - 1 : c]
                out[row : row + 1, 0:FL] = value
                out[row : row + 1, FL:LANES] = jnp.broadcast_to(part, (1, TAIL))
        out[49:56, :] = jnp.zeros((7, LANES), F32)


def rim_product(es, value):
    blocks = []
    for k, e in enumerate(es):
        parts = [jnp.zeros((8, 32), F32)] * 4
        parts[k] = e
        blocks.append(jnp.concatenate(parts, axis=1))
    m_hi, m_lo = halves(jnp.concatenate(blocks, axis=0))
    v_hi, v_lo = halves(value)
    both = dot(jnp.concatenate([m_hi, m_lo], axis=0), v_hi)
    return both[0:32] + (both[32:64] + dot(m_hi, v_lo))


def own_kernel(u_hbm, after_ref, f_ref, mass_ref, left_ref, diff_ref, q_in, m_in, q_ref, m_ref, u_ref, sems):
    del after_ref, q_in, m_in
    first, final = HALO + 1, EX - HALO - 2
    copies = fetch(
        [u_hbm.at[0, c : c + 4] for c in range(first, final, 4)], [u_ref.at[c : c + 4] for c in range(0, 8, 4)], sems
    )
    f = [f_ref[t] for t in range(3)]
    mass = mass_ref[...]
    for c in range(first, final + 1):
        m = form(left_ref, diff_ref, column(f, c))
        m_ref[c] = m
        m_hi, m_lo = halves(m)
        if (c - first) % 4 == 0:
            copies[(c - first) // 4].wait()
        q = product(m_hi, m_lo, u_ref[c - first].reshape(PTS, FL))
        for i in range(4):
            q_ref[c, i, :, 0:FL] = q[32 * i : 32 * i + 32]
            q_ref[c, i, :, FL:LANES] = jnp.broadcast_to(mass[32 * i : 32 * i + 32, c : c + 1], (32, TAIL))
        join_own(q_ref, c)
    join_own(q_ref, final + 1)


def join_own(q_ref, c):
    shared = q_ref[c - 1, 3] + q_ref[c, 0]
    q_ref[c - 1, 3] = shared
    q_ref[c, 0] = shared


def merge_kernel(flags_ref, one_ref, two_ref, own_south_ref, own_north_ref, south_ref, north_ref):
    even = flags_ref[2] != 0
    for out, own, at in ((south_ref, own_south_ref, 0), (north_ref, own_north_ref, 7)):
        out[10:57, :] = own[1:48, :]
        for g in range(GROUPS - 1):
            r = 8 * g + at
            out[g : g + 1, :] = either(even, one_ref[r : r + 1, :], two_ref[r : r + 1, :])
            r = 8 * (g + 1) + at
            out[58 + g : 59 + g, :] = either(even, two_ref[r : r + 1, :], one_ref[r : r + 1, :])
        r = 8 * (GROUPS - 1) + at
        out[9:10, :] = either(even, one_ref[r : r + 1, :], two_ref[r : r + 1, :]) + own[0:1, :]
        out[57:58, :] = own[48:49, :] + either(even, two_ref[at : at + 1, :], one_ref[at : at + 1, :])
        out[67:72, :] = jnp.zeros((5, LANES), F32)


def halo_kernel(flags_ref, one_ref, two_ref, left_ref, rim_ref, diff_ref, near_ref, m_ref, e_ref, west_ref, east_ref):
    even = flags_ref[2] != 0
    west_ref[...] = either(even, one_ref[...], two_ref[...])
    east_ref[...] = either(even, two_ref[...], one_ref[...])
    for side, ref in enumerate((west_ref, east_ref)):
        x = jnp.concatenate(
            [ref[RIM:SENT, 0:PTS], ref[RIM:SENT, PTS : 2 * PTS], jnp.zeros((PTS - 16, PTS), F32)], axis=0
        )
        x = jnp.transpose(x)
        for k in range(HALO):
            fs = [x[:, HALO * t + k : HALO * t + k + 1] for t in range(3)]
            m_ref[HALO * side + k] = form(left_ref, diff_ref, fs)
            e_ref[HALO * side + k] = form(rim_ref, near_ref, end_rows(fs))[0:8]


def edge_masks(flags_ref):
    sub = lax.broadcasted_iota(jnp.int32, (8, LANES), 0)
    return (sub == 0) & (flags_ref[0] != 0), (sub == 7) & (flags_ref[1] != 0)


def first_tile(value, south_ref, row, masks):
    return value + jnp.where(masks[0], south_ref[row : row + 1, :], 0.0)


def last_tile(value, north_ref, row, masks):
    return value + jnp.where(masks[1], north_ref[row : row + 1, :], 0.0)


def column_value(part, e, lo, south_ref, north_ref, masks):
    tiles = []
    for i in range(4):
        row = 3 * (e - lo) + i
        tiles.append(first_tile(part(e, i, 0, 8), south_ref, row, masks))
        tiles.append(part(e, i, 8, 24))
        tiles.append(last_tile(part(e, i, 24, 32), north_ref, row, masks))
    return jnp.concatenate(tiles, axis=0)


def rim_value(part, e, lo, south_ref, north_ref, masks):
    tiles = []
    for i in range(4):
        row = 3 * (e - lo) + i
        tiles.append(last_tile(first_tile(part(e, i), south_ref, row, masks), north_ref, row, masks))
    return jnp.concatenate(tiles, axis=0)


def both_ends(ref, k, i):
    sub = lax.broadcasted_iota(jnp.int32, (8, LANES), 0)
    return jnp.where(sub < 4, ref[k, i, 0:8], ref[k, i, 24:32])


def group_of(k, i):
    return 3 * k + i


def rim_part(q_ref, west_ref, east_ref):
    def part(e, i):
        if (e, i) in ((HALO - 1, 3), (HALO, 0)):
            g = 8 * (GROUPS - 1)
            return west_ref[g : g + 8] + both_ends(q_ref, 0, 0)
        if (e, i) in ((HALO + EX - 1, 3), (HALO + EX, 0)):
            return both_ends(q_ref, EX - 1, 3) + east_ref[0:8]
        if HALO <= e < HALO + EX:
            return both_ends(q_ref, e - HALO, i)
        ref, k = (west_ref, e) if e < HALO else (east_ref, e - HALO - EX)
        g = 8 * group_of(k, i)
        return ref[g : g + 8]

    return part


def edges(part, lo, scaled, flags_ref, from_south_ref, from_north_ref, matrix, south_ref, north_ref):
    hi = WIDE - 1 - lo
    masks = edge_masks(flags_ref)
    res = {}
    scale = {}
    for first in range(0, WIDE, 4):
        values, es = [], []
        for e in range(first, first + 4):
            if lo <= e <= hi:
                value = rim_value(part, e, lo, from_south_ref, from_north_ref, masks)
                if not scaled:
                    inverse = 1.0 / value[:, FL : FL + 1]
                    value = value * inverse
                    for i in range(4):
                        scale[e, i] = (inverse[8 * i : 8 * i + 1], inverse[8 * i + 7 : 8 * i + 8])
                values.append(value)
                es.append(matrix(e))
            else:
                values.append(jnp.zeros((32, LANES), F32))
                es.append(jnp.zeros((8, 32), F32))
        r = rim_product(es, jnp.concatenate(values, axis=0))
        for k in range(4):
            res[first + k] = r[8 * k : 8 * k + 8]
    first, final = lo + 1, hi - 1
    for side, out in enumerate((south_ref, north_ref)):
        for e in range(first, final + 1):
            for i in range(4 if e == final else 3):
                row = 3 * (e - first) + i
                value = res[e][4 * side + i : 4 * side + i + 1]
                if i == 0:
                    value = value + res[e - 1][4 * side + 3 : 4 * side + 4]
                if i == 3:
                    value = value + res[e + 1][4 * side : 4 * side + 1]
                if not scaled:
                    value = value * scale[e, i][side]
                out[row : row + 1, :] = value
        used = 3 * (final - first + 1) + 1
        out[used:, :] = jnp.zeros((out.shape[0] - used, LANES), F32)


def second_edges(flags_ref, q_ref, west_ref, east_ref, e_ref, halo_e_ref, from_south_ref, from_north_ref, south_ref, north_ref):
    part = rim_part(q_ref, west_ref, east_ref)
    edges(part, 0, False, flags_ref, from_south_ref, from_north_ref, rim_matrix(e_ref, halo_e_ref), south_ref, north_ref)


def rim_matrix(e_ref, halo_e_ref):
    def matrix(e):
        if HALO <= e < HALO + EX:
            return e_ref[e - HALO]
        return halo_e_ref[e if e < HALO else e - EX]

    return matrix


def split_matrix(inner_ref, outer_ref):
    def matrix(e):
        inner, k = split_at(e)
        return (inner_ref if inner else outer_ref)[k]

    return matrix


def third_edges(flags_ref, inner_ref, outer_ref, joint_ref, in_e_ref, out_e_ref, from_south_ref, from_north_ref, south_ref, north_ref):
    sub = lax.broadcasted_iota(jnp.int32, (8, LANES), 0)
    whole = split_part(inner_ref, outer_ref, joint_ref)

    def part(e, i):
        return jnp.where(sub < 4, whole(e, i, 0, 8), whole(e, i, 24, 32))

    edges(part, 1, True, flags_ref, from_south_ref, from_north_ref, split_matrix(in_e_ref, out_e_ref), south_ref, north_ref)


def fourth_edges(flags_ref, f_ref, in_e_ref, out_e_ref, from_south_ref, from_north_ref, south_ref, north_ref):
    def part(e, i):
        return both_ends(f_ref, e, i)

    edges(part, 2, True, flags_ref, from_south_ref, from_north_ref, split_matrix(in_e_ref, out_e_ref), south_ref, north_ref)


def join(out_ref, e, q):
    shared = out_ref[e - 1, 3] + q[0:32]
    out_ref[e - 1, 3] = shared
    out_ref[e, 0] = shared


def put(out_ref, e, first, q):
    for i in range(4):
        out_ref[e, i] = q[32 * i : 32 * i + 32]
    if e > first:
        join(out_ref, e, q)


INNER = range(HALO + 1, HALO + EX - 1)
OUTER = [e for e in range(WIDE) if e not in INNER]


def split_at(e):
    return (True, e - INNER[0]) if e in INNER else (False, OUTER.index(e))


def split_part(inner_ref, outer_ref, joint_ref):
    def part(e, i, a, b):
        if (e, i) in ((INNER[0] - 1, 3), (INNER[0], 0)):
            return joint_ref[0, a:b]
        if (e, i) in ((INNER[-1], 3), (INNER[-1] + 1, 0)):
            return joint_ref[1, a:b]
        inner, k = split_at(e)
        return (inner_ref if inner else outer_ref)[k, i, a:b]

    return part


def second_column(value, m, k, rim, out_ref, join_before, twice_ref, lo_ref, scaled_ref):
    inverse = 1.0 / value[:, FL : FL + 1]
    m_hi, m_lo = halves(m * inverse)
    twice = jnp.concatenate([m_hi, m_hi], axis=1)
    twice_ref[k] = twice
    lo_ref[k] = m_lo
    put(out_ref, k, 0 if join_before else k, applied(twice, m_lo, value * inverse))
    rows = jnp.concatenate(
        [inverse[32 * i : 32 * i + 1] for i in range(4)] + [inverse[32 * i + 31 : 32 * i + 32] for i in range(4)], axis=0
    )
    scaled_ref[k] = rim * rows


def second_inner(flags_ref, q_ref, e_ref, from_south_ref, from_north_ref, m_ref, out_ref, twice_ref, lo_ref, scaled_ref):
    def part(e, i, a, b):
        return q_ref[e - HALO, i, a:b]

    masks = edge_masks(flags_ref)
    for k, e in enumerate(INNER):
        value = column_value(part, e, 0, from_south_ref, from_north_ref, masks)
        second_column(value, m_ref[e - HALO], k, e_ref[e - HALO], out_ref, k > 0, twice_ref, lo_ref, scaled_ref)


def second_outer(flags_ref, q_ref, west_ref, east_ref, one_rest_ref, two_rest_ref, spread_rim_ref, spread_ref, e_ref, halo_e_ref, from_south_ref, from_north_ref, m_ref, mh_ref, inner_ref, out_ref, joint_ref, twice_ref, lo_ref, scaled_ref):
    even = flags_ref[2] != 0
    rests = (either(even, one_rest_ref[...], two_rest_ref[...]), either(even, two_rest_ref[...], one_rest_ref[...]))
    wide = [
        moved_rows(spread_rim_ref[...], rim[0:RIM]) + moved_rows(spread_ref[...], rest)
        for rim, rest in zip((west_ref, east_ref), rests)
    ]

    def part(e, i, a, b):
        if (e, i) in ((HALO - 1, 3), (HALO, 0)):
            g = 32 * (GROUPS - 1)
            return wide[0][g + a : g + b] + q_ref[0, 0, a:b]
        if (e, i) in ((HALO + EX - 1, 3), (HALO + EX, 0)):
            return q_ref[EX - 1, 3, a:b] + wide[1][a:b]
        if HALO <= e < HALO + EX:
            return q_ref[e - HALO, i, a:b]
        side, k = (0, e) if e < HALO else (1, e - HALO - EX)
        g = 32 * group_of(k, i)
        return wide[side][g + a : g + b]

    masks = edge_masks(flags_ref)
    for k, e in enumerate(OUTER):
        value = column_value(part, e, 0, from_south_ref, from_north_ref, masks)
        if e < HALO:
            m = mh_ref[e]
        elif e < HALO + EX:
            m = m_ref[e - HALO]
        else:
            m = mh_ref[e - EX]
        second_column(value, m, k, rim_matrix(e_ref, halo_e_ref)(e), out_ref, k not in (0, len(OUTER) // 2), twice_ref, lo_ref, scaled_ref)
    half = len(OUTER) // 2
    joint_ref[0] = out_ref[half - 1, 3] + inner_ref[0, 0]
    joint_ref[1] = inner_ref[len(INNER) - 1, 3] + out_ref[half, 0]


def matrices(e, inner, outer):
    is_inner, k = split_at(e)
    twice_ref, lo_ref = inner if is_inner else outer
    return twice_ref[k], lo_ref[k]


def third_full(flags_ref, inner_ref, outer_ref, joint_ref, from_south_ref, from_north_ref, in_twice, in_lo, out_twice, out_lo, u_ref, out_ref, kept_ref):
    part = split_part(inner_ref, outer_ref, joint_ref)
    masks = edge_masks(flags_ref)
    for e in range(1, WIDE - 1):
        value = column_value(part, e, 1, from_south_ref, from_north_ref, masks)
        if HALO <= e < HALO + EX:
            c = e - HALO
            kept_ref[c] = u_ref[0, c].reshape(PTS, FL) - (2.0 * VISCOSITY) * value[:, 0:FL]
        put(out_ref, e, 1, applied(*matrices(e, (in_twice, in_lo), (out_twice, out_lo)), value))


def fourth_full(flags_ref, f_ref, from_south_ref, from_north_ref, in_twice, in_lo, out_twice, out_lo, kept_ref, out_ref, rim_south_ref, rim_north_ref, z_ref):
    def part(e, i, a, b):
        return f_ref[e, i, a:b]

    masks = edge_masks(flags_ref)
    for e in range(2, WIDE - 2):
        value = column_value(part, e, 2, from_south_ref, from_north_ref, masks)
        put(z_ref, e, 2, applied(*matrices(e, (in_twice, in_lo), (out_twice, out_lo)), value))
        c = e - HALO - 1
        if 0 <= c < EX:
            z = jnp.concatenate([z_ref[e - 1, i, :, 0:FL] for i in range(4)], axis=0)
            done = (kept_ref[c] + (VISCOSITY * VISCOSITY) * z).reshape(4, 8, 4, FL)
            out_ref[0, c] = done
            rim_south_ref[c] = done[:, 0]
            rim_north_ref[c] = done[:, 7]


def patch_kernel(flags_ref, old_ref, rim_south_ref, rim_north_ref, from_south_ref, from_north_ref, out_ref, south_buf, north_buf, sems):
    del old_ref
    sub = lax.broadcasted_iota(jnp.int32, (4, FL), 0)
    masks = ((sub == 0) & (flags_ref[0] != 0), (sub == 3) & (flags_ref[1] != 0))
    copies = []
    for b in range(0, EX, 4):
        for side, (rim, got, buf) in enumerate(
            ((rim_south_ref, from_south_ref, south_buf), (rim_north_ref, from_north_ref, north_buf))
        ):
            for c in range(b, b + 4):
                for i in range(4):
                    row = 3 * c + i
                    more = (VISCOSITY * VISCOSITY) * got[row : row + 1, 0:FL]
                    buf[c, i] = rim[c, i] + jnp.where(masks[side], more, 0.0)
            copies.append(
                pltpu.make_async_copy(buf.at[b : b + 4], out_ref.at[0, b : b + 4, :, 7 * side], sems.at[len(copies)])
            )
            copies[-1].start()
    for copy in copies:
        copy.wait()


VM = pl.BlockSpec(memory_space=pltpu.VMEM)
SM = pl.BlockSpec(memory_space=pltpu.SMEM)
ANY = pl.BlockSpec(memory_space=pl.ANY)
HBM = pl.BlockSpec(memory_space=pltpu.HBM)


def call(body, outs, specs, name, scratch=(), out_specs=None, aliases=None):
    return pl.pallas_call(
        body,
        out_shape=[jax.ShapeDtypeStruct(s, d) for s, d in outs],
        in_specs=specs,
        out_specs=out_specs or [VM] * len(outs),
        scratch_shapes=list(scratch),
        input_output_aliases=aliases or {},
        compiler_params=pltpu.CompilerParams(vmem_limit_bytes=24 * 1024 * 1024),
        name=name,
    )


def moved(array, columns, rows):
    pairs = []
    for i in range(256):
        c, r = divmod(i, PY)
        pairs.append((i, (c + columns) % 32 * PY + (r + rows) % PY))
    return lax.ppermute(array, AXES, pairs)


def swapped(array, odd):
    pairs = []
    for i in range(256):
        c, r = divmod(i, PY)
        pairs.append((i, (((c + odd) ^ 1) - odd) % 32 * PY + r))
    return lax.ppermute(array, AXES, pairs)


def across(to_south, to_north):
    return moved(to_north, 0, 1), moved(to_south, 0, -1)


def per_device(state, jacobian, metric_xx, metric_yy, metric_xy):
    left, rim, diff, near, spread_rim, spread = (jnp.asarray(t) for t in tables())
    flat = [jnp.transpose(g[0], (1, 2, 3, 0)).reshape(PTS, EX) for g in (jacobian, metric_xx, metric_yy, metric_xy)]
    index = lax.axis_index(AXES)
    row = index % PY
    flags = jnp.stack([row != 0, row != PY - 1, index // PY % 2 == 0]).astype(jnp.int32)
    rows = lambda n: ((n, LANES), F32)
    wide = ((WIDE, 4, 32, LANES), F32)
    pinned = lambda *ts: [pltpu.with_memory_space_constraint(t, pltpu.HBM) for t in ts]
    four = (HALO + 1, 4, 8, 4, FL)

    own = [((EX, 4, 32, LANES), F32), ((EX, PTS, PTS), F32)]
    rim_one, layers_one, other, f, mass, left_in, diff_in, q, m = call(
        first_kernel,
        [rows(SENT), rows(32 * GROUPS), (four, F32), ((3, PTS, EX), F32), ((PTS, EX), F32), (left.shape, BF16), (diff.shape, F32), *own],
        [SM] + [HBM] * 7,
        "first",
        scratch=[pltpu.VMEM(four, F32), *[pltpu.VMEM((PTS, EX), F32)] * 4, pltpu.SemaphoreType.DMA((8,))],
    )(flags, *pinned(state, *flat, left, diff))
    one = swapped(rim_one, 1)
    rim_two, layers_two, q, m = call(
        other_kernel, [rows(SENT), rows(32 * GROUPS), *own], [SM] + [VM] * 7, "other", aliases={6: 2, 7: 3}
    )(flags, other, f, mass, left_in, diff_in, q, m)
    two = swapped(rim_two, 0)
    rest_one, rest_two = call(rest_kernel, [rows(176)] * 2, [VM] * 2, "rest")(layers_one, layers_two)
    rest_one = swapped(rest_one, 1)
    rest_two = swapped(rest_two, 0)
    e, own_south, own_north = call(
        rows_kernel,
        [((EX, 8, 32), F32), rows(56), rows(56)],
        [HBM] * 3 + [VM] * 2,
        "rows",
        scratch=[pltpu.VMEM((EX, 4, 4, FL), F32)] * 2
        + [pltpu.VMEM(rim.shape, BF16), pltpu.VMEM(near.shape, F32), pltpu.SemaphoreType.DMA((4,))],
    )(*pinned(state, rim, near), f, mass)
    to_south, to_north = call(merge_kernel, [rows(72)] * 2, [SM] + [VM] * 4, "merge")(flags, one, two, own_south, own_north)
    south1, north1 = across(to_south, to_north)
    q, m = call(
        own_kernel,
        own,
        [HBM, ANY] + [VM] * 6,
        "own",
        scratch=[pltpu.VMEM((8, 4, 8, 4, FL), F32), pltpu.SemaphoreType.DMA((2,))],
        aliases={6: 0, 7: 1},
    )(*pinned(state), to_south, f, mass, left_in, diff_in, q, m)
    mh, halo_e, west, east = call(
        halo_kernel,
        [((2 * HALO, PTS, PTS), F32), ((2 * HALO, 8, 32), F32), rows(SENT), rows(SENT)],
        [SM] + [VM] * 6,
        "halo",
    )(flags, one, two, left_in, rim, diff_in, near)
    to_south, to_north = call(second_edges, [rows(64)] * 2, [SM] + [VM] * 7, "edges2")(
        flags, q, west, east, e, halo_e, south1, north1
    )
    south2, north2 = across(to_south, to_north)
    matrix = lambda n: [((n, PTS, 2 * PTS), BF16), ((n, PTS, PTS), BF16), ((n, 8, 32), F32)]
    inner, in_twice, in_lo, in_pairs = call(
        second_inner, [((14, 4, 32, LANES), F32), *matrix(14)], [SM] + [VM] * 5, "inner2"
    )(flags, q, e, south1, north1, m)
    outer, joint, out_twice, out_lo, out_pairs = call(
        second_outer, [((8, 4, 32, LANES), F32), ((2, 32, LANES), F32), *matrix(8)], [SM] + [VM] * 14, "outer2"
    )(flags, q, west, east, rest_one, rest_two, spread_rim, spread, e, halo_e, south1, north1, m, mh, inner)
    to_south, to_north = call(third_edges, [rows(56)] * 2, [SM] + [VM] * 7, "edges3")(
        flags, inner, outer, joint, in_pairs, out_pairs, south2, north2
    )
    south3, north3 = across(to_south, to_north)
    f, kept = call(third_full, [wide, ((EX, PTS, FL), F32)], [SM] + [VM] * 10, "full3")(
        flags, inner, outer, joint, south2, north2, in_twice, in_lo, out_twice, out_lo, state
    )
    to_south, to_north = call(fourth_edges, [rows(56)] * 2, [SM] + [VM] * 5, "edges4")(
        flags, f, in_pairs, out_pairs, south3, north3
    )
    south4, north4 = across(to_south, to_north)
    out, rim_south, rim_north = call(
        fourth_full,
        [((1, EX, 4, 8, 4, FL), F32), ((EX, 4, 4, FL), F32), ((EX, 4, 4, FL), F32)],
        [SM] + [VM] * 8,
        "full4",
        scratch=[pltpu.VMEM((WIDE, 4, 32, LANES), F32)],
    )(flags, f, south3, north3, in_twice, in_lo, out_twice, out_lo, kept)
    (out,) = call(
        patch_kernel,
        [((1, EX, 4, 8, 4, FL), F32)],
        [SM, ANY] + [VM] * 4,
        "patch",
        scratch=[pltpu.VMEM((EX, 4, 4, FL), F32), pltpu.VMEM((EX, 4, 4, FL), F32), pltpu.SemaphoreType.DMA((8,))],
        out_specs=[ANY],
        aliases={1: 0},
    )(flags, out, rim_south, rim_north, south4, north4)
    return out


def solution(mesh):
    spec = P(AXES)
    return jax.shard_map(per_device, mesh=mesh, in_specs=(spec,) * 5, out_specs=spec, check_vma=False)
```

profile of v0, /device:TPU:1, one launch (start us, length us, event | category | flops | bytes accessed | tf_op | source)
XLA Modules:
  0.0 58.0 jit_solution(2790103123666450396)
XLA Ops:
  0.0 0.1 add_convert_fusion.flags_ref
  0.1 3.6 %first.1 = (f32[88,384]{1,0:T(8,128)S(1)}, f32[320,384]{1,0:T(8,128)S(1)}, f32[4,4,8,4,360]{4,3,2,1,0:T(4,128)S(1)}, f32[3,128,16]{2,1,0:T(8,128)S(1)}, f32[128,...) custom-call(s32[3]{0:T(128)S(1)} %add_convert_fusion.flags_ref, ...), custom_call_target="tpu_custom_call" | custom-call | tf_op jit(solution)/shard_map/first/pallas_call | solution.py:678
  3.7 11.8 %collective-permute-start = (f32[88,384]{1,0:T(8,128)S(1)}, f32[88,384]{1,0:T(8,128)S(1)}, u32[]{:S(2)}, u32[]{:S(2)}) collective-permute-start(f32[88,384]{1,0:T(8,128)S(1)} %get-tuple-element.51), channel_id=1, source_target_pairs={{0,248},{1,249},{2,250},{3,251},{4,252},{5,253},{6,254},{7,255},{8... | collective-permute-start | bytes 405512 | tf_op jit(solution)/shard_map/ppermute | solution.py:659
  15.4 2.1 %other.1 = (f32[88,384]{1,0:T(8,128)S(1)}, f32[320,384]{1,0:T(8,128)S(1)}, f32[16,4,32,384]{3,2,1,0:T(8,128)S(1)}, f32[16,128,128]{2,1,0:T(8,128)S(1)}) custom-call(s32[3]{0:T(128)S(1)} %add_convert_fusion.flags_ref, f32[4,4,8,4,360]{4,3,2,1,0:T(4,128)S(1)} %get-tuple-element.52.u_ref, ...), custom_call_target="tpu_custom_call", output_to_operand_aliasing={{2}: (6, {}), {3}: (7, {})} | custom-call | tf_op jit(solution)/shard_map/other/pallas_call | solution.py:686
  17.5 0.1 collective-permute-start.1
  17.6 0.2 rest.1
  17.8 3.3 %collective-permute-start.4 = (f32[176,384]{1,0:T(8,128)S(1)}, f32[176,384]{1,0:T(8,128)S(1)}, u32[]{:S(2)}, u32[]{:S(2)}) collective-permute-start(f32[176,384]{1,0:T(8,128)S(1)} %get-tuple-element.74), channel_id=1, source_target_pairs={{0,248},{1,249},{2,250},{3,251},{4,252},{5,253},{6,254},{7,255},{8... | collective-permute-start | bytes 811016 | tf_op jit(solution)/shard_map/ppermute | solution.py:659
  21.1 1.6 %rows.1 = (f32[16,8,32]{2,1,0:T(8,128)S(1)}, f32[56,384]{1,0:T(8,128)S(1)}, f32[56,384]{1,0:T(8,128)S(1)}) custom-call(f32[1,16,4,8,4,360]{5,4,3,2,1,0:T(4,128)} %u_ref.1, bf16[2,16,64]{2,1,0:T(8,128)(2,1)} %constant.61.clone.rim_hbm.rim_ref, f32[2,32,32]{2,1,0:T(8,128)} %constant.63.clone.near_hbm.near_ref, f32[3,128,16]{2,1,0:T(8,128)S(1)} %get-tuple-element.53.f_ref, ...), custom_call_target="tpu_custom_call" | custom-call | tf_op jit(solution)/shard_map/rows/pallas_call | solution.py:693
  22.7 0.2 collective-permute-done.1.two_ref
  22.9 0.6 merge.1
  23.5 3.7 %collective-permute-start.2 = (f32[72,384]{1,0:T(8,128)S(1)}, f32[72,384]{1,0:T(8,128)S(1)}, u32[]{:S(2)}, u32[]{:S(2)}) collective-permute-start(f32[72,384]{1,0:T(8,128)S(1)} %get-tuple-element.67), channel_id=1, source_target_pairs={{0,1},{1,2},{2,3},{3,4},{4,5},{5,6},{6,7},{7,0},{8,9},{9,10},{10,1... | collective-permute-start | bytes 331784 | tf_op jit(solution)/shard_map/ppermute | solution.py:651
  27.2 3.3 %own.1 = (f32[16,4,32,384]{3,2,1,0:T(8,128)S(1)}, f32[16,128,128]{2,1,0:T(8,128)S(1)}) custom-call(f32[1,16,4,8,4,360]{5,4,3,2,1,0:T(4,128)} %u_ref.1, f32[72,384]{1,0:T(8,128)S(1)} %get-tuple-element.62.after_ref, f32[3,128,16]{2,1,0:T(8,128)S(1)} %get-tuple-element.53.f_ref, ...), custom_call_target="tpu_custom_call", output_to_operand_aliasing={{0}: (6, {}), {1}: (7, {})} | custom-call | tf_op jit(solution)/shard_map/own/pallas_call | solution.py:703
  30.6 1.5 %halo.1 = (f32[6,128,128]{2,1,0:T(8,128)S(1)}, f32[6,8,32]{2,1,0:T(8,128)S(1)}, f32[88,384]{1,0:T(8,128)S(1)}, f32[88,384]{1,0:T(8,128)S(1)}) custom-call(s32[3]{0:T(128)S(1)} %add_convert_fusion.flags_ref, f32[88,384]{1,0:T(8,128)S(1)} %collective-permute-done.one_ref, f32[88,384]{1,0:T(8,128)S(1)} %collective-permute-done.1.two_ref, ...), custom_call_target="tpu_custom_call" | custom-call | tf_op jit(solution)/shard_map/halo/pallas_call | solution.py:711
  32.1 3.3 %collective-permute-done.3.from_north_ref = f32[72,384]{1,0:T(8,128)S(1)} collective-permute-done((f32[72,384]{1,0:T(8,128)S(1)}, f32[72,384]{1,0:T(8,128)S(1)}, u32[]{:S(2)}, u32[]{:S(2)}) %collective-permute-start.3) | collective-permute-done | bytes 110624 | tf_op jit(solution)/shard_map/ppermute | solution.py:651
  35.4 1.2 %edges2.1 = (f32[64,384]{1,0:T(8,128)S(1)}, f32[64,384]{1,0:T(8,128)S(1)}) custom-call(s32[3]{0:T(128)S(1)} %add_convert_fusion.flags_ref, f32[16,4,32,384]{3,2,1,0:T(8,128)S(1)} %get-tuple-element.65.q_ref, f32[88,384]{1,0:T(8,128)S(1)} %get-tuple-element.70.west_ref, f32[88,384]{1,0:T(8,128)S(1)} %get-tuple-element.71.east_ref, ...), custom_call_target="tpu_custom_call" | custom-call | tf_op jit(solution)/shard_map/edges2/pallas_call | solution.py:717
  36.5 0.0 copy-start.1
  36.6 0.1 collective-permute-start.6
  36.7 0.5 collective-permute-start.7
  37.2 2.1 %inner2.1 = (f32[14,4,32,384]{3,2,1,0:T(8,128)S(1)}, bf16[14,128,256]{2,1,0:T(8,128)(2,1)S(1)}, bf16[14,128,128]{2,1,0:T(8,128)(2,1)S(1)}, f32[14,8,32]{2,1,0:T(8,128)S(1)}) custom-call(s32[3]{0:T(128)S(1)} %add_convert_fusion.flags_ref, f32[16,4,32,384]{3,2,1,0:T(8,128)S(1)} %get-tuple-element.65.q_ref, f32[16,8,32]{2,1,0:T(8,128)S(1)} %get-tuple-element.66.e_ref, ...), custom_call_target="tpu_custom_call" | custom-call | tf_op jit(solution)/shard_map/inner2/pallas_call | solution.py:722
  39.3 2.2 %outer2.1 = (f32[8,4,32,384]{3,2,1,0:T(8,128)S(1)}, f32[2,32,384]{2,1,0:T(8,128)S(1)}, bf16[8,128,256]{2,1,0:T(8,128)(2,1)S(1)}, bf16[8,128,128]{2,1,0:T(8,128)(2,1)S(1)}, f32[8,8,32]{2,1,0:T(8,128)S(1)}) custom-call(s32[3]{0:T(128)S(1)} %add_convert_fusion.flags_ref, f32[16,4,32,384]{3,2,1,0:T(8,128)S(1)} %get-tuple-element.65.q_ref, ...), custom_call_target="tpu_custom_call" | custom-call | tf_op jit(solution)/shard_map/outer2/pallas_call | solution.py:725
  41.5 0.6 collective-permute-done.7.from_north_ref
  42.1 1.0 %edges3.1 = (f32[56,384]{1,0:T(8,128)S(1)}, f32[56,384]{1,0:T(8,128)S(1)}) custom-call(s32[3]{0:T(128)S(1)} %add_convert_fusion.flags_ref, f32[14,4,32,384]{3,2,1,0:T(8,128)S(1)} %get-tuple-element.69.inner_ref, f32[8,4,32,384]{3,2,1,0:T(8,128)S(1)} %get-tuple-element.78.outer_ref, f32[2,32,384]{2,1,0:T(8,128)S(1)} %get-tuple-element.79.joint_ref, ...), custom_call_target="tpu_custom_call" | custom-call | tf_op jit(solution)/shard_map/edges3/pallas_call | solution.py:728
  43.1 1.0 %collective-permute-start.8 = (f32[56,384]{1,0:T(8,128)S(1)}, f32[56,384]{1,0:T(8,128)S(1)}, u32[]{:S(2)}, u32[]{:S(2)}) collective-permute-start(f32[56,384]{1,0:T(8,128)S(1)} %get-tuple-element.89), channel_id=1, source_target_pairs={{0,1},{1,2},{2,3},{3,4},{4,5},{5,6},{6,7},{7,0},{8,9},{9,10},{10,1... | collective-permute-start | bytes 258056 | tf_op jit(solution)/shard_map/ppermute | solution.py:651
  44.1 0.8 %collective-permute-start.9 = (f32[56,384]{1,0:T(8,128)S(1)}, f32[56,384]{1,0:T(8,128)S(1)}, u32[]{:S(2)}, u32[]{:S(2)}) collective-permute-start(f32[56,384]{1,0:T(8,128)S(1)} %get-tuple-element.90), channel_id=1, source_target_pairs={{0,7},{1,0},{2,1},{3,2},{4,3},{5,4},{6,5},{7,6},{8,15},{9,8},{10,9... | collective-permute-start | bytes 258056 | tf_op jit(solution)/shard_map/ppermute | solution.py:651
  44.9 2.4 %full3.1 = (f32[22,4,32,384]{3,2,1,0:T(8,128)S(1)}, f32[16,128,360]{2,1,0:T(8,128)S(1)}) custom-call(s32[3]{0:T(128)S(1)} %add_convert_fusion.flags_ref, f32[14,4,32,384]{3,2,1,0:T(8,128)S(1)} %get-tuple-element.69.inner_ref, f32[8,4,32,384]{3,2,1,0:T(8,128)S(1)} %get-tuple-element.78.outer_ref, f32[2,32,384]{2,1,0:T(8,128)S(1)} %get-tuple-element.79.joint_ref, ...), custom_call_target="tpu_custom_call" | custom-call | tf_op jit(solution)/shard_map/full3/pallas_call | solution.py:732
  47.3 1.0 %collective-permute-done.9.from_north_ref = f32[56,384]{1,0:T(8,128)S(1)} collective-permute-done((f32[56,384]{1,0:T(8,128)S(1)}, f32[56,384]{1,0:T(8,128)S(1)}, u32[]{:S(2)}, u32[]{:S(2)}) %collective-permute-start.9) | collective-permute-done | bytes 86048 | tf_op jit(solution)/shard_map/ppermute | solution.py:651
  48.4 1.0 %edges4.1 = (f32[56,384]{1,0:T(8,128)S(1)}, f32[56,384]{1,0:T(8,128)S(1)}) custom-call(s32[3]{0:T(128)S(1)} %add_convert_fusion.flags_ref, f32[22,4,32,384]{3,2,1,0:T(8,128)S(1)} %get-tuple-element.86.f_ref, f32[14,8,32]{2,1,0:T(8,128)S(1)} %get-tuple-element.87.in_e_ref, f32[8,8,32]{2,1,0:T(8,128)S(1)} %get-tuple-element.88.out_e_ref, ...), custom_call_target="tpu_custom_call" | custom-call | tf_op jit(solution)/shard_map/edges4/pallas_call | solution.py:735
  49.4 0.2 collective-permute-start.10
  49.6 1.5 %collective-permute-start.11 = (f32[56,384]{1,0:T(8,128)S(1)}, f32[56,384]{1,0:T(8,128)S(1)}, u32[]{:S(2)}, u32[]{:S(2)}) collective-permute-start(f32[56,384]{1,0:T(8,128)S(1)} %get-tuple-element.96), channel_id=1, source_target_pairs={{0,7},{1,0},{2,1},{3,2},{4,3},{5,4},{6,5},{7,6},{8,15},{9,8},{10,9... | collective-permute-start | bytes 258056 | tf_op jit(solution)/shard_map/ppermute | solution.py:651
  51.1 3.7 %full4.1 = (f32[1,16,4,8,4,360]{5,4,3,2,1,0:T(4,128)}, f32[16,4,4,360]{3,2,1,0:T(4,128)S(1)}, f32[16,4,4,360]{3,2,1,0:T(4,128)S(1)}) custom-call(s32[3]{0:T(128)S(1)} %add_convert_fusion.flags_ref, f32[22,4,32,384]{3,2,1,0:T(8,128)S(1)} %get-tuple-element.86.f_ref, f32[56,384]{1,0:T(8,128)S(1)} %collective-permute-done.8.from_south_ref, ...), custom_call_target="tpu_custom_call" | custom-call | tf_op jit(solution)/shard_map/full4/pallas_call | solution.py:739
  54.8 1.5 %collective-permute-done.11.from_north_ref = f32[56,384]{1,0:T(8,128)S(1)} collective-permute-done((f32[56,384]{1,0:T(8,128)S(1)}, f32[56,384]{1,0:T(8,128)S(1)}, u32[]{:S(2)}, u32[]{:S(2)}) %collective-permute-start.11) | collective-permute-done | bytes 86048 | tf_op jit(solution)/shard_map/ppermute | solution.py:651
  56.3 1.5 %patch.1 = f32[1,16,4,8,4,360]{5,4,3,2,1,0:T(4,128)} custom-call(s32[3]{0:T(128)S(1)} %add_convert_fusion.flags_ref, f32[1,16,4,8,4,360]{5,4,3,2,1,0:T(4,128)} %get-tuple-element.92.old_ref, f32[16,4,4,360]{3,2,1,0:T(4,128)S(1)} %get-tuple-element.93.rim_south_ref, ...), custom_call_target="tpu_custom_call", output_to_operand_aliasing={{}: (1, {})} | custom-call | tf_op jit(solution)/shard_map/patch/pallas_call | solution.py:746
  (18 shorter events, 0.0 us)
Async XLA Ops:
  3.7 19.0 %collective-permute-start = (f32[88,384]{1,0:T(8,128)S(1)}, f32[88,384]{1,0:T(8,128)S(1)}, u32[]{:S(2)}, u32[]{:S(2)}) collective-permute-start(f32[88,384]{1,0:T(8,128)S(1)} %get-tuple-element.51), channel_id=1, source_target_pairs={{0,248},{1,249},{2,250},{3,251},{4,252},{5,253},{6,254},{7,255},{8... | collective-permute-start | bytes 405512 | tf_op jit(solution)/shard_map/ppermute | solution.py:659
  17.5 5.4 %collective-permute-start.1 = (f32[88,384]{1,0:T(8,128)S(1)}, f32[88,384]{1,0:T(8,128)S(1)}, u32[]{:S(2)}, u32[]{:S(2)}) collective-permute-start(f32[88,384]{1,0:T(8,128)S(1)} %get-tuple-element.59), channel_id=1, source_target_pairs={{0,8},{1,9},{2,10},{3,11},{4,12},{5,13},{6,14},{7,15},{8,0},{9,1},... | collective-permute-start | bytes 405512 | tf_op jit(solution)/shard_map/ppermute | solution.py:659
  17.8 21.5 %collective-permute-start.4 = (f32[176,384]{1,0:T(8,128)S(1)}, f32[176,384]{1,0:T(8,128)S(1)}, u32[]{:S(2)}, u32[]{:S(2)}) collective-permute-start(f32[176,384]{1,0:T(8,128)S(1)} %get-tuple-element.74), channel_id=1, source_target_pairs={{0,248},{1,249},{2,250},{3,251},{4,252},{5,253},{6,254},{7,255},{8... | collective-permute-start | bytes 811016 | tf_op jit(solution)/shard_map/ppermute | solution.py:659
  21.1 18.2 %collective-permute-start.5 = (f32[176,384]{1,0:T(8,128)S(1)}, f32[176,384]{1,0:T(8,128)S(1)}, u32[]{:S(2)}, u32[]{:S(2)}) collective-permute-start(f32[176,384]{1,0:T(8,128)S(1)} %get-tuple-element.75), channel_id=1, source_target_pairs={{0,8},{1,9},{2,10},{3,11},{4,12},{5,13},{6,14},{7,15},{8,0},{9,1},... | collective-permute-start | bytes 811016 | tf_op jit(solution)/shard_map/ppermute | solution.py:659
  23.5 8.6 %collective-permute-start.2 = (f32[72,384]{1,0:T(8,128)S(1)}, f32[72,384]{1,0:T(8,128)S(1)}, u32[]{:S(2)}, u32[]{:S(2)}) collective-permute-start(f32[72,384]{1,0:T(8,128)S(1)} %get-tuple-element.67), channel_id=1, source_target_pairs={{0,1},{1,2},{2,3},{3,4},{4,5},{5,6},{6,7},{7,0},{8,9},{9,10},{10,1... | collective-permute-start | bytes 331784 | tf_op jit(solution)/shard_map/ppermute | solution.py:651
  27.2 8.1 %collective-permute-start.3 = (f32[72,384]{1,0:T(8,128)S(1)}, f32[72,384]{1,0:T(8,128)S(1)}, u32[]{:S(2)}, u32[]{:S(2)}) collective-permute-start(f32[72,384]{1,0:T(8,128)S(1)} %get-tuple-element.62.after_ref), channel_id=1, source_target_pairs={{0,7},{1,0},{2,1},{3,2},{4,3},{5,4},{6,5},{7,6},{8,15},{9,8},{10,9... | collective-permute-start | bytes 331784 | tf_op jit(solution)/shard_map/ppermute | solution.py:651
  27.2 3.3 %copy-start.2 = (f32[2,32,32]{2,1,0:T(8,128)S(1)}, f32[2,32,32]{2,1,0:T(8,128)}, u32[]{:S(2)}) copy-start(f32[2,32,32]{2,1,0:T(8,128)} %constant.63.clone.near_hbm.near_ref) | copy-start | bytes 24580
  27.2 3.4 %copy-start.4 = (bf16[2,16,64]{2,1,0:T(8,128)(2,1)S(1)}, bf16[2,16,64]{2,1,0:T(8,128)(2,1)}, u32[]{:S(2)}) copy-start(bf16[2,16,64]{2,1,0:T(8,128)(2,1)} %constant.61.clone.rim_hbm.rim_ref) | copy-start | bytes 12292
  36.5 2.7 %copy-start.1 = (bf16[320,176]{1,0:T(8,128)(2,1)S(1)}, bf16[320,176]{1,0:T(8,128)(2,1)}, u32[]{:S(2)}) copy-start(bf16[320,176]{1,0:T(8,128)(2,1)} %constant.65.clone.spread_ref) | copy-start | bytes 337924
  36.6 2.7 %copy-start.3 = (bf16[320,80]{1,0:T(8,128)(2,1)S(1)}, bf16[320,80]{1,0:T(8,128)(2,1)}, u32[]{:S(2)}) copy-start(bf16[320,80]{1,0:T(8,128)(2,1)} %constant.64.clone.spread_rim_ref) | copy-start | bytes 153604
  36.6 4.9 %collective-permute-start.6 = (f32[64,384]{1,0:T(8,128)S(1)}, f32[64,384]{1,0:T(8,128)S(1)}, u32[]{:S(2)}, u32[]{:S(2)}) collective-permute-start(f32[64,384]{1,0:T(8,128)S(1)} %get-tuple-element.80), channel_id=1, source_target_pairs={{0,1},{1,2},{2,3},{3,4},{4,5},{5,6},{6,7},{7,0},{8,9},{9,10},{10,1... | collective-permute-start | bytes 294920 | tf_op jit(solution)/shard_map/ppermute | solution.py:651
  36.7 5.4 %collective-permute-start.7 = (f32[64,384]{1,0:T(8,128)S(1)}, f32[64,384]{1,0:T(8,128)S(1)}, u32[]{:S(2)}, u32[]{:S(2)}) collective-permute-start(f32[64,384]{1,0:T(8,128)S(1)} %get-tuple-element.81), channel_id=1, source_target_pairs={{0,7},{1,0},{2,1},{3,2},{4,3},{5,4},{6,5},{7,6},{8,15},{9,8},{10,9... | collective-permute-start | bytes 294920 | tf_op jit(solution)/shard_map/ppermute | solution.py:651
  41.5 3.4 %copy-start = (f32[1,16,4,8,4,360]{5,4,3,2,1,0:T(4,128)S(1)}, f32[1,16,4,8,4,360]{5,4,3,2,1,0:T(4,128)}, u32[]{:S(2)}) copy-start(f32[1,16,4,8,4,360]{5,4,3,2,1,0:T(4,128)} %u_ref.1) | copy-start | bytes 8847364
  43.1 4.2 %collective-permute-start.8 = (f32[56,384]{1,0:T(8,128)S(1)}, f32[56,384]{1,0:T(8,128)S(1)}, u32[]{:S(2)}, u32[]{:S(2)}) collective-permute-start(f32[56,384]{1,0:T(8,128)S(1)} %get-tuple-element.89), channel_id=1, source_target_pairs={{0,1},{1,2},{2,3},{3,4},{4,5},{5,6},{6,7},{7,0},{8,9},{9,10},{10,1... | collective-permute-start | bytes 258056 | tf_op jit(solution)/shard_map/ppermute | solution.py:651
  44.1 4.2 %collective-permute-start.9 = (f32[56,384]{1,0:T(8,128)S(1)}, f32[56,384]{1,0:T(8,128)S(1)}, u32[]{:S(2)}, u32[]{:S(2)}) collective-permute-start(f32[56,384]{1,0:T(8,128)S(1)} %get-tuple-element.90), channel_id=1, source_target_pairs={{0,7},{1,0},{2,1},{3,2},{4,3},{5,4},{6,5},{7,6},{8,15},{9,8},{10,9... | collective-permute-start | bytes 258056 | tf_op jit(solution)/shard_map/ppermute | solution.py:651
  49.4 5.4 %collective-permute-start.10 = (f32[56,384]{1,0:T(8,128)S(1)}, f32[56,384]{1,0:T(8,128)S(1)}, u32[]{:S(2)}, u32[]{:S(2)}) collective-permute-start(f32[56,384]{1,0:T(8,128)S(1)} %get-tuple-element.95), channel_id=1, source_target_pairs={{0,1},{1,2},{2,3},{3,4},{4,5},{5,6},{6,7},{7,0},{8,9},{9,10},{10,1... | collective-permute-start | bytes 258056 | tf_op jit(solution)/shard_map/ppermute | solution.py:651
  49.6 6.7 %collective-permute-start.11 = (f32[56,384]{1,0:T(8,128)S(1)}, f32[56,384]{1,0:T(8,128)S(1)}, u32[]{:S(2)}, u32[]{:S(2)}) collective-permute-start(f32[56,384]{1,0:T(8,128)S(1)} %get-tuple-element.96), channel_id=1, source_target_pairs={{0,7},{1,0},{2,1},{3,2},{4,3},{5,4},{6,5},{7,6},{8,15},{9,8},{10,9... | collective-permute-start | bytes 258056 | tf_op jit(solution)/shard_map/ppermute | solution.py:651
where the time goes:
time: 58.1 us; the launch traced here: 58 us
  Pallas kernels  28 us (48%)
  starting transfers between devices  22.9 us (39%)
  waiting for transfers between devices  6.61 us (11%)
    ppermute x4, starting transfers between devices, swapped(): return lax.ppermute(array, AXES, pairs)  15.1 us
    ppermute x8, starting transfers between devices, moved(): return lax.ppermute(array, AXES, pairs)  7.8 us
    ppermute x8, waiting for transfers between devices, moved(): return lax.ppermute(array, AXES, pairs)  6.38 us
    pallas_call x1, Pallas kernels, per_device(): call(fourth_full, [((1, EX, 4, 8, 4, FL), F32), ((EX, 4, 4, FL), F32), ((...  3.73 us
    pallas_call x1, Pallas kernels, per_device(): call(first_kernel, [rows(SENT), rows(32 * GROUPS), (four, F32), ((3, PTS,...  3.58 us
    pallas_call x1, Pallas kernels, per_device(): call(own_kernel, own, [HBM, ANY] + [VM] * 6, 'own', scratch=[pltpu.VMEM((...  3.33 us
    pallas_call x1, Pallas kernels, per_device(): call(third_full, [wide, ((EX, PTS, FL), F32)], [SM] + [VM] * 10, 'full3')  2.39 us
    pallas_call x1, Pallas kernels, per_device(): call(second_outer, [((8, 4, 32, LANES), F32), ((2, 32, LANES), F32), *mat...  2.21 us
  transfers between devices with their start and end apart: 12, of which 5 were waited for; matrix products, arithmetic and copies ran while one was open for 0% of the time, Pallas kernels for 36%

commit v1 on v0

--- a/solution.py
+++ b/solution.py
@@ -21,6 +21,7 @@
 SENT = RIM + 8
 REST = 17
 TAIL = LANES - FL
+QUADS = -(-WIDE // 4)
 AXES = ("face", "blk")
 VISCOSITY = 1e-4
 F32 = jnp.float32
@@ -155,8 +156,10 @@
 def side_columns(want_west, u_ref, f, mass, left_ref, diff_ref, rim_out_ref, layers_ref, q_ref, m_ref):
     lane = lax.broadcasted_iota(jnp.int32, (PTS, PTS), 1)
     raw, part = {}, {}
+    flux = jnp.concatenate([fluxes(diff_ref, *column(f, k)) for k in range(HALO + 1)], axis=1)
+    together = product(left_ref[0], left_ref[1], flux)
     for k in range(HALO + 1):
-        m = form(left_ref, diff_ref, column(f, k))
+        m = together[:, PTS * k : PTS * k + PTS]
         m_ref[jnp.where(want_west, k, EX - HALO - 1 + k)] = m
         m_hi, m_lo = halves(m)
         q = product(m_hi, m_lo, u_ref[k].reshape(PTS, FL))
@@ -203,14 +206,14 @@
     return either(want_west, t[:, 0 : HALO + 1], t[:, EX - HALO - 1 : EX])
 
 
-def first_kernel(flags_ref, u_hbm, jac_hbm, xx_hbm, yy_hbm, xy_hbm, left_hbm, diff_hbm, rim_out_ref, layers_ref, other_ref, f_ref, mass_ref, left_ref, diff_ref, q_ref, m_ref, u_ref, jac_ref, xx_ref, yy_ref, xy_ref, sems):
-    want_west = flags_ref[2] != 0
+def first_kernel(u_hbm, jac_hbm, xx_hbm, yy_hbm, xy_hbm, left_hbm, diff_hbm, rim_hbm, near_hbm, rim_out_ref, layers_ref, other_ref, f_ref, mass_ref, left_ref, diff_ref, rim_ref, near_ref, low_ref, high_ref, q_ref, m_ref, u_ref, jac_ref, xx_ref, yy_ref, xy_ref, sems):
+    want_west = even_column()
     size = HALO + 1
     here = jnp.where(want_west, 0, EX - size)
     there = jnp.where(want_west, EX - size, 0)
     copies = fetch(
-        (jac_hbm, xx_hbm, yy_hbm, xy_hbm, left_hbm, diff_hbm, u_hbm.at[0, pl.ds(here, size)], u_hbm.at[0, pl.ds(there, size)]),
-        (jac_ref, xx_ref, yy_ref, xy_ref, left_ref, diff_ref, u_ref, other_ref),
+        (jac_hbm, xx_hbm, yy_hbm, xy_hbm, left_hbm, diff_hbm, u_hbm.at[0, pl.ds(here, size)], u_hbm.at[0, pl.ds(there, size)], rim_hbm, near_hbm, u_hbm.at[0, :, :, 0], u_hbm.at[0, :, :, 7]),
+        (jac_ref, xx_ref, yy_ref, xy_ref, left_ref, diff_ref, u_ref, other_ref, rim_ref, near_ref, low_ref, high_ref),
         sems,
     )
     for copy in copies[:6]:
@@ -221,12 +224,13 @@
     mass_ref[...] = mass
     copies[6].wait()
     side_columns(want_west, u_ref, [nearest(want_west, t) for t in f], nearest(want_west, mass), left_ref, diff_ref, rim_out_ref, layers_ref, q_ref, m_ref)
-    copies[7].wait()
-
-
-def other_kernel(flags_ref, u_ref, f_ref, mass_ref, left_ref, diff_ref, q_in, m_in, rim_out_ref, layers_ref, q_ref, m_ref):
+    for copy in copies[7:]:
+        copy.wait()
+
+
+def other_kernel(u_ref, f_ref, mass_ref, left_ref, diff_ref, q_in, m_in, rim_out_ref, layers_ref, q_ref, m_ref):
     del q_in, m_in
-    want_west = flags_ref[2] == 0
+    want_west = jnp.logical_not(even_column())
     f = [nearest(want_west, f_ref[t]) for t in range(3)]
     side_columns(want_west, u_ref, f, nearest(want_west, mass_ref[...]), left_ref, diff_ref, rim_out_ref, layers_ref, q_ref, m_ref)
 
@@ -240,48 +244,61 @@
     return [jnp.concatenate([t[32 * i + a : 32 * i + a + 4] for i in range(4) for a in (0, 28)], axis=0) for t in f]
 
 
-def rows_kernel(u_hbm, rim_hbm, near_hbm, f_ref, mass_ref, e_ref, south_ref, north_ref, low_ref, high_ref, rim_ref, near_ref, sems):
-    copies = fetch(
-        (rim_hbm, near_hbm, u_hbm.at[0, :, :, 0], u_hbm.at[0, :, :, 7]), (rim_ref, near_ref, low_ref, high_ref), sems
-    )
-    for copy in copies[:2]:
-        copy.wait()
+def rows_kernel(low_ref, high_ref, rim_ref, near_ref, f_ref, mass_ref, e_ref, south_ref, north_ref):
     f = end_rows([f_ref[t] for t in range(3)])
     for c in range(EX):
         e_ref[c] = form(rim_ref, near_ref, column(f, c))[0:8]
-    for copy in copies[2:]:
-        copy.wait()
-    res = {}
+    matrices = [quad([e_ref[c + k] for k in range(4)]) for c in range(0, EX, 4)]
+    mass = mass_ref[...]
+    outs = (south_ref, north_ref)
+    carry = [None, None]
     for c in range(0, EX, 4):
         tiles = [ref[c + k, i] for k in range(4) for i in range(4) for ref in (low_ref, high_ref)]
-        r = rim_product([e_ref[c + k] for k in range(4)], jnp.concatenate(tiles, axis=0))
-        for k in range(4):
-            res[c + k] = r[8 * k : 8 * k + 8]
-    mass = mass_ref[...]
-    for side, (out, at) in enumerate(((south_ref, 0), (north_ref, 31))):
+        r = rim_product(matrices[c // 4], jnp.concatenate(tiles, axis=0))
+        for side, out in enumerate(outs):
+            rows = with_carry(r, side, carry[side])
+            carry[side] = rows[12:13]
+            out[3 * c : 3 * c + 12, 0:FL] = rows[0:12]
+    for side, (out, at) in enumerate(zip(outs, (0, 31))):
+        out[48:49, 0:FL] = carry[side]
         for c in range(EX):
             for i in range(4 if c == EX - 1 else 3):
                 row = 3 * c + i
-                value = res[c][4 * side + i : 4 * side + i + 1]
                 part = mass[32 * i + at : 32 * i + at + 1, c : c + 1]
                 if i == 0 and c > 0:
-                    value = value + res[c - 1][4 * side + 3 : 4 * side + 4]
                     part = part + mass[96 + at : 97 + at, c - 1 : c]
-                out[row : row + 1, 0:FL] = value
                 out[row : row + 1, FL:LANES] = jnp.broadcast_to(part, (1, TAIL))
         out[49:56, :] = jnp.zeros((7, LANES), F32)
 
 
-def rim_product(es, value):
+def quad(es):
     blocks = []
     for k, e in enumerate(es):
-        parts = [jnp.zeros((8, 32), F32)] * 4
-        parts[k] = e
-        blocks.append(jnp.concatenate(parts, axis=1))
-    m_hi, m_lo = halves(jnp.concatenate(blocks, axis=0))
+        rows = []
+        for side in range(2):
+            if k:
+                rows.append(jnp.zeros((3 * k, 32), F32))
+            rows.append(e[4 * side : 4 * side + 4])
+            rows.append(jnp.zeros((12 - 3 * k, 32), F32))
+        blocks.append(jnp.concatenate(rows, axis=0))
+    high, low = halves(jnp.concatenate(blocks, axis=1))
+    return jnp.concatenate(
+        [jnp.concatenate([high, high], axis=1), jnp.concatenate([low, jnp.zeros_like(low)], axis=1)], axis=0
+    )
+
+
+def rim_product(matrix, value):
     v_hi, v_lo = halves(value)
-    both = dot(jnp.concatenate([m_hi, m_lo], axis=0), v_hi)
-    return both[0:32] + (both[32:64] + dot(m_hi, v_lo))
+    both = dot(matrix, jnp.concatenate([v_hi, v_lo], axis=0))
+    return both[0:32] + both[32:64]
+
+
+def with_carry(r, side, carry):
+    rows = r[16 * side : 16 * side + 16]
+    if carry is None:
+        return rows
+    sub = lax.broadcasted_iota(jnp.int32, rows.shape, 0)
+    return rows + jnp.where(sub == 0, carry, 0.0)
 
 
 def own_kernel(u_hbm, after_ref, f_ref, mass_ref, left_ref, diff_ref, q_in, m_in, q_ref, m_ref, u_ref, sems):
@@ -312,8 +329,8 @@
     q_ref[c, 0] = shared
 
 
-def merge_kernel(flags_ref, one_ref, two_ref, own_south_ref, own_north_ref, south_ref, north_ref):
-    even = flags_ref[2] != 0
+def merge_kernel(one_ref, two_ref, own_south_ref, own_north_ref, south_ref, north_ref):
+    even = even_column()
     for out, own, at in ((south_ref, own_south_ref, 0), (north_ref, own_north_ref, 7)):
         out[10:57, :] = own[1:48, :]
         for g in range(GROUPS - 1):
@@ -327,8 +344,8 @@
         out[67:72, :] = jnp.zeros((5, LANES), F32)
 
 
-def halo_kernel(flags_ref, one_ref, two_ref, left_ref, rim_ref, diff_ref, near_ref, m_ref, e_ref, west_ref, east_ref):
-    even = flags_ref[2] != 0
+def halo_kernel(one_ref, two_ref, own_e_ref, left_ref, rim_ref, diff_ref, near_ref, m_ref, e_ref, west_ref, east_ref, quads_ref):
+    even = even_column()
     west_ref[...] = either(even, one_ref[...], two_ref[...])
     east_ref[...] = either(even, two_ref[...], one_ref[...])
     for side, ref in enumerate((west_ref, east_ref)):
@@ -340,11 +357,30 @@
             fs = [x[:, HALO * t + k : HALO * t + k + 1] for t in range(3)]
             m_ref[HALO * side + k] = form(left_ref, diff_ref, fs)
             e_ref[HALO * side + k] = form(rim_ref, near_ref, end_rows(fs))[0:8]
-
-
-def edge_masks(flags_ref):
+    put_quads(rim_matrix(own_e_ref, e_ref), quads_ref)
+
+
+def put_quads(matrix, quads_ref):
+    for q in range(QUADS):
+        columns = range(4 * q, 4 * q + 4)
+        quads_ref[q] = quad([matrix(e) if e < WIDE else jnp.zeros((8, 32), F32) for e in columns])
+
+
+def place():
+    return lax.axis_index("face") * 64 + lax.axis_index("blk")
+
+
+def even_column():
+    return lax.rem(lax.div(place(), PY), 2) == 0
+
+
+def has_side(side):
+    return lax.rem(place(), PY) != (0, PY - 1)[side]
+
+
+def edge_masks():
     sub = lax.broadcasted_iota(jnp.int32, (8, LANES), 0)
-    return (sub == 0) & (flags_ref[0] != 0), (sub == 7) & (flags_ref[1] != 0)
+    return (sub == 0) & (has_side(0)), (sub == 7) & (has_side(1))
 
 
 def first_tile(value, south_ref, row, masks):
@@ -398,49 +434,42 @@
     return part
 
 
-def edges(part, lo, scaled, flags_ref, from_south_ref, from_north_ref, matrix, south_ref, north_ref):
+def edges(part, lo, scales, from_south_ref, from_north_ref, quads_ref, south_ref, north_ref):
     hi = WIDE - 1 - lo
-    masks = edge_masks(flags_ref)
-    res = {}
-    scale = {}
-    for first in range(0, WIDE, 4):
-        values, es = [], []
-        for e in range(first, first + 4):
+    masks = edge_masks()
+    start, stop = 3 * (lo + 1), 3 * (hi - 1) + 4
+    carry = [None, None]
+    for q in range(QUADS):
+        values = []
+        for e in range(4 * q, 4 * q + 4):
             if lo <= e <= hi:
                 value = rim_value(part, e, lo, from_south_ref, from_north_ref, masks)
-                if not scaled:
-                    inverse = 1.0 / value[:, FL : FL + 1]
-                    value = value * inverse
-                    for i in range(4):
-                        scale[e, i] = (inverse[8 * i : 8 * i + 1], inverse[8 * i + 7 : 8 * i + 8])
+                if scales is not None:
+                    value = value * (1.0 / value[:, FL : FL + 1])
                 values.append(value)
-                es.append(matrix(e))
             else:
                 values.append(jnp.zeros((32, LANES), F32))
-                es.append(jnp.zeros((8, 32), F32))
-        r = rim_product(es, jnp.concatenate(values, axis=0))
-        for k in range(4):
-            res[first + k] = r[8 * k : 8 * k + 8]
-    first, final = lo + 1, hi - 1
-    for side, out in enumerate((south_ref, north_ref)):
-        for e in range(first, final + 1):
-            for i in range(4 if e == final else 3):
-                row = 3 * (e - first) + i
-                value = res[e][4 * side + i : 4 * side + i + 1]
-                if i == 0:
-                    value = value + res[e - 1][4 * side + 3 : 4 * side + 4]
-                if i == 3:
-                    value = value + res[e + 1][4 * side : 4 * side + 1]
-                if not scaled:
-                    value = value * scale[e, i][side]
-                out[row : row + 1, :] = value
-        used = 3 * (final - first + 1) + 1
-        out[used:, :] = jnp.zeros((out.shape[0] - used, LANES), F32)
-
-
-def second_edges(flags_ref, q_ref, west_ref, east_ref, e_ref, halo_e_ref, from_south_ref, from_north_ref, south_ref, north_ref):
+        r = rim_product(quads_ref[q], jnp.concatenate(values, axis=0))
+        for side, out in enumerate((south_ref, north_ref)):
+            rows = with_carry(r, side, carry[side])
+            carry[side] = rows[12:13]
+            a, b = max(start, 12 * q), min(stop, 12 * q + 12)
+            if a < b:
+                rows = rows[a - 12 * q : b - 12 * q]
+                if scales is not None:
+                    rows = rows * scales[side][a:b]
+                out[a - start : b - start, :] = rows
+    for out in (south_ref, north_ref):
+        out[stop - start :, :] = jnp.zeros((out.shape[0] - stop + start, LANES), F32)
+
+
+def second_edges(q_ref, west_ref, east_ref, quads_ref, sent_south_ref, sent_north_ref, from_south_ref, from_north_ref, south_ref, north_ref):
+    scales = []
+    for side, (sent, got) in enumerate(((sent_south_ref, from_south_ref), (sent_north_ref, from_north_ref))):
+        other = jnp.where(has_side(side), got[:, FL : FL + 1], 0.0)
+        scales.append(1.0 / (sent[:, FL : FL + 1] + other))
     part = rim_part(q_ref, west_ref, east_ref)
-    edges(part, 0, False, flags_ref, from_south_ref, from_north_ref, rim_matrix(e_ref, halo_e_ref), south_ref, north_ref)
+    edges(part, 0, scales, from_south_ref, from_north_ref, quads_ref, south_ref, north_ref)
 
 
 def rim_matrix(e_ref, halo_e_ref):
@@ -452,29 +481,21 @@
     return matrix
 
 
-def split_matrix(inner_ref, outer_ref):
-    def matrix(e):
-        inner, k = split_at(e)
-        return (inner_ref if inner else outer_ref)[k]
-
-    return matrix
-
-
-def third_edges(flags_ref, inner_ref, outer_ref, joint_ref, in_e_ref, out_e_ref, from_south_ref, from_north_ref, south_ref, north_ref):
+def third_edges(inner_ref, outer_ref, joint_ref, quads_ref, from_south_ref, from_north_ref, south_ref, north_ref):
     sub = lax.broadcasted_iota(jnp.int32, (8, LANES), 0)
     whole = split_part(inner_ref, outer_ref, joint_ref)
 
     def part(e, i):
         return jnp.where(sub < 4, whole(e, i, 0, 8), whole(e, i, 24, 32))
 
-    edges(part, 1, True, flags_ref, from_south_ref, from_north_ref, split_matrix(in_e_ref, out_e_ref), south_ref, north_ref)
-
-
-def fourth_edges(flags_ref, f_ref, in_e_ref, out_e_ref, from_south_ref, from_north_ref, south_ref, north_ref):
+    edges(part, 1, None, from_south_ref, from_north_ref, quads_ref, south_ref, north_ref)
+
+
+def fourth_edges(f_ref, quads_ref, from_south_ref, from_north_ref, south_ref, north_ref):
     def part(e, i):
         return both_ends(f_ref, e, i)
 
-    edges(part, 2, True, flags_ref, from_south_ref, from_north_ref, split_matrix(in_e_ref, out_e_ref), south_ref, north_ref)
+    edges(part, 2, None, from_south_ref, from_north_ref, quads_ref, south_ref, north_ref)
 
 
 def join(out_ref, e, q):
@@ -523,18 +544,18 @@
     scaled_ref[k] = rim * rows
 
 
-def second_inner(flags_ref, q_ref, e_ref, from_south_ref, from_north_ref, m_ref, out_ref, twice_ref, lo_ref, scaled_ref):
+def second_inner(q_ref, e_ref, from_south_ref, from_north_ref, m_ref, out_ref, twice_ref, lo_ref, scaled_ref):
     def part(e, i, a, b):
         return q_ref[e - HALO, i, a:b]
 
-    masks = edge_masks(flags_ref)
+    masks = edge_masks()
     for k, e in enumerate(INNER):
         value = column_value(part, e, 0, from_south_ref, from_north_ref, masks)
         second_column(value, m_ref[e - HALO], k, e_ref[e - HALO], out_ref, k > 0, twice_ref, lo_ref, scaled_ref)
 
 
-def second_outer(flags_ref, q_ref, west_ref, east_ref, one_rest_ref, two_rest_ref, spread_rim_ref, spread_ref, e_ref, halo_e_ref, from_south_ref, from_north_ref, m_ref, mh_ref, inner_ref, out_ref, joint_ref, twice_ref, lo_ref, scaled_ref):
-    even = flags_ref[2] != 0
+def second_outer(q_ref, west_ref, east_ref, one_rest_ref, two_rest_ref, spread_rim_ref, spread_ref, e_ref, halo_e_ref, from_south_ref, from_north_ref, m_ref, mh_ref, inner_ref, in_e_ref, out_ref, joint_ref, twice_ref, lo_ref, scaled_ref, quads_ref):
+    even = even_column()
     rests = (either(even, one_rest_ref[...], two_rest_ref[...]), either(even, two_rest_ref[...], one_rest_ref[...]))
     wide = [
         moved_rows(spread_rim_ref[...], rim[0:RIM]) + moved_rows(spread_ref[...], rest)
@@ -553,7 +574,7 @@
         g = 32 * group_of(k, i)
         return wide[side][g + a : g + b]
 
-    masks = edge_masks(flags_ref)
+    masks = edge_masks()
     for k, e in enumerate(OUTER):
         value = column_value(part, e, 0, from_south_ref, from_north_ref, masks)
         if e < HALO:
@@ -567,6 +588,12 @@
     joint_ref[0] = out_ref[half - 1, 3] + inner_ref[0, 0]
     joint_ref[1] = inner_ref[len(INNER) - 1, 3] + out_ref[half, 0]
 
+    def matrix(e):
+        inner, k = split_at(e)
+        return (in_e_ref if inner else scaled_ref)[k]
+
+    put_quads(matrix, quads_ref)
+
 
 def matrices(e, inner, outer):
     is_inner, k = split_at(e)
@@ -574,9 +601,9 @@
     return twice_ref[k], lo_ref[k]
 
 
-def third_full(flags_ref, inner_ref, outer_ref, joint_ref, from_south_ref, from_north_ref, in_twice, in_lo, out_twice, out_lo, u_ref, out_ref, kept_ref):
+def third_full(inner_ref, outer_ref, joint_ref, from_south_ref, from_north_ref, in_twice, in_lo, out_twice, out_lo, u_ref, out_ref, kept_ref):
     part = split_part(inner_ref, outer_ref, joint_ref)
-    masks = edge_masks(flags_ref)
+    masks = edge_masks()
     for e in range(1, WIDE - 1):
         value = column_value(part, e, 1, from_south_ref, from_north_ref, masks)
         if HALO <= e < HALO + EX:
@@ -585,11 +612,11 @@
         put(out_ref, e, 1, applied(*matrices(e, (in_twice, in_lo), (out_twice, out_lo)), value))
 
 
-def fourth_full(flags_ref, f_ref, from_south_ref, from_north_ref, in_twice, in_lo, out_twice, out_lo, kept_ref, out_ref, rim_south_ref, rim_north_ref, z_ref):
+def fourth_full(f_ref, from_south_ref, from_north_ref, in_twice, in_lo, out_twice, out_lo, kept_ref, out_ref, rim_south_ref, rim_north_ref, z_ref):
     def part(e, i, a, b):
         return f_ref[e, i, a:b]
 
-    masks = edge_masks(flags_ref)
+    masks = edge_masks()
     for e in range(2, WIDE - 2):
         value = column_value(part, e, 2, from_south_ref, from_north_ref, masks)
         put(z_ref, e, 2, applied(*matrices(e, (in_twice, in_lo), (out_twice, out_lo)), value))
@@ -602,10 +629,10 @@
             rim_north_ref[c] = done[:, 7]
 
 
-def patch_kernel(flags_ref, old_ref, rim_south_ref, rim_north_ref, from_south_ref, from_north_ref, out_ref, south_buf, north_buf, sems):
+def patch_kernel(old_ref, rim_south_ref, rim_north_ref, from_south_ref, from_north_ref, out_ref, south_buf, north_buf, sems):
     del old_ref
     sub = lax.broadcasted_iota(jnp.int32, (4, FL), 0)
-    masks = ((sub == 0) & (flags_ref[0] != 0), (sub == 3) & (flags_ref[1] != 0))
+    masks = ((sub == 0) & (has_side(0)), (sub == 3) & (has_side(1)))
     copies = []
     for b in range(0, EX, 4):
         for side, (rim, got, buf) in enumerate(
@@ -625,7 +652,6 @@
 
 
 VM = pl.BlockSpec(memory_space=pltpu.VMEM)
-SM = pl.BlockSpec(memory_space=pltpu.SMEM)
 ANY = pl.BlockSpec(memory_space=pl.ANY)
 HBM = pl.BlockSpec(memory_space=pltpu.HBM)
 
@@ -666,26 +692,23 @@
 def per_device(state, jacobian, metric_xx, metric_yy, metric_xy):
     left, rim, diff, near, spread_rim, spread = (jnp.asarray(t) for t in tables())
     flat = [jnp.transpose(g[0], (1, 2, 3, 0)).reshape(PTS, EX) for g in (jacobian, metric_xx, metric_yy, metric_xy)]
-    index = lax.axis_index(AXES)
-    row = index % PY
-    flags = jnp.stack([row != 0, row != PY - 1, index // PY % 2 == 0]).astype(jnp.int32)
     rows = lambda n: ((n, LANES), F32)
     wide = ((WIDE, 4, 32, LANES), F32)
     pinned = lambda *ts: [pltpu.with_memory_space_constraint(t, pltpu.HBM) for t in ts]
     four = (HALO + 1, 4, 8, 4, FL)
 
     own = [((EX, 4, 32, LANES), F32), ((EX, PTS, PTS), F32)]
-    rim_one, layers_one, other, f, mass, left_in, diff_in, q, m = call(
+    rim_one, layers_one, other, f, mass, left_in, diff_in, rim_in, near_in, low, high, q, m = call(
         first_kernel,
-        [rows(SENT), rows(32 * GROUPS), (four, F32), ((3, PTS, EX), F32), ((PTS, EX), F32), (left.shape, BF16), (diff.shape, F32), *own],
-        [SM] + [HBM] * 7,
+        [rows(SENT), rows(32 * GROUPS), (four, F32), ((3, PTS, EX), F32), ((PTS, EX), F32), (left.shape, BF16), (diff.shape, F32), (rim.shape, BF16), (near.shape, F32), *[((EX, 4, 4, FL), F32)] * 2, *own],
+        [HBM] * 9,
         "first",
-        scratch=[pltpu.VMEM(four, F32), *[pltpu.VMEM((PTS, EX), F32)] * 4, pltpu.SemaphoreType.DMA((8,))],
-    )(flags, *pinned(state, *flat, left, diff))
+        scratch=[pltpu.VMEM(four, F32), *[pltpu.VMEM((PTS, EX), F32)] * 4, pltpu.SemaphoreType.DMA((12,))],
+    )(*pinned(state, *flat, left, diff, rim, near))
     one = swapped(rim_one, 1)
     rim_two, layers_two, q, m = call(
-        other_kernel, [rows(SENT), rows(32 * GROUPS), *own], [SM] + [VM] * 7, "other", aliases={6: 2, 7: 3}
-    )(flags, other, f, mass, left_in, diff_in, q, m)
+        other_kernel, [rows(SENT), rows(32 * GROUPS), *own], [VM] * 7, "other", aliases={5: 2, 6: 3}
+    )(other, f, mass, left_in, diff_in, q, m)
     two = swapped(rim_two, 0)
     rest_one, rest_two = call(rest_kernel, [rows(176)] * 2, [VM] * 2, "rest")(layers_one, layers_two)
     rest_one = swapped(rest_one, 1)
@@ -693,12 +716,10 @@
     e, own_south, own_north = call(
         rows_kernel,
         [((EX, 8, 32), F32), rows(56), rows(56)],
-        [HBM] * 3 + [VM] * 2,
+        [VM] * 6,
         "rows",
-        scratch=[pltpu.VMEM((EX, 4, 4, FL), F32)] * 2
-        + [pltpu.VMEM(rim.shape, BF16), pltpu.VMEM(near.shape, F32), pltpu.SemaphoreType.DMA((4,))],
-    )(*pinned(state, rim, near), f, mass)
-    to_south, to_north = call(merge_kernel, [rows(72)] * 2, [SM] + [VM] * 4, "merge")(flags, one, two, own_south, own_north)
+    )(low, high, rim_in, near_in, f, mass)
+    to_south, to_north = call(merge_kernel, [rows(72)] * 2, [VM] * 4, "merge")(one, two, own_south, own_north)
     south1, north1 = across(to_south, to_north)
     q, m = call(
         own_kernel,
@@ -708,50 +729,50 @@
         scratch=[pltpu.VMEM((8, 4, 8, 4, FL), F32), pltpu.SemaphoreType.DMA((2,))],
         aliases={6: 0, 7: 1},
     )(*pinned(state), to_south, f, mass, left_in, diff_in, q, m)
-    mh, halo_e, west, east = call(
+    mh, halo_e, west, east, quads = call(
         halo_kernel,
-        [((2 * HALO, PTS, PTS), F32), ((2 * HALO, 8, 32), F32), rows(SENT), rows(SENT)],
-        [SM] + [VM] * 6,
+        [((2 * HALO, PTS, PTS), F32), ((2 * HALO, 8, 32), F32), rows(SENT), rows(SENT), ((QUADS, 64, 2 * PTS), BF16)],
+        [VM] * 7,
         "halo",
-    )(flags, one, two, left_in, rim, diff_in, near)
-    to_south, to_north = call(second_edges, [rows(64)] * 2, [SM] + [VM] * 7, "edges2")(
-        flags, q, west, east, e, halo_e, south1, north1
+    )(one, two, e, left_in, rim_in, diff_in, near_in)
+    to_south, to_north = call(second_edges, [rows(64)] * 2, [VM] * 8, "edges2")(
+        q, west, east, quads, to_south, to_north, south1, north1
     )
     south2, north2 = across(to_south, to_north)
     matrix = lambda n: [((n, PTS, 2 * PTS), BF16), ((n, PTS, PTS), BF16), ((n, 8, 32), F32)]
-    inner, in_twice, in_lo, in_pairs = call(
-        second_inner, [((14, 4, 32, LANES), F32), *matrix(14)], [SM] + [VM] * 5, "inner2"
-    )(flags, q, e, south1, north1, m)
-    outer, joint, out_twice, out_lo, out_pairs = call(
-        second_outer, [((8, 4, 32, LANES), F32), ((2, 32, LANES), F32), *matrix(8)], [SM] + [VM] * 14, "outer2"
-    )(flags, q, west, east, rest_one, rest_two, spread_rim, spread, e, halo_e, south1, north1, m, mh, inner)
-    to_south, to_north = call(third_edges, [rows(56)] * 2, [SM] + [VM] * 7, "edges3")(
-        flags, inner, outer, joint, in_pairs, out_pairs, south2, north2
+    inner, in_twice, in_lo, in_e = call(
+        second_inner, [((14, 4, 32, LANES), F32), *matrix(14)], [VM] * 5, "inner2"
+    )(q, e, south1, north1, m)
+    outer, joint, out_twice, out_lo, _, quads = call(
+        second_outer, [((8, 4, 32, LANES), F32), ((2, 32, LANES), F32), *matrix(8), ((QUADS, 64, 2 * PTS), BF16)], [VM] * 15, "outer2"
+    )(q, west, east, rest_one, rest_two, spread_rim, spread, e, halo_e, south1, north1, m, mh, inner, in_e)
+    to_south, to_north = call(third_edges, [rows(56)] * 2, [VM] * 6, "edges3")(
+        inner, outer, joint, quads, south2, north2
     )
     south3, north3 = across(to_south, to_north)
-    f, kept = call(third_full, [wide, ((EX, PTS, FL), F32)], [SM] + [VM] * 10, "full3")(
-        flags, inner, outer, joint, south2, north2, in_twice, in_lo, out_twice, out_lo, state
-    )
-    to_south, to_north = call(fourth_edges, [rows(56)] * 2, [SM] + [VM] * 5, "edges4")(
-        flags, f, in_pairs, out_pairs, south3, north3
+    f, kept = call(third_full, [wide, ((EX, PTS, FL), F32)], [VM] * 10, "full3")(
+        inner, outer, joint, south2, north2, in_twice, in_lo, out_twice, out_lo, state
+    )
+    to_south, to_north = call(fourth_edges, [rows(56)] * 2, [VM] * 4, "edges4")(
+        f, quads, south3, north3
     )
     south4, north4 = across(to_south, to_north)
     out, rim_south, rim_north = call(
         fourth_full,
         [((1, EX, 4, 8, 4, FL), F32), ((EX, 4, 4, FL), F32), ((EX, 4, 4, FL), F32)],
-        [SM] + [VM] * 8,
+        [VM] * 8,
         "full4",
         scratch=[pltpu.VMEM((WIDE, 4, 32, LANES), F32)],
-    )(flags, f, south3, north3, in_twice, in_lo, out_twice, out_lo, kept)
+    )(f, south3, north3, in_twice, in_lo, out_twice, out_lo, kept)
     (out,) = call(
         patch_kernel,
         [((1, EX, 4, 8, 4, FL), F32)],
-        [SM, ANY] + [VM] * 4,
+        [ANY] + [VM] * 4,
         "patch",
         scratch=[pltpu.VMEM((EX, 4, 4, FL), F32), pltpu.VMEM((EX, 4, 4, FL), F32), pltpu.SemaphoreType.DMA((8,))],
         out_specs=[ANY],
-        aliases={1: 0},
-    )(flags, out, rim_south, rim_north, south4, north4)
+        aliases={0: 0},
+    )(out, rim_south, rim_north, south4, north4)
     return out
 
 

time: 58.1 us -> 54.8 us (0.943)
  Pallas kernels: 28 us -> 20.4 us
  waiting for transfers between devices: 6.61 us -> 11.2 us
    pallas_call x9, Pallas kernels: 13.5 us -> 7.75 us  [the longest x1 1.74 us: per_device(): call(third_full, [wide, ((EX, PTS, FL), F32)], [VM] * 10, 'full3')]
    ppermute x8, waiting for transfers between devices: 6.38 us -> 10.2 us  [moved(): return lax.ppermute(array, AXES, pairs)]
    ppermute x4, waiting for transfers between devices: 0.22 us -> 1.05 us  [swapped(): return lax.ppermute(array, AXES, pairs)]
    pallas_call x1, Pallas kernels: 3.58 us -> 2.95 us  [per_device(): call(first_kernel, [rows(SENT), rows(32 * GROUPS), (four, F32), ((3, PTS,...]
  transfers between devices with their start and end apart: 12 -> 12, of which waited for: 5 -> 5; matrix products, arithmetic and copies ran while one was open for 0% -> 0% of each run, Pallas kernels for 36% -> 29%
where the time goes in v1:
time: 54.8 us; the launch traced here: 54.6 us
  starting transfers between devices  22.6 us (41%)
  Pallas kernels  20.4 us (37%)
  waiting for transfers between devices  11.2 us (20%)
    ppermute x4, starting transfers between devices, swapped(): return lax.ppermute(array, AXES, pairs)  15.1 us
    ppermute x8, waiting for transfers between devices, moved(): return lax.ppermute(array, AXES, pairs)  10.2 us
    ppermute x8, starting transfers between devices, moved(): return lax.ppermute(array, AXES, pairs)  7.51 us
    pallas_call x1, Pallas kernels, per_device(): call(own_kernel, own, [HBM, ANY] + [VM] * 6, 'own', scratch=[pltpu.VMEM((...  3.33 us
    pallas_call x1, Pallas kernels, per_device(): call(fourth_full, [((1, EX, 4, 8, 4, FL), F32), ((EX, 4, 4, FL), F32), ((...  3.19 us
    pallas_call x1, Pallas kernels, per_device(): call(first_kernel, [rows(SENT), rows(32 * GROUPS), (four, F32), ((3, PTS,...  2.95 us
    pallas_call x1, Pallas kernels, per_device(): call(second_outer, [((8, 4, 32, LANES), F32), ((2, 32, LANES), F32), *mat...  2.03 us
    pallas_call x1, Pallas kernels, per_device(): call(third_full, [wide, ((EX, PTS, FL), F32)], [VM] * 10, 'full3')  1.74 us
  transfers between devices with their start and end apart: 12, of which 5 were waited for; matrix products, arithmetic and copies ran while one was open for 0% of the time, Pallas kernels for 29%

profile of v1, /device:TPU:1, one launch (start us, length us, event | category | flops | bytes accessed | tf_op | source)
XLA Modules:
  0.0 54.6 jit_solution(1348337353957122405)
XLA Ops:
  0.0 2.9 %first.1 = (f32[88,384]{1,0:T(8,128)S(1)}, f32[320,384]{1,0:T(8,128)S(1)}, f32[4,4,8,4,360]{4,3,2,1,0:T(4,128)S(1)}, f32[3,128,16]{2,1,0:T(8,128)S(1)}, f32[128,...) custom-call(f32[1,16,4,8,4,360]{5,4,3,2,1,0:T(4,128)} %u_ref.1, ...), custom_call_target="tpu_custom_call" | custom-call | tf_op jit(solution)/shard_map/first/pallas_call | solution.py:701
  3.0 11.8 %collective-permute-start = (f32[88,384]{1,0:T(8,128)S(1)}, f32[88,384]{1,0:T(8,128)S(1)}, u32[]{:S(2)}, u32[]{:S(2)}) collective-permute-start(f32[88,384]{1,0:T(8,128)S(1)} %get-tuple-element.56), channel_id=1, source_target_pairs={{0,248},{1,249},{2,250},{3,251},{4,252},{5,253},{6,254},{7,255},{8... | collective-permute-start | bytes 405512 | tf_op jit(solution)/shard_map/ppermute | solution.py:685
  14.7 1.4 %other.1 = (f32[88,384]{1,0:T(8,128)S(1)}, f32[320,384]{1,0:T(8,128)S(1)}, f32[16,4,32,384]{3,2,1,0:T(8,128)S(1)}, f32[16,128,128]{2,1,0:T(8,128)S(1)}) custom-call(f32[4,4,8,4,360]{4,3,2,1,0:T(4,128)S(1)} %get-tuple-element.57.u_ref, f32[3,128,16]{2,1,0:T(8,128)S(1)} %get-tuple-element.58.f_ref, ...), custom_call_target="tpu_custom_call", output_to_operand_aliasing={{2}: (5, {}), {3}: (6, {})} | custom-call | tf_op jit(solution)/shard_map/other/pallas_call | solution.py:709
  16.1 0.1 collective-permute-start.1
  16.2 0.2 rest.1
  16.3 3.3 %collective-permute-start.4 = (f32[176,384]{1,0:T(8,128)S(1)}, f32[176,384]{1,0:T(8,128)S(1)}, u32[]{:S(2)}, u32[]{:S(2)}) collective-permute-start(f32[176,384]{1,0:T(8,128)S(1)} %get-tuple-element.83), channel_id=1, source_target_pairs={{0,248},{1,249},{2,250},{3,251},{4,252},{5,253},{6,254},{7,255},{8... | collective-permute-start | bytes 811016 | tf_op jit(solution)/shard_map/ppermute | solution.py:685
  19.6 0.0 collective-permute-start.5
  19.6 0.8 %rows.1 = (f32[16,8,32]{2,1,0:T(8,128)S(1)}, f32[56,384]{1,0:T(8,128)S(1)}, f32[56,384]{1,0:T(8,128)S(1)}) custom-call(f32[16,4,4,360]{3,2,1,0:T(4,128)S(1)} %get-tuple-element.65.low_ref, f32[16,4,4,360]{3,2,1,0:T(4,128)S(1)} %get-tuple-element.66.high_ref, bf16[2,16,64]{2,1,0:T(8,128)(2,1)S(1)} %get-tuple-element.67.rim_ref, ...), custom_call_target="tpu_custom_call" | custom-call | tf_op jit(solution)/shard_map/rows/pallas_call | solution.py:716
  20.5 1.0 %collective-permute-done.1.two_ref = f32[88,384]{1,0:T(8,128)S(1)} collective-permute-done((f32[88,384]{1,0:T(8,128)S(1)}, f32[88,384]{1,0:T(8,128)S(1)}, u32[]{:S(2)}, u32[]{:S(2)}) %collective-permute-start.1) | collective-permute-done | bytes 135200 | tf_op jit(solution)/shard_map/ppermute | solution.py:685
  21.5 4.4 %collective-permute-start.2 = (f32[72,384]{1,0:T(8,128)S(1)}, f32[72,384]{1,0:T(8,128)S(1)}, u32[]{:S(2)}, u32[]{:S(2)}) collective-permute-start(f32[72,384]{1,0:T(8,128)S(1)} %get-tuple-element.76.sent_north_ref), channel_id=1, source_target_pairs={{0,1},{1,2},{2,3},{3,4},{4,5},{5,6},{6,7},{7,0},{8,9},{9,10},{10,1... | collective-permute-start | bytes 331784 | tf_op jit(solution)/shard_map/ppermute | solution.py:677
  26.0 3.3 %own.1 = (f32[16,4,32,384]{3,2,1,0:T(8,128)S(1)}, f32[16,128,128]{2,1,0:T(8,128)S(1)}) custom-call(f32[1,16,4,8,4,360]{5,4,3,2,1,0:T(4,128)} %u_ref.1, f32[72,384]{1,0:T(8,128)S(1)} %get-tuple-element.71.after_ref.sent_south_ref, f32[3,128,16]{2,1,0:T(8,128)S(1)} %get-tuple-element.58.f_ref, ...), custom_call_target="tpu_custom_call", output_to_operand_aliasing={{0}: (6, {}), {1}: (7, {})} | custom-call | tf_op jit(solution)/shard_map/own/pallas_call | solution.py:724
  29.3 1.0 %halo.1 = (f32[6,128,128]{2,1,0:T(8,128)S(1)}, f32[6,8,32]{2,1,0:T(8,128)S(1)}, f32[88,384]{1,0:T(8,128)S(1)}, f32[88,384]{1,0:T(8,128)S(1)}, bf16[6,64,256]{2,1,0:T(8,128)(2,1)S(1)}) custom-call(f32[88,384]{1,0:T(8,128)S(1)} %collective-permute-done.one_ref, f32[88,384]{1,0:T(8,128)S(1)} %collective-permute-done.1.two_ref, ...), custom_call_target="tpu_custom_call" | custom-call | tf_op jit(solution)/shard_map/halo/pallas_call | solution.py:732
  30.3 4.3 %collective-permute-done.3.from_north_ref = f32[72,384]{1,0:T(8,128)S(1)} collective-permute-done((f32[72,384]{1,0:T(8,128)S(1)}, f32[72,384]{1,0:T(8,128)S(1)}, u32[]{:S(2)}, u32[]{:S(2)}) %collective-permute-start.3) | collective-permute-done | bytes 110624 | tf_op jit(solution)/shard_map/ppermute | solution.py:677
  34.7 0.5 edges2.1
  35.2 0.0 copy-start.1
  35.2 0.0 copy-start.2
  35.2 0.1 collective-permute-start.6
  35.3 0.7 %collective-permute-start.7 = (f32[64,384]{1,0:T(8,128)S(1)}, f32[64,384]{1,0:T(8,128)S(1)}, u32[]{:S(2)}, u32[]{:S(2)}) collective-permute-start(f32[64,384]{1,0:T(8,128)S(1)} %get-tuple-element.92), channel_id=1, source_target_pairs={{0,7},{1,0},{2,1},{3,2},{4,3},{5,4},{6,5},{7,6},{8,15},{9,8},{10,9... | collective-permute-start | bytes 294920 | tf_op jit(solution)/shard_map/ppermute | solution.py:677
  36.0 1.4 %inner2.1 = (f32[14,4,32,384]{3,2,1,0:T(8,128)S(1)}, bf16[14,128,256]{2,1,0:T(8,128)(2,1)S(1)}, bf16[14,128,128]{2,1,0:T(8,128)(2,1)S(1)}, f32[14,8,32]{2,1,0:T(8,128)S(1)}) custom-call(f32[16,4,32,384]{3,2,1,0:T(8,128)S(1)} %get-tuple-element.74.q_ref, f32[16,8,32]{2,1,0:T(8,128)S(1)} %get-tuple-element.75.e_ref.own_e_ref, ...), custom_call_target="tpu_custom_call" | custom-call | tf_op jit(solution)/shard_map/inner2/pallas_call | solution.py:743
  37.5 2.0 %outer2.1 = (f32[8,4,32,384]{3,2,1,0:T(8,128)S(1)}, f32[2,32,384]{2,1,0:T(8,128)S(1)}, bf16[8,128,256]{2,1,0:T(8,128)(2,1)S(1)}, bf16[8,128,128]{2,1,0:T(8,128)(...) custom-call(f32[16,4,32,384]{3,2,1,0:T(8,128)S(1)} %get-tuple-element.74.q_ref, ...), custom_call_target="tpu_custom_call" | custom-call | tf_op jit(solution)/shard_map/outer2/pallas_call | solution.py:746
  39.5 1.2 %collective-permute-done.7.from_north_ref = f32[64,384]{1,0:T(8,128)S(1)} collective-permute-done((f32[64,384]{1,0:T(8,128)S(1)}, f32[64,384]{1,0:T(8,128)S(1)}, u32[]{:S(2)}, u32[]{:S(2)}) %collective-permute-start.7) | collective-permute-done | bytes 98336 | tf_op jit(solution)/shard_map/ppermute | solution.py:677
  40.7 0.5 edges3.1
  41.2 1.0 %collective-permute-start.8 = (f32[56,384]{1,0:T(8,128)S(1)}, f32[56,384]{1,0:T(8,128)S(1)}, u32[]{:S(2)}, u32[]{:S(2)}) collective-permute-start(f32[56,384]{1,0:T(8,128)S(1)} %get-tuple-element.99), channel_id=1, source_target_pairs={{0,1},{1,2},{2,3},{3,4},{4,5},{5,6},{6,7},{7,0},{8,9},{9,10},{10,1... | collective-permute-start | bytes 258056 | tf_op jit(solution)/shard_map/ppermute | solution.py:677
  42.2 0.4 collective-permute-start.9
  42.6 1.7 %full3.1 = (f32[22,4,32,384]{3,2,1,0:T(8,128)S(1)}, f32[16,128,360]{2,1,0:T(8,128)S(1)}) custom-call(f32[14,4,32,384]{3,2,1,0:T(8,128)S(1)} %get-tuple-element.78.inner_ref, f32[8,4,32,384]{3,2,1,0:T(8,128)S(1)} %get-tuple-element.88.outer_ref, f32[2,32,384]{2,1,0:T(8,128)S(1)} %get-tuple-element.89.joint_ref, ...), custom_call_target="tpu_custom_call" | custom-call | tf_op jit(solution)/shard_map/full3/pallas_call | solution.py:753
  44.3 2.7 %collective-permute-done.9.from_north_ref = f32[56,384]{1,0:T(8,128)S(1)} collective-permute-done((f32[56,384]{1,0:T(8,128)S(1)}, f32[56,384]{1,0:T(8,128)S(1)}, u32[]{:S(2)}, u32[]{:S(2)}) %collective-permute-start.9) | collective-permute-done | bytes 86048 | tf_op jit(solution)/shard_map/ppermute | solution.py:677
  47.0 0.4 edges4.1
  47.4 0.1 collective-permute-start.10
  47.5 0.9 %collective-permute-start.11 = (f32[56,384]{1,0:T(8,128)S(1)}, f32[56,384]{1,0:T(8,128)S(1)}, u32[]{:S(2)}, u32[]{:S(2)}) collective-permute-start(f32[56,384]{1,0:T(8,128)S(1)} %get-tuple-element.106), channel_id=1, source_target_pairs={{0,7},{1,0},{2,1},{3,2},{4,3},{5,4},{6,5},{7,6},{8,15},{9,8},{10,9... | collective-permute-start | bytes 258056 | tf_op jit(solution)/shard_map/ppermute | solution.py:677
  48.4 3.2 %full4.1 = (f32[1,16,4,8,4,360]{5,4,3,2,1,0:T(4,128)}, f32[16,4,4,360]{3,2,1,0:T(4,128)S(1)}, f32[16,4,4,360]{3,2,1,0:T(4,128)S(1)}) custom-call(f32[22,4,32,384]{3,2,1,0:T(8,128)S(1)} %get-tuple-element.97.f_ref, f32[56,384]{1,0:T(8,128)S(1)} %collective-permute-done.8.from_south_ref, f32[56,384]{1,0:T(8,128)S(1)} %collective-permute-done.9.from_north_ref, ...), custom_call_target="tpu_custom_call" | custom-call | tf_op jit(solution)/shard_map/full4/pallas_call | solution.py:760
  51.6 1.9 %collective-permute-done.11.from_north_ref = f32[56,384]{1,0:T(8,128)S(1)} collective-permute-done((f32[56,384]{1,0:T(8,128)S(1)}, f32[56,384]{1,0:T(8,128)S(1)}, u32[]{:S(2)}, u32[]{:S(2)}) %collective-permute-start.11) | collective-permute-done | bytes 86048 | tf_op jit(solution)/shard_map/ppermute | solution.py:677
  53.5 1.0 %patch.1 = f32[1,16,4,8,4,360]{5,4,3,2,1,0:T(4,128)} custom-call(f32[1,16,4,8,4,360]{5,4,3,2,1,0:T(4,128)} %get-tuple-element.102.old_ref, f32[16,4,4,360]{3,2,1,0:T(4,128)S(1)} %get-tuple-element.103.rim_south_ref, f32[16,4,4,360]{3,2,1,0:T(4,128)S(1)} %get-tuple-element.104.rim_north_ref, ...), custom_call_target="tpu_custom_call", output_to_operand_aliasing={{}: (0, {})} | custom-call | tf_op jit(solution)/shard_map/patch/pallas_call | solution.py:767
  (13 shorter events, 0.1 us)
Async XLA Ops:
  3.0 17.5 %collective-permute-start = (f32[88,384]{1,0:T(8,128)S(1)}, f32[88,384]{1,0:T(8,128)S(1)}, u32[]{:S(2)}, u32[]{:S(2)}) collective-permute-start(f32[88,384]{1,0:T(8,128)S(1)} %get-tuple-element.56), channel_id=1, source_target_pairs={{0,248},{1,249},{2,250},{3,251},{4,252},{5,253},{6,254},{7,255},{8... | collective-permute-start | bytes 405512 | tf_op jit(solution)/shard_map/ppermute | solution.py:685
  16.1 5.4 %collective-permute-start.1 = (f32[88,384]{1,0:T(8,128)S(1)}, f32[88,384]{1,0:T(8,128)S(1)}, u32[]{:S(2)}, u32[]{:S(2)}) collective-permute-start(f32[88,384]{1,0:T(8,128)S(1)} %get-tuple-element.64), channel_id=1, source_target_pairs={{0,8},{1,9},{2,10},{3,11},{4,12},{5,13},{6,14},{7,15},{8,0},{9,1},... | collective-permute-start | bytes 405512 | tf_op jit(solution)/shard_map/ppermute | solution.py:685
  16.3 21.1 %collective-permute-start.4 = (f32[176,384]{1,0:T(8,128)S(1)}, f32[176,384]{1,0:T(8,128)S(1)}, u32[]{:S(2)}, u32[]{:S(2)}) collective-permute-start(f32[176,384]{1,0:T(8,128)S(1)} %get-tuple-element.83), channel_id=1, source_target_pairs={{0,248},{1,249},{2,250},{3,251},{4,252},{5,253},{6,254},{7,255},{8... | collective-permute-start | bytes 811016 | tf_op jit(solution)/shard_map/ppermute | solution.py:685
  19.6 17.8 %collective-permute-start.5 = (f32[176,384]{1,0:T(8,128)S(1)}, f32[176,384]{1,0:T(8,128)S(1)}, u32[]{:S(2)}, u32[]{:S(2)}) collective-permute-start(f32[176,384]{1,0:T(8,128)S(1)} %get-tuple-element.84), channel_id=1, source_target_pairs={{0,8},{1,9},{2,10},{3,11},{4,12},{5,13},{6,14},{7,15},{8,0},{9,1},... | collective-permute-start | bytes 811016 | tf_op jit(solution)/shard_map/ppermute | solution.py:685
  21.5 8.8 %collective-permute-start.2 = (f32[72,384]{1,0:T(8,128)S(1)}, f32[72,384]{1,0:T(8,128)S(1)}, u32[]{:S(2)}, u32[]{:S(2)}) collective-permute-start(f32[72,384]{1,0:T(8,128)S(1)} %get-tuple-element.76.sent_north_ref), channel_id=1, source_target_pairs={{0,1},{1,2},{2,3},{3,4},{4,5},{5,6},{6,7},{7,0},{8,9},{9,10},{10,1... | collective-permute-start | bytes 331784 | tf_op jit(solution)/shard_map/ppermute | solution.py:677
  26.0 8.7 %collective-permute-start.3 = (f32[72,384]{1,0:T(8,128)S(1)}, f32[72,384]{1,0:T(8,128)S(1)}, u32[]{:S(2)}, u32[]{:S(2)}) collective-permute-start(f32[72,384]{1,0:T(8,128)S(1)} %get-tuple-element.71.after_ref.sent_south_ref), channel_id=1, source_target_pairs={{0,7},{1,0},{2,1},{3,2},{4,3},{5,4},{6,5},{7,6},{8,15},{9,8},{10,9... | collective-permute-start | bytes 331784 | tf_op jit(solution)/shard_map/ppermute | solution.py:677
  35.2 2.3 %copy-start.1 = (bf16[320,176]{1,0:T(8,128)(2,1)S(1)}, bf16[320,176]{1,0:T(8,128)(2,1)}, u32[]{:S(2)}) copy-start(bf16[320,176]{1,0:T(8,128)(2,1)} %constant.17.clone.spread_ref) | copy-start | bytes 337924
  35.2 2.3 %copy-start.2 = (bf16[320,80]{1,0:T(8,128)(2,1)S(1)}, bf16[320,80]{1,0:T(8,128)(2,1)}, u32[]{:S(2)}) copy-start(bf16[320,80]{1,0:T(8,128)(2,1)} %constant.16.clone.spread_rim_ref) | copy-start | bytes 153604
  35.2 4.3 %collective-permute-start.6 = (f32[64,384]{1,0:T(8,128)S(1)}, f32[64,384]{1,0:T(8,128)S(1)}, u32[]{:S(2)}, u32[]{:S(2)}) collective-permute-start(f32[64,384]{1,0:T(8,128)S(1)} %get-tuple-element.91), channel_id=1, source_target_pairs={{0,1},{1,2},{2,3},{3,4},{4,5},{5,6},{6,7},{7,0},{8,9},{9,10},{10,1... | collective-permute-start | bytes 294920 | tf_op jit(solution)/shard_map/ppermute | solution.py:677
  35.3 5.4 %collective-permute-start.7 = (f32[64,384]{1,0:T(8,128)S(1)}, f32[64,384]{1,0:T(8,128)S(1)}, u32[]{:S(2)}, u32[]{:S(2)}) collective-permute-start(f32[64,384]{1,0:T(8,128)S(1)} %get-tuple-element.92), channel_id=1, source_target_pairs={{0,7},{1,0},{2,1},{3,2},{4,3},{5,4},{6,5},{7,6},{8,15},{9,8},{10,9... | collective-permute-start | bytes 294920 | tf_op jit(solution)/shard_map/ppermute | solution.py:677
  39.5 3.0 %copy-start = (f32[1,16,4,8,4,360]{5,4,3,2,1,0:T(4,128)S(1)}, f32[1,16,4,8,4,360]{5,4,3,2,1,0:T(4,128)}, u32[]{:S(2)}) copy-start(f32[1,16,4,8,4,360]{5,4,3,2,1,0:T(4,128)} %u_ref.1) | copy-start | bytes 8847364
  41.2 3.1 %collective-permute-start.8 = (f32[56,384]{1,0:T(8,128)S(1)}, f32[56,384]{1,0:T(8,128)S(1)}, u32[]{:S(2)}, u32[]{:S(2)}) collective-permute-start(f32[56,384]{1,0:T(8,128)S(1)} %get-tuple-element.99), channel_id=1, source_target_pairs={{0,1},{1,2},{2,3},{3,4},{4,5},{5,6},{6,7},{7,0},{8,9},{9,10},{10,1... | collective-permute-start | bytes 258056 | tf_op jit(solution)/shard_map/ppermute | solution.py:677
  42.2 4.8 %collective-permute-start.9 = (f32[56,384]{1,0:T(8,128)S(1)}, f32[56,384]{1,0:T(8,128)S(1)}, u32[]{:S(2)}, u32[]{:S(2)}) collective-permute-start(f32[56,384]{1,0:T(8,128)S(1)} %get-tuple-element.100), channel_id=1, source_target_pairs={{0,7},{1,0},{2,1},{3,2},{4,3},{5,4},{6,5},{7,6},{8,15},{9,8},{10,9... | collective-permute-start | bytes 258056 | tf_op jit(solution)/shard_map/ppermute | solution.py:677
  47.4 4.2 %collective-permute-start.10 = (f32[56,384]{1,0:T(8,128)S(1)}, f32[56,384]{1,0:T(8,128)S(1)}, u32[]{:S(2)}, u32[]{:S(2)}) collective-permute-start(f32[56,384]{1,0:T(8,128)S(1)} %get-tuple-element.105), channel_id=1, source_target_pairs={{0,1},{1,2},{2,3},{3,4},{4,5},{5,6},{6,7},{7,0},{8,9},{9,10},{10,1... | collective-permute-start | bytes 258056 | tf_op jit(solution)/shard_map/ppermute | solution.py:677
  47.5 6.0 %collective-permute-start.11 = (f32[56,384]{1,0:T(8,128)S(1)}, f32[56,384]{1,0:T(8,128)S(1)}, u32[]{:S(2)}, u32[]{:S(2)}) collective-permute-start(f32[56,384]{1,0:T(8,128)S(1)} %get-tuple-element.106), channel_id=1, source_target_pairs={{0,7},{1,0},{2,1},{3,2},{4,3},{5,4},{6,5},{7,6},{8,15},{9,8},{10,9... | collective-permute-start | bytes 258056 | tf_op jit(solution)/shard_map/ppermute | solution.py:677

commit v2 on v1

--- a/solution.py
+++ b/solution.py
@@ -18,8 +18,12 @@
 GROUPS = 3 * HALO + 1
 LINE = 25
 RIM = 8 * GROUPS
-SENT = RIM + 8
 REST = 17
+ROWS = REST * GROUPS
+USED = FL + 1 - 256
+SHARE = USED // 5
+FULL = 142
+PACKED = 488
 TAIL = LANES - FL
 QUADS = -(-WIDE // 4)
 AXES = ("face", "blk")
@@ -154,7 +158,6 @@
 
 
 def side_columns(want_west, u_ref, f, mass, left_ref, diff_ref, rim_out_ref, layers_ref, q_ref, m_ref):
-    lane = lax.broadcasted_iota(jnp.int32, (PTS, PTS), 1)
     raw, part = {}, {}
     flux = jnp.concatenate([fluxes(diff_ref, *column(f, k)) for k in range(HALO + 1)], axis=1)
     together = product(left_ref[0], left_ref[1], flux)
@@ -182,24 +185,48 @@
         for lanes, value in ((slice(0, FL), row), (slice(FL, LANES), tail)):
             rim_out_ref[8 * g : 8 * g + 8, lanes] = jnp.where(sub[:, lanes] < 4, value[0:8], value[24:32])
             layers_ref[32 * g : 32 * g + 32, lanes] = value
-    x = jnp.zeros((PTS, PTS), F32)
+    at = FL + 1
     for t in range(3):
         for k in range(HALO):
-            x = jnp.where(lane == HALO * t + k, either(want_west, f[t][:, k : k + 1], f[t][:, k + 1 : k + 2]), x)
-    x = jnp.transpose(x)
-    rim_out_ref[RIM:SENT, 0:PTS] = x[0:8]
-    rim_out_ref[RIM:SENT, PTS : 2 * PTS] = x[8:16]
-    rim_out_ref[RIM:SENT, 2 * PTS :] = jnp.zeros((8, PTS), F32)
-
-
-def gather_rest(layers_ref, out_ref):
+            value = either(want_west, f[t][:, k : k + 1], f[t][:, k + 1 : k + 2])
+            rim_out_ref[:, at : at + 1] = value[0:RIM]
+            rim_out_ref[0 : PTS - RIM, at + 9 : at + 10] = value[RIM:PTS]
+            at += 1
+
+
+def gather_rest(layers_ref, out_ref, third_ref):
     for g in range(GROUPS):
         for ey in range(1, 7):
             size = 3 if ey < 6 else 2
             to = REST * g + 3 * (ey - 1)
             at = 32 * g + 4 * ey + 1
-            out_ref[to : to + size, :] = layers_ref[at : at + size, :]
-    out_ref[REST * GROUPS :, :] = jnp.zeros((6, LANES), F32)
+            out_ref[to : to + size, :] = layers_ref[at : at + size, 0:128]
+            out_ref[ROWS + to : ROWS + to + size, :] = layers_ref[at : at + size, 128:256]
+            third_ref[to : to + size, :] = layers_ref[at : at + size, 256:384]
+    last = third_ref[FULL:ROWS, :]
+    size = ROWS - FULL
+    lane = lax.broadcasted_iota(jnp.int32, (size, 128), 1)
+    for p in range(5):
+        shifted = pltpu.roll(last, USED - SHARE * p, 1)
+        rows = slice(size * p, size * p + size)
+        out_ref[2 * ROWS + rows.start : 2 * ROWS + rows.stop, :] = jnp.where(lane < USED, third_ref[rows, :], shifted)
+    out_ref[2 * ROWS + 5 * size : 2 * ROWS + FULL, :] = third_ref[5 * size : FULL, :]
+    out_ref[2 * ROWS + FULL :, :] = jnp.zeros((PACKED - 2 * ROWS - FULL, 128), F32)
+
+
+def unpack_rest(got, out_ref):
+    size = ROWS - FULL
+    lane = lax.broadcasted_iota(jnp.int32, (size, 128), 1)
+    out_ref[0:ROWS, 0:128] = got[0:ROWS]
+    out_ref[0:ROWS, 128:256] = got[ROWS : 2 * ROWS]
+    out_ref[0:FULL, 256:384] = got[2 * ROWS : 2 * ROWS + FULL]
+    last = jnp.zeros((size, 128), F32)
+    for p in range(5):
+        at = 2 * ROWS + size * p
+        shifted = pltpu.roll(got[at : at + size], 128 - (USED - SHARE * p), 1)
+        last = jnp.where((lane >= SHARE * p) & (lane < SHARE * p + SHARE), shifted, last)
+    out_ref[FULL:ROWS, 256:384] = last
+    out_ref[ROWS:, :] = jnp.zeros((out_ref.shape[0] - ROWS, LANES), F32)
 
 
 def nearest(want_west, t):
@@ -235,9 +262,9 @@
     side_columns(want_west, u_ref, f, nearest(want_west, mass_ref[...]), left_ref, diff_ref, rim_out_ref, layers_ref, q_ref, m_ref)
 
 
-def rest_kernel(first_ref, other_ref, one_ref, two_ref):
-    gather_rest(first_ref, one_ref)
-    gather_rest(other_ref, two_ref)
+def rest_kernel(first_ref, other_ref, one_ref, two_ref, third_ref):
+    gather_rest(first_ref, one_ref, third_ref)
+    gather_rest(other_ref, two_ref, third_ref)
 
 
 def end_rows(f):
@@ -349,12 +376,10 @@
     west_ref[...] = either(even, one_ref[...], two_ref[...])
     east_ref[...] = either(even, two_ref[...], one_ref[...])
     for side, ref in enumerate((west_ref, east_ref)):
-        x = jnp.concatenate(
-            [ref[RIM:SENT, 0:PTS], ref[RIM:SENT, PTS : 2 * PTS], jnp.zeros((PTS - 16, PTS), F32)], axis=0
-        )
-        x = jnp.transpose(x)
+        at = FL + 1
         for k in range(HALO):
-            fs = [x[:, HALO * t + k : HALO * t + k + 1] for t in range(3)]
+            lanes = [at + HALO * t + k for t in range(3)]
+            fs = [jnp.concatenate([ref[:, a : a + 1], ref[0 : PTS - RIM, a + 9 : a + 10]], axis=0) for a in lanes]
             m_ref[HALO * side + k] = form(left_ref, diff_ref, fs)
             e_ref[HALO * side + k] = form(rim_ref, near_ref, end_rows(fs))[0:8]
     put_quads(rim_matrix(own_e_ref, e_ref), quads_ref)
@@ -554,11 +579,13 @@
         second_column(value, m_ref[e - HALO], k, e_ref[e - HALO], out_ref, k > 0, twice_ref, lo_ref, scaled_ref)
 
 
-def second_outer(q_ref, west_ref, east_ref, one_rest_ref, two_rest_ref, spread_rim_ref, spread_ref, e_ref, halo_e_ref, from_south_ref, from_north_ref, m_ref, mh_ref, inner_ref, in_e_ref, out_ref, joint_ref, twice_ref, lo_ref, scaled_ref, quads_ref):
+def second_outer(q_ref, west_ref, east_ref, one_rest_ref, two_rest_ref, spread_rim_ref, spread_ref, e_ref, halo_e_ref, from_south_ref, from_north_ref, m_ref, mh_ref, inner_ref, in_e_ref, out_ref, joint_ref, twice_ref, lo_ref, scaled_ref, quads_ref, rest_a, rest_b):
     even = even_column()
-    rests = (either(even, one_rest_ref[...], two_rest_ref[...]), either(even, two_rest_ref[...], one_rest_ref[...]))
+    unpack_rest(either(even, one_rest_ref[...], two_rest_ref[...]), rest_a)
+    unpack_rest(either(even, two_rest_ref[...], one_rest_ref[...]), rest_b)
+    rests = (rest_a[...], rest_b[...])
     wide = [
-        moved_rows(spread_rim_ref[...], rim[0:RIM]) + moved_rows(spread_ref[...], rest)
+        moved_rows(spread_rim_ref[...], rim[...]) + moved_rows(spread_ref[...], rest)
         for rim, rest in zip((west_ref, east_ref), rests)
     ]
 
@@ -700,17 +727,19 @@
     own = [((EX, 4, 32, LANES), F32), ((EX, PTS, PTS), F32)]
     rim_one, layers_one, other, f, mass, left_in, diff_in, rim_in, near_in, low, high, q, m = call(
         first_kernel,
-        [rows(SENT), rows(32 * GROUPS), (four, F32), ((3, PTS, EX), F32), ((PTS, EX), F32), (left.shape, BF16), (diff.shape, F32), (rim.shape, BF16), (near.shape, F32), *[((EX, 4, 4, FL), F32)] * 2, *own],
+        [rows(RIM), rows(32 * GROUPS), (four, F32), ((3, PTS, EX), F32), ((PTS, EX), F32), (left.shape, BF16), (diff.shape, F32), (rim.shape, BF16), (near.shape, F32), *[((EX, 4, 4, FL), F32)] * 2, *own],
         [HBM] * 9,
         "first",
         scratch=[pltpu.VMEM(four, F32), *[pltpu.VMEM((PTS, EX), F32)] * 4, pltpu.SemaphoreType.DMA((12,))],
     )(*pinned(state, *flat, left, diff, rim, near))
     one = swapped(rim_one, 1)
     rim_two, layers_two, q, m = call(
-        other_kernel, [rows(SENT), rows(32 * GROUPS), *own], [VM] * 7, "other", aliases={5: 2, 6: 3}
+        other_kernel, [rows(RIM), rows(32 * GROUPS), *own], [VM] * 7, "other", aliases={5: 2, 6: 3}
     )(other, f, mass, left_in, diff_in, q, m)
     two = swapped(rim_two, 0)
-    rest_one, rest_two = call(rest_kernel, [rows(176)] * 2, [VM] * 2, "rest")(layers_one, layers_two)
+    rest_one, rest_two = call(
+        rest_kernel, [((PACKED, 128), F32)] * 2, [VM] * 2, "rest", scratch=[pltpu.VMEM((176, 128), F32)]
+    )(layers_one, layers_two)
     rest_one = swapped(rest_one, 1)
     rest_two = swapped(rest_two, 0)
     e, own_south, own_north = call(
@@ -731,7 +760,7 @@
     )(*pinned(state), to_south, f, mass, left_in, diff_in, q, m)
     mh, halo_e, west, east, quads = call(
         halo_kernel,
-        [((2 * HALO, PTS, PTS), F32), ((2 * HALO, 8, 32), F32), rows(SENT), rows(SENT), ((QUADS, 64, 2 * PTS), BF16)],
+        [((2 * HALO, PTS, PTS), F32), ((2 * HALO, 8, 32), F32), rows(RIM), rows(RIM), ((QUADS, 64, 2 * PTS), BF16)],
         [VM] * 7,
         "halo",
     )(one, two, e, left_in, rim_in, diff_in, near_in)
@@ -744,7 +773,7 @@
         second_inner, [((14, 4, 32, LANES), F32), *matrix(14)], [VM] * 5, "inner2"
     )(q, e, south1, north1, m)
     outer, joint, out_twice, out_lo, _, quads = call(
-        second_outer, [((8, 4, 32, LANES), F32), ((2, 32, LANES), F32), *matrix(8), ((QUADS, 64, 2 * PTS), BF16)], [VM] * 15, "outer2"
+        second_outer, [((8, 4, 32, LANES), F32), ((2, 32, LANES), F32), *matrix(8), ((QUADS, 64, 2 * PTS), BF16)], [VM] * 15, "outer2", scratch=[pltpu.VMEM((176, LANES), F32)] * 2
     )(q, west, east, rest_one, rest_two, spread_rim, spread, e, halo_e, south1, north1, m, mh, inner, in_e)
     to_south, to_north = call(third_edges, [rows(56)] * 2, [VM] * 6, "edges3")(
         inner, outer, joint, quads, south2, north2

time: 54.8 us -> 53 us (0.967)
  starting transfers between devices: 22.6 us -> 21.3 us
    ppermute x8, starting transfers between devices: 7.51 us -> 6.14 us  [moved(): return lax.ppermute(array, AXES, pairs)]
where the time goes in v2:
time: 53 us; the launch traced here: 52.9 us
  starting transfers between devices  21.3 us (40%)
  Pallas kernels  20.2 us (38%)
  waiting for transfers between devices  11.1 us (21%)
    ppermute x4, starting transfers between devices, swapped(): return lax.ppermute(array, AXES, pairs)  15.2 us
    ppermute x8, waiting for transfers between devices, moved(): return lax.ppermute(array, AXES, pairs)  10.2 us
    ppermute x8, starting transfers between devices, moved(): return lax.ppermute(array, AXES, pairs)  6.14 us
    pallas_call x1, Pallas kernels, per_device(): call(own_kernel, own, [HBM, ANY] + [VM] * 6, 'own', scratch=[pltpu.VMEM((...  3.31 us
    pallas_call x1, Pallas kernels, per_device(): call(fourth_full, [((1, EX, 4, 8, 4, FL), F32), ((EX, 4, 4, FL), F32), ((...  3.21 us
    pallas_call x1, Pallas kernels, per_device(): call(first_kernel, [rows(RIM), rows(32 * GROUPS), (four, F32), ((3, PTS,...  2.81 us
    pallas_call x1, Pallas kernels, per_device(): call(second_outer, [((8, 4, 32, LANES), F32), ((2, 32, LANES), F32), *mat...  1.78 us
    pallas_call x1, Pallas kernels, per_device(): call(third_full, [wide, ((EX, PTS, FL), F32)], [VM] * 10, 'full3')  1.74 us
  transfers between devices with their start and end apart: 12, of which 5 were waited for; matrix products, arithmetic and copies ran while one was open for 0% of the time, Pallas kernels for 29%

profile of v2, /device:TPU:1, one launch (start us, length us, event | category | flops | bytes accessed | tf_op | source)
XLA Modules:
  0.0 52.9 jit_solution(9023871755496575573)
XLA Ops:
  0.0 2.8 %first.1 = (f32[80,384]{1,0:T(8,128)S(1)}, f32[320,384]{1,0:T(8,128)S(1)}, f32[4,4,8,4,360]{4,3,2,1,0:T(4,128)S(1)}, f32[3,128,16]{2,1,0:T(8,128)S(1)}, f32[128,...) custom-call(f32[1,16,4,8,4,360]{5,4,3,2,1,0:T(4,128)} %u_ref.1, ...), custom_call_target="tpu_custom_call" | custom-call | tf_op jit(solution)/shard_map/first/pallas_call | solution.py:728
  2.8 11.8 %collective-permute-start = (f32[80,384]{1,0:T(8,128)S(1)}, f32[80,384]{1,0:T(8,128)S(1)}, u32[]{:S(2)}, u32[]{:S(2)}) collective-permute-start(f32[80,384]{1,0:T(8,128)S(1)} %get-tuple-element.56), channel_id=1, source_target_pairs={{0,248},{1,249},{2,250},{3,251},{4,252},{5,253},{6,254},{7,255},{8... | collective-permute-start | bytes 368648 | tf_op jit(solution)/shard_map/ppermute | solution.py:712
  14.6 1.3 %other.1 = (f32[80,384]{1,0:T(8,128)S(1)}, f32[320,384]{1,0:T(8,128)S(1)}, f32[16,4,32,384]{3,2,1,0:T(8,128)S(1)}, f32[16,128,128]{2,1,0:T(8,128)S(1)}) custom-call(f32[4,4,8,4,360]{4,3,2,1,0:T(4,128)S(1)} %get-tuple-element.57.u_ref, f32[3,128,16]{2,1,0:T(8,128)S(1)} %get-tuple-element.58.f_ref, ...), custom_call_target="tpu_custom_call", output_to_operand_aliasing={{2}: (5, {}), {3}: (6, {})} | custom-call | tf_op jit(solution)/shard_map/other/pallas_call | solution.py:736
  15.9 0.1 collective-permute-start.1
  16.0 0.2 rest.1
  16.2 3.3 %collective-permute-start.4 = (f32[488,128]{1,0:T(8,128)S(1)}, f32[488,128]{1,0:T(8,128)S(1)}, u32[]{:S(2)}, u32[]{:S(2)}) collective-permute-start(f32[488,128]{1,0:T(8,128)S(1)} %get-tuple-element.83), channel_id=1, source_target_pairs={{0,248},{1,249},{2,250},{3,251},{4,252},{5,253},{6,254},{7,255},{8... | collective-permute-start | bytes 749576 | tf_op jit(solution)/shard_map/ppermute | solution.py:712
  19.5 0.8 %rows.1 = (f32[16,8,32]{2,1,0:T(8,128)S(1)}, f32[56,384]{1,0:T(8,128)S(1)}, f32[56,384]{1,0:T(8,128)S(1)}) custom-call(f32[16,4,4,360]{3,2,1,0:T(4,128)S(1)} %get-tuple-element.65.low_ref, f32[16,4,4,360]{3,2,1,0:T(4,128)S(1)} %get-tuple-element.66.high_ref, bf16[2,16,64]{2,1,0:T(8,128)(2,1)S(1)} %get-tuple-element.67.rim_ref, ...), custom_call_target="tpu_custom_call" | custom-call | tf_op jit(solution)/shard_map/rows/pallas_call | solution.py:745
  20.3 0.0 collective-permute-done.one_ref
  20.3 0.9 %collective-permute-done.1.two_ref = f32[80,384]{1,0:T(8,128)S(1)} collective-permute-done((f32[80,384]{1,0:T(8,128)S(1)}, f32[80,384]{1,0:T(8,128)S(1)}, u32[]{:S(2)}, u32[]{:S(2)}) %collective-permute-start.1) | collective-permute-done | bytes 122912 | tf_op jit(solution)/shard_map/ppermute | solution.py:712
  21.2 3.8 %collective-permute-start.2 = (f32[72,384]{1,0:T(8,128)S(1)}, f32[72,384]{1,0:T(8,128)S(1)}, u32[]{:S(2)}, u32[]{:S(2)}) collective-permute-start(f32[72,384]{1,0:T(8,128)S(1)} %get-tuple-element.76.sent_north_ref), channel_id=1, source_target_pairs={{0,1},{1,2},{2,3},{3,4},{4,5},{5,6},{6,7},{7,0},{8,9},{9,10},{10,1... | collective-permute-start | bytes 331784 | tf_op jit(solution)/shard_map/ppermute | solution.py:704
  25.1 3.3 %own.1 = (f32[16,4,32,384]{3,2,1,0:T(8,128)S(1)}, f32[16,128,128]{2,1,0:T(8,128)S(1)}) custom-call(f32[1,16,4,8,4,360]{5,4,3,2,1,0:T(4,128)} %u_ref.1, f32[72,384]{1,0:T(8,128)S(1)} %get-tuple-element.71.after_ref.sent_south_ref, f32[3,128,16]{2,1,0:T(8,128)S(1)} %get-tuple-element.58.f_ref, ...), custom_call_target="tpu_custom_call", output_to_operand_aliasing={{0}: (6, {}), {1}: (7, {})} | custom-call | tf_op jit(solution)/shard_map/own/pallas_call | solution.py:753
  28.4 1.1 %halo.1 = (f32[6,128,128]{2,1,0:T(8,128)S(1)}, f32[6,8,32]{2,1,0:T(8,128)S(1)}, f32[80,384]{1,0:T(8,128)S(1)}, f32[80,384]{1,0:T(8,128)S(1)}, bf16[6,64,256]{2,1,0:T(8,128)(2,1)S(1)}) custom-call(f32[80,384]{1,0:T(8,128)S(1)} %collective-permute-done.one_ref, f32[80,384]{1,0:T(8,128)S(1)} %collective-permute-done.1.two_ref, ...), custom_call_target="tpu_custom_call" | custom-call | tf_op jit(solution)/shard_map/halo/pallas_call | solution.py:761
  29.5 3.6 %collective-permute-done.3.from_north_ref = f32[72,384]{1,0:T(8,128)S(1)} collective-permute-done((f32[72,384]{1,0:T(8,128)S(1)}, f32[72,384]{1,0:T(8,128)S(1)}, u32[]{:S(2)}, u32[]{:S(2)}) %collective-permute-start.3) | collective-permute-done | bytes 110624 | tf_op jit(solution)/shard_map/ppermute | solution.py:704
  33.2 0.6 %edges2.1 = (f32[64,384]{1,0:T(8,128)S(1)}, f32[64,384]{1,0:T(8,128)S(1)}) custom-call(f32[16,4,32,384]{3,2,1,0:T(8,128)S(1)} %get-tuple-element.74.q_ref, f32[80,384]{1,0:T(8,128)S(1)} %get-tuple-element.79.west_ref, f32[80,384]{1,0:T(8,128)S(1)} %get-tuple-element.80.east_ref, bf16[6,64,256]{2,1,0:T(8,128)(2,1)S(1)} %get-tuple-element.90.quads_ref, ...), custom_call_target="tpu_custom_call" | custom-call | tf_op jit(solution)/shard_map/edges2/pallas_call | solution.py:767
  33.7 0.0 copy-start.1
  33.8 0.0 copy-start.2
  33.8 0.1 collective-permute-start.6
  33.9 0.5 collective-permute-start.7
  34.4 1.4 %inner2.1 = (f32[14,4,32,384]{3,2,1,0:T(8,128)S(1)}, bf16[14,128,256]{2,1,0:T(8,128)(2,1)S(1)}, bf16[14,128,128]{2,1,0:T(8,128)(2,1)S(1)}, f32[14,8,32]{2,1,0:T(8,128)S(1)}) custom-call(f32[16,4,32,384]{3,2,1,0:T(8,128)S(1)} %get-tuple-element.74.q_ref, f32[16,8,32]{2,1,0:T(8,128)S(1)} %get-tuple-element.75.e_ref.own_e_ref, ...), custom_call_target="tpu_custom_call" | custom-call | tf_op jit(solution)/shard_map/inner2/pallas_call | solution.py:772
  35.9 1.8 %outer2.1 = (f32[8,4,32,384]{3,2,1,0:T(8,128)S(1)}, f32[2,32,384]{2,1,0:T(8,128)S(1)}, bf16[8,128,256]{2,1,0:T(8,128)(2,1)S(1)}, bf16[8,128,128]{2,1,0:T(8,128)(...) custom-call(f32[16,4,32,384]{3,2,1,0:T(8,128)S(1)} %get-tuple-element.74.q_ref, ...), custom_call_target="tpu_custom_call" | custom-call | tf_op jit(solution)/shard_map/outer2/pallas_call | solution.py:775
  37.7 1.6 %collective-permute-done.7.from_north_ref = f32[64,384]{1,0:T(8,128)S(1)} collective-permute-done((f32[64,384]{1,0:T(8,128)S(1)}, f32[64,384]{1,0:T(8,128)S(1)}, u32[]{:S(2)}, u32[]{:S(2)}) %collective-permute-start.7) | collective-permute-done | bytes 98336 | tf_op jit(solution)/shard_map/ppermute | solution.py:704
  39.3 0.5 edges3.1
  39.7 0.1 collective-permute-start.8
  39.8 0.8 %collective-permute-start.9 = (f32[56,384]{1,0:T(8,128)S(1)}, f32[56,384]{1,0:T(8,128)S(1)}, u32[]{:S(2)}, u32[]{:S(2)}) collective-permute-start(f32[56,384]{1,0:T(8,128)S(1)} %get-tuple-element.100), channel_id=1, source_target_pairs={{0,7},{1,0},{2,1},{3,2},{4,3},{5,4},{6,5},{7,6},{8,15},{9,8},{10,9... | collective-permute-start | bytes 258056 | tf_op jit(solution)/shard_map/ppermute | solution.py:704
  40.7 1.7 %full3.1 = (f32[22,4,32,384]{3,2,1,0:T(8,128)S(1)}, f32[16,128,360]{2,1,0:T(8,128)S(1)}) custom-call(f32[14,4,32,384]{3,2,1,0:T(8,128)S(1)} %get-tuple-element.78.inner_ref, f32[8,4,32,384]{3,2,1,0:T(8,128)S(1)} %get-tuple-element.88.outer_ref, f32[2,32,384]{2,1,0:T(8,128)S(1)} %get-tuple-element.89.joint_ref, ...), custom_call_target="tpu_custom_call" | custom-call | tf_op jit(solution)/shard_map/full3/pallas_call | solution.py:782
  42.4 2.9 %collective-permute-done.9.from_north_ref = f32[56,384]{1,0:T(8,128)S(1)} collective-permute-done((f32[56,384]{1,0:T(8,128)S(1)}, f32[56,384]{1,0:T(8,128)S(1)}, u32[]{:S(2)}, u32[]{:S(2)}) %collective-permute-start.9) | collective-permute-done | bytes 86048 | tf_op jit(solution)/shard_map/ppermute | solution.py:704
  45.4 0.4 edges4.1
  45.8 0.1 collective-permute-start.10
  45.9 0.7 %collective-permute-start.11 = (f32[56,384]{1,0:T(8,128)S(1)}, f32[56,384]{1,0:T(8,128)S(1)}, u32[]{:S(2)}, u32[]{:S(2)}) collective-permute-start(f32[56,384]{1,0:T(8,128)S(1)} %get-tuple-element.106), channel_id=1, source_target_pairs={{0,7},{1,0},{2,1},{3,2},{4,3},{5,4},{6,5},{7,6},{8,15},{9,8},{10,9... | collective-permute-start | bytes 258056 | tf_op jit(solution)/shard_map/ppermute | solution.py:704
  46.6 3.2 %full4.1 = (f32[1,16,4,8,4,360]{5,4,3,2,1,0:T(4,128)}, f32[16,4,4,360]{3,2,1,0:T(4,128)S(1)}, f32[16,4,4,360]{3,2,1,0:T(4,128)S(1)}) custom-call(f32[22,4,32,384]{3,2,1,0:T(8,128)S(1)} %get-tuple-element.97.f_ref, f32[56,384]{1,0:T(8,128)S(1)} %collective-permute-done.8.from_south_ref, f32[56,384]{1,0:T(8,128)S(1)} %collective-permute-done.9.from_north_ref, ...), custom_call_target="tpu_custom_call" | custom-call | tf_op jit(solution)/shard_map/full4/pallas_call | solution.py:789
  49.8 2.0 %collective-permute-done.11.from_north_ref = f32[56,384]{1,0:T(8,128)S(1)} collective-permute-done((f32[56,384]{1,0:T(8,128)S(1)}, f32[56,384]{1,0:T(8,128)S(1)}, u32[]{:S(2)}, u32[]{:S(2)}) %collective-permute-start.11) | collective-permute-done | bytes 86048 | tf_op jit(solution)/shard_map/ppermute | solution.py:704
  51.8 1.0 %patch.1 = f32[1,16,4,8,4,360]{5,4,3,2,1,0:T(4,128)} custom-call(f32[1,16,4,8,4,360]{5,4,3,2,1,0:T(4,128)} %get-tuple-element.102.old_ref, f32[16,4,4,360]{3,2,1,0:T(4,128)S(1)} %get-tuple-element.103.rim_south_ref, f32[16,4,4,360]{3,2,1,0:T(4,128)S(1)} %get-tuple-element.104.rim_north_ref, ...), custom_call_target="tpu_custom_call", output_to_operand_aliasing={{}: (0, {})} | custom-call | tf_op jit(solution)/shard_map/patch/pallas_call | solution.py:796
  (13 shorter events, 0.1 us)
Async XLA Ops:
  2.8 17.5 %collective-permute-start = (f32[80,384]{1,0:T(8,128)S(1)}, f32[80,384]{1,0:T(8,128)S(1)}, u32[]{:S(2)}, u32[]{:S(2)}) collective-permute-start(f32[80,384]{1,0:T(8,128)S(1)} %get-tuple-element.56), channel_id=1, source_target_pairs={{0,248},{1,249},{2,250},{3,251},{4,252},{5,253},{6,254},{7,255},{8... | collective-permute-start | bytes 368648 | tf_op jit(solution)/shard_map/ppermute | solution.py:712
  15.9 5.3 %collective-permute-start.1 = (f32[80,384]{1,0:T(8,128)S(1)}, f32[80,384]{1,0:T(8,128)S(1)}, u32[]{:S(2)}, u32[]{:S(2)}) collective-permute-start(f32[80,384]{1,0:T(8,128)S(1)} %get-tuple-element.64), channel_id=1, source_target_pairs={{0,8},{1,9},{2,10},{3,11},{4,12},{5,13},{6,14},{7,15},{8,0},{9,1},... | collective-permute-start | bytes 368648 | tf_op jit(solution)/shard_map/ppermute | solution.py:712
  16.2 19.7 %collective-permute-start.4 = (f32[488,128]{1,0:T(8,128)S(1)}, f32[488,128]{1,0:T(8,128)S(1)}, u32[]{:S(2)}, u32[]{:S(2)}) collective-permute-start(f32[488,128]{1,0:T(8,128)S(1)} %get-tuple-element.83), channel_id=1, source_target_pairs={{0,248},{1,249},{2,250},{3,251},{4,252},{5,253},{6,254},{7,255},{8... | collective-permute-start | bytes 749576 | tf_op jit(solution)/shard_map/ppermute | solution.py:712
  19.5 16.4 %collective-permute-start.5 = (f32[488,128]{1,0:T(8,128)S(1)}, f32[488,128]{1,0:T(8,128)S(1)}, u32[]{:S(2)}, u32[]{:S(2)}) collective-permute-start(f32[488,128]{1,0:T(8,128)S(1)} %get-tuple-element.84), channel_id=1, source_target_pairs={{0,8},{1,9},{2,10},{3,11},{4,12},{5,13},{6,14},{7,15},{8,0},{9,1},... | collective-permute-start | bytes 749576 | tf_op jit(solution)/shard_map/ppermute | solution.py:712
  21.2 8.3 %collective-permute-start.2 = (f32[72,384]{1,0:T(8,128)S(1)}, f32[72,384]{1,0:T(8,128)S(1)}, u32[]{:S(2)}, u32[]{:S(2)}) collective-permute-start(f32[72,384]{1,0:T(8,128)S(1)} %get-tuple-element.76.sent_north_ref), channel_id=1, source_target_pairs={{0,1},{1,2},{2,3},{3,4},{4,5},{5,6},{6,7},{7,0},{8,9},{9,10},{10,1... | collective-permute-start | bytes 331784 | tf_op jit(solution)/shard_map/ppermute | solution.py:704
  25.1 8.1 %collective-permute-start.3 = (f32[72,384]{1,0:T(8,128)S(1)}, f32[72,384]{1,0:T(8,128)S(1)}, u32[]{:S(2)}, u32[]{:S(2)}) collective-permute-start(f32[72,384]{1,0:T(8,128)S(1)} %get-tuple-element.71.after_ref.sent_south_ref), channel_id=1, source_target_pairs={{0,7},{1,0},{2,1},{3,2},{4,3},{5,4},{6,5},{7,6},{8,15},{9,8},{10,9... | collective-permute-start | bytes 331784 | tf_op jit(solution)/shard_map/ppermute | solution.py:704
  33.7 2.1 %copy-start.1 = (bf16[320,176]{1,0:T(8,128)(2,1)S(1)}, bf16[320,176]{1,0:T(8,128)(2,1)}, u32[]{:S(2)}) copy-start(bf16[320,176]{1,0:T(8,128)(2,1)} %constant.17.clone.spread_ref) | copy-start | bytes 337924
  33.8 2.1 %copy-start.2 = (bf16[320,80]{1,0:T(8,128)(2,1)S(1)}, bf16[320,80]{1,0:T(8,128)(2,1)}, u32[]{:S(2)}) copy-start(bf16[320,80]{1,0:T(8,128)(2,1)} %constant.16.clone.spread_rim_ref) | copy-start | bytes 153604
  33.8 3.9 %collective-permute-start.6 = (f32[64,384]{1,0:T(8,128)S(1)}, f32[64,384]{1,0:T(8,128)S(1)}, u32[]{:S(2)}, u32[]{:S(2)}) collective-permute-start(f32[64,384]{1,0:T(8,128)S(1)} %get-tuple-element.91), channel_id=1, source_target_pairs={{0,1},{1,2},{2,3},{3,4},{4,5},{5,6},{6,7},{7,0},{8,9},{9,10},{10,1... | collective-permute-start | bytes 294920 | tf_op jit(solution)/shard_map/ppermute | solution.py:704
  33.9 5.4 %collective-permute-start.7 = (f32[64,384]{1,0:T(8,128)S(1)}, f32[64,384]{1,0:T(8,128)S(1)}, u32[]{:S(2)}, u32[]{:S(2)}) collective-permute-start(f32[64,384]{1,0:T(8,128)S(1)} %get-tuple-element.92), channel_id=1, source_target_pairs={{0,7},{1,0},{2,1},{3,2},{4,3},{5,4},{6,5},{7,6},{8,15},{9,8},{10,9... | collective-permute-start | bytes 294920 | tf_op jit(solution)/shard_map/ppermute | solution.py:704
  37.6 3.0 %copy-start = (f32[1,16,4,8,4,360]{5,4,3,2,1,0:T(4,128)S(1)}, f32[1,16,4,8,4,360]{5,4,3,2,1,0:T(4,128)}, u32[]{:S(2)}) copy-start(f32[1,16,4,8,4,360]{5,4,3,2,1,0:T(4,128)} %u_ref.1) | copy-start | bytes 8847364
  39.7 2.7 %collective-permute-start.8 = (f32[56,384]{1,0:T(8,128)S(1)}, f32[56,384]{1,0:T(8,128)S(1)}, u32[]{:S(2)}, u32[]{:S(2)}) collective-permute-start(f32[56,384]{1,0:T(8,128)S(1)} %get-tuple-element.99), channel_id=1, source_target_pairs={{0,1},{1,2},{2,3},{3,4},{4,5},{5,6},{6,7},{7,0},{8,9},{9,10},{10,1... | collective-permute-start | bytes 258056 | tf_op jit(solution)/shard_map/ppermute | solution.py:704
  39.8 5.5 %collective-permute-start.9 = (f32[56,384]{1,0:T(8,128)S(1)}, f32[56,384]{1,0:T(8,128)S(1)}, u32[]{:S(2)}, u32[]{:S(2)}) collective-permute-start(f32[56,384]{1,0:T(8,128)S(1)} %get-tuple-element.100), channel_id=1, source_target_pairs={{0,7},{1,0},{2,1},{3,2},{4,3},{5,4},{6,5},{7,6},{8,15},{9,8},{10,9... | collective-permute-start | bytes 258056 | tf_op jit(solution)/shard_map/ppermute | solution.py:704
  45.8 4.0 %collective-permute-start.10 = (f32[56,384]{1,0:T(8,128)S(1)}, f32[56,384]{1,0:T(8,128)S(1)}, u32[]{:S(2)}, u32[]{:S(2)}) collective-permute-start(f32[56,384]{1,0:T(8,128)S(1)} %get-tuple-element.105), channel_id=1, source_target_pairs={{0,1},{1,2},{2,3},{3,4},{4,5},{5,6},{6,7},{7,0},{8,9},{9,10},{10,1... | collective-permute-start | bytes 258056 | tf_op jit(solution)/shard_map/ppermute | solution.py:704
  45.9 5.9 %collective-permute-start.11 = (f32[56,384]{1,0:T(8,128)S(1)}, f32[56,384]{1,0:T(8,128)S(1)}, u32[]{:S(2)}, u32[]{:S(2)}) collective-permute-start(f32[56,384]{1,0:T(8,128)S(1)} %get-tuple-element.106), channel_id=1, source_target_pairs={{0,7},{1,0},{2,1},{3,2},{4,3},{5,4},{6,5},{7,6},{8,15},{9,8},{10,9... | collective-permute-start | bytes 258056 | tf_op jit(solution)/shard_map/ppermute | solution.py:704

commit v3 on v2

--- a/solution.py
+++ b/solution.py
@@ -158,37 +158,45 @@
 
 
 def side_columns(want_west, u_ref, f, mass, left_ref, diff_ref, rim_out_ref, layers_ref, q_ref, m_ref):
+    flux = jnp.concatenate([fluxes(diff_ref, *column(f, k)) for k in range(HALO)], axis=1)
+    together = product(left_ref[0], left_ref[1], flux)
     raw, part = {}, {}
-    flux = jnp.concatenate([fluxes(diff_ref, *column(f, k)) for k in range(HALO + 1)], axis=1)
-    together = product(left_ref[0], left_ref[1], flux)
-    for k in range(HALO + 1):
+    for k in range(HALO):
         m = together[:, PTS * k : PTS * k + PTS]
-        m_ref[jnp.where(want_west, k, EX - HALO - 1 + k)] = m
+        m_ref[jnp.where(want_west, k, EX - HALO + k)] = m
         m_hi, m_lo = halves(m)
         q = product(m_hi, m_lo, u_ref[k].reshape(PTS, FL))
         for i in range(4):
             raw[k, i] = q[32 * i : 32 * i + 32]
             part[k, i] = mass[32 * i : 32 * i + 32, k : k + 1]
     for values in (raw, part):
-        for k in range(HALO):
+        for k in range(HALO - 1):
             values[k, 3] = values[k + 1, 0] = values[k, 3] + values[k + 1, 0]
-    for k in range(HALO + 1):
-        c = jnp.where(want_west, k, EX - HALO - 1 + k)
+    for k in range(HALO):
+        c = jnp.where(want_west, k, EX - HALO + k)
         for i in range(4):
             q_ref[c, i, :, 0:FL] = raw[k, i]
             q_ref[c, i, :, FL:LANES] = jnp.broadcast_to(part[k, i], (32, TAIL))
+    near = [either(want_west, left_ref[p, 0:32, :], left_ref[p, 96:128, :]) for p in range(2)]
+    m_hi, m_lo = halves(product(near[0], near[1], fluxes(diff_ref, *column(f, HALO))))
+    extra = product(m_hi, m_lo, u_ref[HALO].reshape(PTS, FL))
+    extra_part = either(want_west, mass[0:32, HALO : HALO + 1], mass[96:128, HALO : HALO + 1])
     sub = lax.broadcasted_iota(jnp.int32, (8, LANES), 0)
     for g in range(GROUPS):
         k, i = (g // 3, g % 3) if g < GROUPS - 1 else (HALO - 1, 3)
-        row = either(want_west, raw[k, i], raw[k + 1, i])
-        tail = jnp.broadcast_to(either(want_west, part[k, i], part[k + 1, i]), (32, TAIL))
+        row, more = raw[k, i], part[k, i]
+        if g in (0, GROUPS - 1):
+            joined = want_west if g else jnp.logical_not(want_west)
+            row = row + either(joined, extra, 0.0)
+            more = more + either(joined, extra_part, 0.0)
+        tail = jnp.broadcast_to(more, (32, TAIL))
         for lanes, value in ((slice(0, FL), row), (slice(FL, LANES), tail)):
             rim_out_ref[8 * g : 8 * g + 8, lanes] = jnp.where(sub[:, lanes] < 4, value[0:8], value[24:32])
             layers_ref[32 * g : 32 * g + 32, lanes] = value
     at = FL + 1
     for t in range(3):
         for k in range(HALO):
-            value = either(want_west, f[t][:, k : k + 1], f[t][:, k + 1 : k + 2])
+            value = f[t][:, k : k + 1]
             rim_out_ref[:, at : at + 1] = value[0:RIM]
             rim_out_ref[0 : PTS - RIM, at + 9 : at + 10] = value[RIM:PTS]
             at += 1
@@ -230,17 +238,19 @@
 
 
 def nearest(want_west, t):
-    return either(want_west, t[:, 0 : HALO + 1], t[:, EX - HALO - 1 : EX])
+    at = EX - HALO
+    return jnp.concatenate([either(want_west, t[:, 0:HALO], t[:, at:EX]), either(want_west, t[:, HALO : HALO + 1], t[:, at - 1 : at])], axis=1)
 
 
 def first_kernel(u_hbm, jac_hbm, xx_hbm, yy_hbm, xy_hbm, left_hbm, diff_hbm, rim_hbm, near_hbm, rim_out_ref, layers_ref, other_ref, f_ref, mass_ref, left_ref, diff_ref, rim_ref, near_ref, low_ref, high_ref, q_ref, m_ref, u_ref, jac_ref, xx_ref, yy_ref, xy_ref, sems):
     want_west = even_column()
-    size = HALO + 1
-    here = jnp.where(want_west, 0, EX - size)
-    there = jnp.where(want_west, EX - size, 0)
+    here = jnp.where(want_west, 0, EX - HALO)
+    there = EX - HALO - here
+    here_next = jnp.where(want_west, HALO, EX - HALO - 1)
+    there_next = EX - 1 - here_next
     copies = fetch(
-        (jac_hbm, xx_hbm, yy_hbm, xy_hbm, left_hbm, diff_hbm, u_hbm.at[0, pl.ds(here, size)], u_hbm.at[0, pl.ds(there, size)], rim_hbm, near_hbm, u_hbm.at[0, :, :, 0], u_hbm.at[0, :, :, 7]),
-        (jac_ref, xx_ref, yy_ref, xy_ref, left_ref, diff_ref, u_ref, other_ref, rim_ref, near_ref, low_ref, high_ref),
+        (jac_hbm, xx_hbm, yy_hbm, xy_hbm, left_hbm, diff_hbm, u_hbm.at[0, pl.ds(here, HALO)], u_hbm.at[0, pl.ds(here_next, 1)], u_hbm.at[0, pl.ds(there, HALO)], u_hbm.at[0, pl.ds(there_next, 1)], rim_hbm, near_hbm, u_hbm.at[0, :, :, 0], u_hbm.at[0, :, :, 7]),
+        (jac_ref, xx_ref, yy_ref, xy_ref, left_ref, diff_ref, u_ref.at[0:HALO], u_ref.at[HALO:], other_ref.at[0:HALO], other_ref.at[HALO:], rim_ref, near_ref, low_ref, high_ref),
         sems,
     )
     for copy in copies[:6]:
@@ -250,8 +260,9 @@
         f_ref[t] = f[t]
     mass_ref[...] = mass
     copies[6].wait()
+    copies[7].wait()
     side_columns(want_west, u_ref, [nearest(want_west, t) for t in f], nearest(want_west, mass), left_ref, diff_ref, rim_out_ref, layers_ref, q_ref, m_ref)
-    for copy in copies[7:]:
+    for copy in copies[8:]:
         copy.wait()
 
 
@@ -330,9 +341,9 @@
 
 def own_kernel(u_hbm, after_ref, f_ref, mass_ref, left_ref, diff_ref, q_in, m_in, q_ref, m_ref, u_ref, sems):
     del after_ref, q_in, m_in
-    first, final = HALO + 1, EX - HALO - 2
+    first, final = HALO, EX - HALO - 1
     copies = fetch(
-        [u_hbm.at[0, c : c + 4] for c in range(first, final, 4)], [u_ref.at[c : c + 4] for c in range(0, 8, 4)], sems
+        [u_hbm.at[0, c : c + 5] for c in range(first, final, 5)], [u_ref.at[c : c + 5] for c in range(0, 10, 5)], sems
     )
     f = [f_ref[t] for t in range(3)]
     mass = mass_ref[...]
@@ -340,8 +351,8 @@
         m = form(left_ref, diff_ref, column(f, c))
         m_ref[c] = m
         m_hi, m_lo = halves(m)
-        if (c - first) % 4 == 0:
-            copies[(c - first) // 4].wait()
+        if (c - first) % 5 == 0:
+            copies[(c - first) // 5].wait()
         q = product(m_hi, m_lo, u_ref[c - first].reshape(PTS, FL))
         for i in range(4):
             q_ref[c, i, :, 0:FL] = q[32 * i : 32 * i + 32]
@@ -730,7 +741,7 @@
         [rows(RIM), rows(32 * GROUPS), (four, F32), ((3, PTS, EX), F32), ((PTS, EX), F32), (left.shape, BF16), (diff.shape, F32), (rim.shape, BF16), (near.shape, F32), *[((EX, 4, 4, FL), F32)] * 2, *own],
         [HBM] * 9,
         "first",
-        scratch=[pltpu.VMEM(four, F32), *[pltpu.VMEM((PTS, EX), F32)] * 4, pltpu.SemaphoreType.DMA((12,))],
+        scratch=[pltpu.VMEM(four, F32), *[pltpu.VMEM((PTS, EX), F32)] * 4, pltpu.SemaphoreType.DMA((14,))],
     )(*pinned(state, *flat, left, diff, rim, near))
     one = swapped(rim_one, 1)
     rim_two, layers_two, q, m = call(
@@ -755,7 +766,7 @@
         own,
         [HBM, ANY] + [VM] * 6,
         "own",
-        scratch=[pltpu.VMEM((8, 4, 8, 4, FL), F32), pltpu.SemaphoreType.DMA((2,))],
+        scratch=[pltpu.VMEM((10, 4, 8, 4, FL), F32), pltpu.SemaphoreType.DMA((2,))],
         aliases={6: 0, 7: 1},
     )(*pinned(state), to_south, f, mass, left_in, diff_in, q, m)
     mh, halo_e, west, east, quads = call(

time: 53 us -> 52.8 us (level)
  waiting for transfers between devices: 11.1 us -> 10.4 us
    ppermute x8, waiting for transfers between devices: 10.2 us -> 9.47 us  [moved(): return lax.ppermute(array, AXES, pairs)]
    pallas_call x1, Pallas kernels: 3.31 us -> 3.92 us  [per_device(): call(own_kernel, own, [HBM, ANY] + [VM] * 6, 'own', scratch=[pltpu.VMEM((...]
  transfers between devices with their start and end apart: 12 -> 12, of which waited for: 5 -> 5; matrix products, arithmetic and copies ran while one was open for 0% -> 0% of each run, Pallas kernels for 29% -> 30%
where the time goes in v3:
time: 52.8 us; the launch traced here: 52.7 us
  starting transfers between devices  21.4 us (41%)
  Pallas kernels  20.5 us (39%)
  waiting for transfers between devices  10.4 us (20%)
    ppermute x4, starting transfers between devices, swapped(): return lax.ppermute(array, AXES, pairs)  15.2 us
    ppermute x8, waiting for transfers between devices, moved(): return lax.ppermute(array, AXES, pairs)  9.47 us
    ppermute x8, starting transfers between devices, moved(): return lax.ppermute(array, AXES, pairs)  6.27 us
    pallas_call x1, Pallas kernels, per_device(): call(own_kernel, own, [HBM, ANY] + [VM] * 6, 'own', scratch=[pltpu.VMEM((...  3.92 us
    pallas_call x1, Pallas kernels, per_device(): call(fourth_full, [((1, EX, 4, 8, 4, FL), F32), ((EX, 4, 4, FL), F32), ((...  3.2 us
    pallas_call x1, Pallas kernels, per_device(): call(first_kernel, [rows(RIM), rows(32 * GROUPS), (four, F32), ((3, PTS,...  2.62 us
    pallas_call x1, Pallas kernels, per_device(): call(second_outer, [((8, 4, 32, LANES), F32), ((2, 32, LANES), F32), *mat...  1.78 us
    pallas_call x1, Pallas kernels, per_device(): call(third_full, [wide, ((EX, PTS, FL), F32)], [VM] * 10, 'full3')  1.74 us
  transfers between devices with their start and end apart: 12, of which 5 were waited for; matrix products, arithmetic and copies ran while one was open for 0% of the time, Pallas kernels for 30%

profile of v3, /device:TPU:1, one launch (start us, length us, event | category | flops | bytes accessed | tf_op | source)
XLA Modules:
  0.0 52.7 jit_solution(14451054112941511652)
XLA Ops:
  0.0 2.6 %first.1 = (f32[80,384]{1,0:T(8,128)S(1)}, f32[320,384]{1,0:T(8,128)S(1)}, f32[4,4,8,4,360]{4,3,2,1,0:T(4,128)S(1)}, f32[3,128,16]{2,1,0:T(8,128)S(1)}, f32[128,...) custom-call(f32[1,16,4,8,4,360]{5,4,3,2,1,0:T(4,128)} %u_ref.1, ...), custom_call_target="tpu_custom_call" | custom-call | tf_op jit(solution)/shard_map/first/pallas_call | solution.py:739
  2.6 11.8 %collective-permute-start = (f32[80,384]{1,0:T(8,128)S(1)}, f32[80,384]{1,0:T(8,128)S(1)}, u32[]{:S(2)}, u32[]{:S(2)}) collective-permute-start(f32[80,384]{1,0:T(8,128)S(1)} %get-tuple-element.56), channel_id=1, source_target_pairs={{0,248},{1,249},{2,250},{3,251},{4,252},{5,253},{6,254},{7,255},{8... | collective-permute-start | bytes 368648 | tf_op jit(solution)/shard_map/ppermute | solution.py:723
  14.4 1.2 %other.1 = (f32[80,384]{1,0:T(8,128)S(1)}, f32[320,384]{1,0:T(8,128)S(1)}, f32[16,4,32,384]{3,2,1,0:T(8,128)S(1)}, f32[16,128,128]{2,1,0:T(8,128)S(1)}) custom-call(f32[4,4,8,4,360]{4,3,2,1,0:T(4,128)S(1)} %get-tuple-element.57.u_ref, f32[3,128,16]{2,1,0:T(8,128)S(1)} %get-tuple-element.58.f_ref, ...), custom_call_target="tpu_custom_call", output_to_operand_aliasing={{2}: (5, {}), {3}: (6, {})} | custom-call | tf_op jit(solution)/shard_map/other/pallas_call | solution.py:747
  15.6 0.1 collective-permute-start.1
  15.7 0.2 rest.1
  15.9 3.3 %collective-permute-start.4 = (f32[488,128]{1,0:T(8,128)S(1)}, f32[488,128]{1,0:T(8,128)S(1)}, u32[]{:S(2)}, u32[]{:S(2)}) collective-permute-start(f32[488,128]{1,0:T(8,128)S(1)} %get-tuple-element.83), channel_id=1, source_target_pairs={{0,248},{1,249},{2,250},{3,251},{4,252},{5,253},{6,254},{7,255},{8... | collective-permute-start | bytes 749576 | tf_op jit(solution)/shard_map/ppermute | solution.py:723
  19.2 0.8 %rows.1 = (f32[16,8,32]{2,1,0:T(8,128)S(1)}, f32[56,384]{1,0:T(8,128)S(1)}, f32[56,384]{1,0:T(8,128)S(1)}) custom-call(f32[16,4,4,360]{3,2,1,0:T(4,128)S(1)} %get-tuple-element.65.low_ref, f32[16,4,4,360]{3,2,1,0:T(4,128)S(1)} %get-tuple-element.66.high_ref, bf16[2,16,64]{2,1,0:T(8,128)(2,1)S(1)} %get-tuple-element.67.rim_ref, ...), custom_call_target="tpu_custom_call" | custom-call | tf_op jit(solution)/shard_map/rows/pallas_call | solution.py:756
  20.0 0.0 collective-permute-done.one_ref
  20.0 0.9 %collective-permute-done.1.two_ref = f32[80,384]{1,0:T(8,128)S(1)} collective-permute-done((f32[80,384]{1,0:T(8,128)S(1)}, f32[80,384]{1,0:T(8,128)S(1)}, u32[]{:S(2)}, u32[]{:S(2)}) %collective-permute-start.1) | collective-permute-done | bytes 122912 | tf_op jit(solution)/shard_map/ppermute | solution.py:723
  21.0 3.9 %collective-permute-start.2 = (f32[72,384]{1,0:T(8,128)S(1)}, f32[72,384]{1,0:T(8,128)S(1)}, u32[]{:S(2)}, u32[]{:S(2)}) collective-permute-start(f32[72,384]{1,0:T(8,128)S(1)} %get-tuple-element.76.sent_north_ref), channel_id=1, source_target_pairs={{0,1},{1,2},{2,3},{3,4},{4,5},{5,6},{6,7},{7,0},{8,9},{9,10},{10,1... | collective-permute-start | bytes 331784 | tf_op jit(solution)/shard_map/ppermute | solution.py:715
  24.9 3.9 %own.1 = (f32[16,4,32,384]{3,2,1,0:T(8,128)S(1)}, f32[16,128,128]{2,1,0:T(8,128)S(1)}) custom-call(f32[1,16,4,8,4,360]{5,4,3,2,1,0:T(4,128)} %u_ref.1, f32[72,384]{1,0:T(8,128)S(1)} %get-tuple-element.71.after_ref.sent_south_ref, f32[3,128,16]{2,1,0:T(8,128)S(1)} %get-tuple-element.58.f_ref, ...), custom_call_target="tpu_custom_call", output_to_operand_aliasing={{0}: (6, {}), {1}: (7, {})} | custom-call | tf_op jit(solution)/shard_map/own/pallas_call | solution.py:764
  28.9 1.1 %halo.1 = (f32[6,128,128]{2,1,0:T(8,128)S(1)}, f32[6,8,32]{2,1,0:T(8,128)S(1)}, f32[80,384]{1,0:T(8,128)S(1)}, f32[80,384]{1,0:T(8,128)S(1)}, bf16[6,64,256]{2,1,0:T(8,128)(2,1)S(1)}) custom-call(f32[80,384]{1,0:T(8,128)S(1)} %collective-permute-done.one_ref, f32[80,384]{1,0:T(8,128)S(1)} %collective-permute-done.1.two_ref, ...), custom_call_target="tpu_custom_call" | custom-call | tf_op jit(solution)/shard_map/halo/pallas_call | solution.py:772
  30.0 3.0 %collective-permute-done.3.from_north_ref = f32[72,384]{1,0:T(8,128)S(1)} collective-permute-done((f32[72,384]{1,0:T(8,128)S(1)}, f32[72,384]{1,0:T(8,128)S(1)}, u32[]{:S(2)}, u32[]{:S(2)}) %collective-permute-start.3) | collective-permute-done | bytes 110624 | tf_op jit(solution)/shard_map/ppermute | solution.py:715
  33.0 0.6 %edges2.1 = (f32[64,384]{1,0:T(8,128)S(1)}, f32[64,384]{1,0:T(8,128)S(1)}) custom-call(f32[16,4,32,384]{3,2,1,0:T(8,128)S(1)} %get-tuple-element.74.q_ref, f32[80,384]{1,0:T(8,128)S(1)} %get-tuple-element.79.west_ref, f32[80,384]{1,0:T(8,128)S(1)} %get-tuple-element.80.east_ref, bf16[6,64,256]{2,1,0:T(8,128)(2,1)S(1)} %get-tuple-element.90.quads_ref, ...), custom_call_target="tpu_custom_call" | custom-call | tf_op jit(solution)/shard_map/edges2/pallas_call | solution.py:778
  33.6 0.0 copy-start.1
  33.6 0.0 copy-start.2
  33.6 0.1 collective-permute-start.6
  33.7 0.5 collective-permute-start.7
  34.2 1.4 %inner2.1 = (f32[14,4,32,384]{3,2,1,0:T(8,128)S(1)}, bf16[14,128,256]{2,1,0:T(8,128)(2,1)S(1)}, bf16[14,128,128]{2,1,0:T(8,128)(2,1)S(1)}, f32[14,8,32]{2,1,0:T(8,128)S(1)}) custom-call(f32[16,4,32,384]{3,2,1,0:T(8,128)S(1)} %get-tuple-element.74.q_ref, f32[16,8,32]{2,1,0:T(8,128)S(1)} %get-tuple-element.75.e_ref.own_e_ref, ...), custom_call_target="tpu_custom_call" | custom-call | tf_op jit(solution)/shard_map/inner2/pallas_call | solution.py:783
  35.7 1.8 %outer2.1 = (f32[8,4,32,384]{3,2,1,0:T(8,128)S(1)}, f32[2,32,384]{2,1,0:T(8,128)S(1)}, bf16[8,128,256]{2,1,0:T(8,128)(2,1)S(1)}, bf16[8,128,128]{2,1,0:T(8,128)(...) custom-call(f32[16,4,32,384]{3,2,1,0:T(8,128)S(1)} %get-tuple-element.74.q_ref, ...), custom_call_target="tpu_custom_call" | custom-call | tf_op jit(solution)/shard_map/outer2/pallas_call | solution.py:786
  37.5 1.6 %collective-permute-done.7.from_north_ref = f32[64,384]{1,0:T(8,128)S(1)} collective-permute-done((f32[64,384]{1,0:T(8,128)S(1)}, f32[64,384]{1,0:T(8,128)S(1)}, u32[]{:S(2)}, u32[]{:S(2)}) %collective-permute-start.7) | collective-permute-done | bytes 98336 | tf_op jit(solution)/shard_map/ppermute | solution.py:715
  39.1 0.5 edges3.1
  39.5 0.1 collective-permute-start.8
  39.6 0.8 %collective-permute-start.9 = (f32[56,384]{1,0:T(8,128)S(1)}, f32[56,384]{1,0:T(8,128)S(1)}, u32[]{:S(2)}, u32[]{:S(2)}) collective-permute-start(f32[56,384]{1,0:T(8,128)S(1)} %get-tuple-element.100), channel_id=1, source_target_pairs={{0,7},{1,0},{2,1},{3,2},{4,3},{5,4},{6,5},{7,6},{8,15},{9,8},{10,9... | collective-permute-start | bytes 258056 | tf_op jit(solution)/shard_map/ppermute | solution.py:715
  40.5 1.7 %full3.1 = (f32[22,4,32,384]{3,2,1,0:T(8,128)S(1)}, f32[16,128,360]{2,1,0:T(8,128)S(1)}) custom-call(f32[14,4,32,384]{3,2,1,0:T(8,128)S(1)} %get-tuple-element.78.inner_ref, f32[8,4,32,384]{3,2,1,0:T(8,128)S(1)} %get-tuple-element.88.outer_ref, f32[2,32,384]{2,1,0:T(8,128)S(1)} %get-tuple-element.89.joint_ref, ...), custom_call_target="tpu_custom_call" | custom-call | tf_op jit(solution)/shard_map/full3/pallas_call | solution.py:793
  42.2 2.9 %collective-permute-done.9.from_north_ref = f32[56,384]{1,0:T(8,128)S(1)} collective-permute-done((f32[56,384]{1,0:T(8,128)S(1)}, f32[56,384]{1,0:T(8,128)S(1)}, u32[]{:S(2)}, u32[]{:S(2)}) %collective-permute-start.9) | collective-permute-done | bytes 86048 | tf_op jit(solution)/shard_map/ppermute | solution.py:715
  45.2 0.4 edges4.1
  45.6 0.1 collective-permute-start.10
  45.7 0.7 %collective-permute-start.11 = (f32[56,384]{1,0:T(8,128)S(1)}, f32[56,384]{1,0:T(8,128)S(1)}, u32[]{:S(2)}, u32[]{:S(2)}) collective-permute-start(f32[56,384]{1,0:T(8,128)S(1)} %get-tuple-element.106), channel_id=1, source_target_pairs={{0,7},{1,0},{2,1},{3,2},{4,3},{5,4},{6,5},{7,6},{8,15},{9,8},{10,9... | collective-permute-start | bytes 258056 | tf_op jit(solution)/shard_map/ppermute | solution.py:715
  46.4 3.2 %full4.1 = (f32[1,16,4,8,4,360]{5,4,3,2,1,0:T(4,128)}, f32[16,4,4,360]{3,2,1,0:T(4,128)S(1)}, f32[16,4,4,360]{3,2,1,0:T(4,128)S(1)}) custom-call(f32[22,4,32,384]{3,2,1,0:T(8,128)S(1)} %get-tuple-element.97.f_ref, f32[56,384]{1,0:T(8,128)S(1)} %collective-permute-done.8.from_south_ref, f32[56,384]{1,0:T(8,128)S(1)} %collective-permute-done.9.from_north_ref, ...), custom_call_target="tpu_custom_call" | custom-call | tf_op jit(solution)/shard_map/full4/pallas_call | solution.py:800
  49.6 2.0 %collective-permute-done.11.from_north_ref = f32[56,384]{1,0:T(8,128)S(1)} collective-permute-done((f32[56,384]{1,0:T(8,128)S(1)}, f32[56,384]{1,0:T(8,128)S(1)}, u32[]{:S(2)}, u32[]{:S(2)}) %collective-permute-start.11) | collective-permute-done | bytes 86048 | tf_op jit(solution)/shard_map/ppermute | solution.py:715
  51.6 1.0 %patch.1 = f32[1,16,4,8,4,360]{5,4,3,2,1,0:T(4,128)} custom-call(f32[1,16,4,8,4,360]{5,4,3,2,1,0:T(4,128)} %get-tuple-element.102.old_ref, f32[16,4,4,360]{3,2,1,0:T(4,128)S(1)} %get-tuple-element.103.rim_south_ref, f32[16,4,4,360]{3,2,1,0:T(4,128)S(1)} %get-tuple-element.104.rim_north_ref, ...), custom_call_target="tpu_custom_call", output_to_operand_aliasing={{}: (0, {})} | custom-call | tf_op jit(solution)/shard_map/patch/pallas_call | solution.py:807
  (13 shorter events, 0.1 us)
Async XLA Ops:
  2.6 17.4 %collective-permute-start = (f32[80,384]{1,0:T(8,128)S(1)}, f32[80,384]{1,0:T(8,128)S(1)}, u32[]{:S(2)}, u32[]{:S(2)}) collective-permute-start(f32[80,384]{1,0:T(8,128)S(1)} %get-tuple-element.56), channel_id=1, source_target_pairs={{0,248},{1,249},{2,250},{3,251},{4,252},{5,253},{6,254},{7,255},{8... | collective-permute-start | bytes 368648 | tf_op jit(solution)/shard_map/ppermute | solution.py:723
  15.6 5.3 %collective-permute-start.1 = (f32[80,384]{1,0:T(8,128)S(1)}, f32[80,384]{1,0:T(8,128)S(1)}, u32[]{:S(2)}, u32[]{:S(2)}) collective-permute-start(f32[80,384]{1,0:T(8,128)S(1)} %get-tuple-element.64), channel_id=1, source_target_pairs={{0,8},{1,9},{2,10},{3,11},{4,12},{5,13},{6,14},{7,15},{8,0},{9,1},... | collective-permute-start | bytes 368648 | tf_op jit(solution)/shard_map/ppermute | solution.py:723
  15.9 19.7 %collective-permute-start.4 = (f32[488,128]{1,0:T(8,128)S(1)}, f32[488,128]{1,0:T(8,128)S(1)}, u32[]{:S(2)}, u32[]{:S(2)}) collective-permute-start(f32[488,128]{1,0:T(8,128)S(1)} %get-tuple-element.83), channel_id=1, source_target_pairs={{0,248},{1,249},{2,250},{3,251},{4,252},{5,253},{6,254},{7,255},{8... | collective-permute-start | bytes 749576 | tf_op jit(solution)/shard_map/ppermute | solution.py:723
  19.2 16.4 %collective-permute-start.5 = (f32[488,128]{1,0:T(8,128)S(1)}, f32[488,128]{1,0:T(8,128)S(1)}, u32[]{:S(2)}, u32[]{:S(2)}) collective-permute-start(f32[488,128]{1,0:T(8,128)S(1)} %get-tuple-element.84), channel_id=1, source_target_pairs={{0,8},{1,9},{2,10},{3,11},{4,12},{5,13},{6,14},{7,15},{8,0},{9,1},... | collective-permute-start | bytes 749576 | tf_op jit(solution)/shard_map/ppermute | solution.py:723
  21.0 9.0 %collective-permute-start.2 = (f32[72,384]{1,0:T(8,128)S(1)}, f32[72,384]{1,0:T(8,128)S(1)}, u32[]{:S(2)}, u32[]{:S(2)}) collective-permute-start(f32[72,384]{1,0:T(8,128)S(1)} %get-tuple-element.76.sent_north_ref), channel_id=1, source_target_pairs={{0,1},{1,2},{2,3},{3,4},{4,5},{5,6},{6,7},{7,0},{8,9},{9,10},{10,1... | collective-permute-start | bytes 331784 | tf_op jit(solution)/shard_map/ppermute | solution.py:715
  24.9 8.1 %collective-permute-start.3 = (f32[72,384]{1,0:T(8,128)S(1)}, f32[72,384]{1,0:T(8,128)S(1)}, u32[]{:S(2)}, u32[]{:S(2)}) collective-permute-start(f32[72,384]{1,0:T(8,128)S(1)} %get-tuple-element.71.after_ref.sent_south_ref), channel_id=1, source_target_pairs={{0,7},{1,0},{2,1},{3,2},{4,3},{5,4},{6,5},{7,6},{8,15},{9,8},{10,9... | collective-permute-start | bytes 331784 | tf_op jit(solution)/shard_map/ppermute | solution.py:715
  33.6 2.1 %copy-start.1 = (bf16[320,176]{1,0:T(8,128)(2,1)S(1)}, bf16[320,176]{1,0:T(8,128)(2,1)}, u32[]{:S(2)}) copy-start(bf16[320,176]{1,0:T(8,128)(2,1)} %constant.17.clone.spread_ref) | copy-start | bytes 337924
  33.6 2.1 %copy-start.2 = (bf16[320,80]{1,0:T(8,128)(2,1)S(1)}, bf16[320,80]{1,0:T(8,128)(2,1)}, u32[]{:S(2)}) copy-start(bf16[320,80]{1,0:T(8,128)(2,1)} %constant.16.clone.spread_rim_ref) | copy-start | bytes 153604
  33.6 3.9 %collective-permute-start.6 = (f32[64,384]{1,0:T(8,128)S(1)}, f32[64,384]{1,0:T(8,128)S(1)}, u32[]{:S(2)}, u32[]{:S(2)}) collective-permute-start(f32[64,384]{1,0:T(8,128)S(1)} %get-tuple-element.91), channel_id=1, source_target_pairs={{0,1},{1,2},{2,3},{3,4},{4,5},{5,6},{6,7},{7,0},{8,9},{9,10},{10,1... | collective-permute-start | bytes 294920 | tf_op jit(solution)/shard_map/ppermute | solution.py:715
  33.7 5.4 %collective-permute-start.7 = (f32[64,384]{1,0:T(8,128)S(1)}, f32[64,384]{1,0:T(8,128)S(1)}, u32[]{:S(2)}, u32[]{:S(2)}) collective-permute-start(f32[64,384]{1,0:T(8,128)S(1)} %get-tuple-element.92), channel_id=1, source_target_pairs={{0,7},{1,0},{2,1},{3,2},{4,3},{5,4},{6,5},{7,6},{8,15},{9,8},{10,9... | collective-permute-start | bytes 294920 | tf_op jit(solution)/shard_map/ppermute | solution.py:715
  37.5 3.0 %copy-start = (f32[1,16,4,8,4,360]{5,4,3,2,1,0:T(4,128)S(1)}, f32[1,16,4,8,4,360]{5,4,3,2,1,0:T(4,128)}, u32[]{:S(2)}) copy-start(f32[1,16,4,8,4,360]{5,4,3,2,1,0:T(4,128)} %u_ref.1) | copy-start | bytes 8847364
  39.5 2.7 %collective-permute-start.8 = (f32[56,384]{1,0:T(8,128)S(1)}, f32[56,384]{1,0:T(8,128)S(1)}, u32[]{:S(2)}, u32[]{:S(2)}) collective-permute-start(f32[56,384]{1,0:T(8,128)S(1)} %get-tuple-element.99), channel_id=1, source_target_pairs={{0,1},{1,2},{2,3},{3,4},{4,5},{5,6},{6,7},{7,0},{8,9},{9,10},{10,1... | collective-permute-start | bytes 258056 | tf_op jit(solution)/shard_map/ppermute | solution.py:715
  39.6 5.5 %collective-permute-start.9 = (f32[56,384]{1,0:T(8,128)S(1)}, f32[56,384]{1,0:T(8,128)S(1)}, u32[]{:S(2)}, u32[]{:S(2)}) collective-permute-start(f32[56,384]{1,0:T(8,128)S(1)} %get-tuple-element.100), channel_id=1, source_target_pairs={{0,7},{1,0},{2,1},{3,2},{4,3},{5,4},{6,5},{7,6},{8,15},{9,8},{10,9... | collective-permute-start | bytes 258056 | tf_op jit(solution)/shard_map/ppermute | solution.py:715
  45.6 4.0 %collective-permute-start.10 = (f32[56,384]{1,0:T(8,128)S(1)}, f32[56,384]{1,0:T(8,128)S(1)}, u32[]{:S(2)}, u32[]{:S(2)}) collective-permute-start(f32[56,384]{1,0:T(8,128)S(1)} %get-tuple-element.105), channel_id=1, source_target_pairs={{0,1},{1,2},{2,3},{3,4},{4,5},{5,6},{6,7},{7,0},{8,9},{9,10},{10,1... | collective-permute-start | bytes 258056 | tf_op jit(solution)/shard_map/ppermute | solution.py:715
  45.7 5.9 %collective-permute-start.11 = (f32[56,384]{1,0:T(8,128)S(1)}, f32[56,384]{1,0:T(8,128)S(1)}, u32[]{:S(2)}, u32[]{:S(2)}) collective-permute-start(f32[56,384]{1,0:T(8,128)S(1)} %get-tuple-element.106), channel_id=1, source_target_pairs={{0,7},{1,0},{2,1},{3,2},{4,3},{5,4},{6,5},{7,6},{8,15},{9,8},{10,9... | collective-permute-start | bytes 258056 | tf_op jit(solution)/shard_map/ppermute | solution.py:715

commit v4 on v3

--- a/solution.py
+++ b/solution.py
@@ -165,7 +165,7 @@
         m = together[:, PTS * k : PTS * k + PTS]
         m_ref[jnp.where(want_west, k, EX - HALO + k)] = m
         m_hi, m_lo = halves(m)
-        q = product(m_hi, m_lo, u_ref[k].reshape(PTS, FL))
+        q = product(m_hi, m_lo, u_ref[jnp.where(want_west, k, EX - HALO + k)].reshape(PTS, FL))
         for i in range(4):
             raw[k, i] = q[32 * i : 32 * i + 32]
             part[k, i] = mass[32 * i : 32 * i + 32, k : k + 1]
@@ -179,7 +179,7 @@
             q_ref[c, i, :, FL:LANES] = jnp.broadcast_to(part[k, i], (32, TAIL))
     near = [either(want_west, left_ref[p, 0:32, :], left_ref[p, 96:128, :]) for p in range(2)]
     m_hi, m_lo = halves(product(near[0], near[1], fluxes(diff_ref, *column(f, HALO))))
-    extra = product(m_hi, m_lo, u_ref[HALO].reshape(PTS, FL))
+    extra = product(m_hi, m_lo, u_ref[jnp.where(want_west, HALO, EX - HALO - 1)].reshape(PTS, FL))
     extra_part = either(want_west, mass[0:32, HALO : HALO + 1], mass[96:128, HALO : HALO + 1])
     sub = lax.broadcasted_iota(jnp.int32, (8, LANES), 0)
     for g in range(GROUPS):
@@ -242,15 +242,13 @@
     return jnp.concatenate([either(want_west, t[:, 0:HALO], t[:, at:EX]), either(want_west, t[:, HALO : HALO + 1], t[:, at - 1 : at])], axis=1)
 
 
-def first_kernel(u_hbm, jac_hbm, xx_hbm, yy_hbm, xy_hbm, left_hbm, diff_hbm, rim_hbm, near_hbm, rim_out_ref, layers_ref, other_ref, f_ref, mass_ref, left_ref, diff_ref, rim_ref, near_ref, low_ref, high_ref, q_ref, m_ref, u_ref, jac_ref, xx_ref, yy_ref, xy_ref, sems):
+def first_kernel(u_hbm, jac_hbm, xx_hbm, yy_hbm, xy_hbm, left_hbm, diff_hbm, rim_hbm, near_hbm, rim_out_ref, layers_ref, f_ref, mass_ref, left_ref, diff_ref, rim_ref, near_ref, q_ref, m_ref, u_ref, jac_ref, xx_ref, yy_ref, xy_ref, sems):
     want_west = even_column()
-    here = jnp.where(want_west, 0, EX - HALO)
-    there = EX - HALO - here
-    here_next = jnp.where(want_west, HALO, EX - HALO - 1)
-    there_next = EX - 1 - here_next
+    size = HALO + 1
+    here = pl.ds(jnp.where(want_west, 0, EX - size), size)
     copies = fetch(
-        (jac_hbm, xx_hbm, yy_hbm, xy_hbm, left_hbm, diff_hbm, u_hbm.at[0, pl.ds(here, HALO)], u_hbm.at[0, pl.ds(here_next, 1)], u_hbm.at[0, pl.ds(there, HALO)], u_hbm.at[0, pl.ds(there_next, 1)], rim_hbm, near_hbm, u_hbm.at[0, :, :, 0], u_hbm.at[0, :, :, 7]),
-        (jac_ref, xx_ref, yy_ref, xy_ref, left_ref, diff_ref, u_ref.at[0:HALO], u_ref.at[HALO:], other_ref.at[0:HALO], other_ref.at[HALO:], rim_ref, near_ref, low_ref, high_ref),
+        (jac_hbm, xx_hbm, yy_hbm, xy_hbm, left_hbm, diff_hbm, u_hbm.at[0, here], rim_hbm, near_hbm),
+        (jac_ref, xx_ref, yy_ref, xy_ref, left_ref, diff_ref, u_ref.at[here], rim_ref, near_ref),
         sems,
     )
     for copy in copies[:6]:
@@ -260,9 +258,8 @@
         f_ref[t] = f[t]
     mass_ref[...] = mass
     copies[6].wait()
-    copies[7].wait()
     side_columns(want_west, u_ref, [nearest(want_west, t) for t in f], nearest(want_west, mass), left_ref, diff_ref, rim_out_ref, layers_ref, q_ref, m_ref)
-    for copy in copies[8:]:
+    for copy in copies[7:]:
         copy.wait()
 
 
@@ -282,7 +279,7 @@
     return [jnp.concatenate([t[32 * i + a : 32 * i + a + 4] for i in range(4) for a in (0, 28)], axis=0) for t in f]
 
 
-def rows_kernel(low_ref, high_ref, rim_ref, near_ref, f_ref, mass_ref, e_ref, south_ref, north_ref):
+def rows_kernel(u_ref, rim_ref, near_ref, f_ref, mass_ref, e_ref, south_ref, north_ref):
     f = end_rows([f_ref[t] for t in range(3)])
     for c in range(EX):
         e_ref[c] = form(rim_ref, near_ref, column(f, c))[0:8]
@@ -291,7 +288,7 @@
     outs = (south_ref, north_ref)
     carry = [None, None]
     for c in range(0, EX, 4):
-        tiles = [ref[c + k, i] for k in range(4) for i in range(4) for ref in (low_ref, high_ref)]
+        tiles = [u_ref[c + k, i, ey] for k in range(4) for i in range(4) for ey in (0, 7)]
         r = rim_product(matrices[c // 4], jnp.concatenate(tiles, axis=0))
         for side, out in enumerate(outs):
             rows = with_carry(r, side, carry[side])
@@ -339,21 +336,16 @@
     return rows + jnp.where(sub == 0, carry, 0.0)
 
 
-def own_kernel(u_hbm, after_ref, f_ref, mass_ref, left_ref, diff_ref, q_in, m_in, q_ref, m_ref, u_ref, sems):
+def own_kernel(u_ref, after_ref, f_ref, mass_ref, left_ref, diff_ref, q_in, m_in, q_ref, m_ref):
     del after_ref, q_in, m_in
     first, final = HALO, EX - HALO - 1
-    copies = fetch(
-        [u_hbm.at[0, c : c + 5] for c in range(first, final, 5)], [u_ref.at[c : c + 5] for c in range(0, 10, 5)], sems
-    )
     f = [f_ref[t] for t in range(3)]
     mass = mass_ref[...]
     for c in range(first, final + 1):
         m = form(left_ref, diff_ref, column(f, c))
         m_ref[c] = m
         m_hi, m_lo = halves(m)
-        if (c - first) % 5 == 0:
-            copies[(c - first) // 5].wait()
-        q = product(m_hi, m_lo, u_ref[c - first].reshape(PTS, FL))
+        q = product(m_hi, m_lo, u_ref[c].reshape(PTS, FL))
         for i in range(4):
             q_ref[c, i, :, 0:FL] = q[32 * i : 32 * i + 32]
             q_ref[c, i, :, FL:LANES] = jnp.broadcast_to(mass[32 * i : 32 * i + 32, c : c + 1], (32, TAIL))
@@ -733,20 +725,21 @@
     rows = lambda n: ((n, LANES), F32)
     wide = ((WIDE, 4, 32, LANES), F32)
     pinned = lambda *ts: [pltpu.with_memory_space_constraint(t, pltpu.HBM) for t in ts]
-    four = (HALO + 1, 4, 8, 4, FL)
+    every = (EX, 4, 8, 4, FL)
 
     own = [((EX, 4, 32, LANES), F32), ((EX, PTS, PTS), F32)]
-    rim_one, layers_one, other, f, mass, left_in, diff_in, rim_in, near_in, low, high, q, m = call(
+    u = state.reshape(every)
+    rim_one, layers_one, f, mass, left_in, diff_in, rim_in, near_in, q, m = call(
         first_kernel,
-        [rows(RIM), rows(32 * GROUPS), (four, F32), ((3, PTS, EX), F32), ((PTS, EX), F32), (left.shape, BF16), (diff.shape, F32), (rim.shape, BF16), (near.shape, F32), *[((EX, 4, 4, FL), F32)] * 2, *own],
+        [rows(RIM), rows(32 * GROUPS), ((3, PTS, EX), F32), ((PTS, EX), F32), (left.shape, BF16), (diff.shape, F32), (rim.shape, BF16), (near.shape, F32), *own],
         [HBM] * 9,
         "first",
-        scratch=[pltpu.VMEM(four, F32), *[pltpu.VMEM((PTS, EX), F32)] * 4, pltpu.SemaphoreType.DMA((14,))],
+        scratch=[pltpu.VMEM(every, F32), *[pltpu.VMEM((PTS, EX), F32)] * 4, pltpu.SemaphoreType.DMA((10,))],
     )(*pinned(state, *flat, left, diff, rim, near))
     one = swapped(rim_one, 1)
     rim_two, layers_two, q, m = call(
         other_kernel, [rows(RIM), rows(32 * GROUPS), *own], [VM] * 7, "other", aliases={5: 2, 6: 3}
-    )(other, f, mass, left_in, diff_in, q, m)
+    )(u, f, mass, left_in, diff_in, q, m)
     two = swapped(rim_two, 0)
     rest_one, rest_two = call(
         rest_kernel, [((PACKED, 128), F32)] * 2, [VM] * 2, "rest", scratch=[pltpu.VMEM((176, 128), F32)]
@@ -756,19 +749,18 @@
     e, own_south, own_north = call(
         rows_kernel,
         [((EX, 8, 32), F32), rows(56), rows(56)],
-        [VM] * 6,
+        [VM] * 5,
         "rows",
-    )(low, high, rim_in, near_in, f, mass)
+    )(u, rim_in, near_in, f, mass)
     to_south, to_north = call(merge_kernel, [rows(72)] * 2, [VM] * 4, "merge")(one, two, own_south, own_north)
     south1, north1 = across(to_south, to_north)
     q, m = call(
         own_kernel,
         own,
-        [HBM, ANY] + [VM] * 6,
+        [VM, ANY] + [VM] * 6,
         "own",
-        scratch=[pltpu.VMEM((10, 4, 8, 4, FL), F32), pltpu.SemaphoreType.DMA((2,))],
         aliases={6: 0, 7: 1},
-    )(*pinned(state), to_south, f, mass, left_in, diff_in, q, m)
+    )(u, to_south, f, mass, left_in, diff_in, q, m)
     mh, halo_e, west, east, quads = call(
         halo_kernel,
         [((2 * HALO, PTS, PTS), F32), ((2 * HALO, 8, 32), F32), rows(RIM), rows(RIM), ((QUADS, 64, 2 * PTS), BF16)],

time: 52.8 us -> 52.9 us (level)
  waiting for transfers between devices: 10.4 us -> 11.7 us
  Pallas kernels: 20.5 us -> 19.4 us
    ppermute x8, waiting for transfers between devices: 9.47 us -> 10.7 us  [moved(): return lax.ppermute(array, AXES, pairs)]
    pallas_call x3, Pallas kernels: 7.35 us -> 6.39 us  [the longest x1 2.84 us: per_device(): call(own_kernel, own, [VM, ANY] + [VM] * 6, 'own', aliases={6: 0, 7: 1})]
  transfers between devices with their start and end apart: 12 -> 12, of which waited for: 5 -> 5; matrix products, arithmetic and copies ran while one was open for 0% -> 0% of each run, Pallas kernels for 30% -> 28%
where the time goes in v4:
time: 52.9 us; the launch traced here: 52.8 us
  starting transfers between devices  21.3 us (40%)
  Pallas kernels  19.4 us (37%)
  waiting for transfers between devices  11.7 us (22%)
    ppermute x4, starting transfers between devices, swapped(): return lax.ppermute(array, AXES, pairs)  15.2 us
    ppermute x8, waiting for transfers between devices, moved(): return lax.ppermute(array, AXES, pairs)  10.7 us
    ppermute x8, starting transfers between devices, moved(): return lax.ppermute(array, AXES, pairs)  6.18 us
    pallas_call x1, Pallas kernels, per_device(): call(fourth_full, [((1, EX, 4, 8, 4, FL), F32), ((EX, 4, 4, FL), F32), ((...  3.19 us
    pallas_call x1, Pallas kernels, per_device(): call(own_kernel, own, [VM, ANY] + [VM] * 6, 'own', aliases={6: 0, 7: 1})  2.84 us
    pallas_call x1, Pallas kernels, per_device(): call(first_kernel, [rows(RIM), rows(32 * GROUPS), ((3, PTS, EX), F32), ((...  2.75 us
    pallas_call x1, Pallas kernels, per_device(): call(second_outer, [((8, 4, 32, LANES), F32), ((2, 32, LANES), F32), *mat...  1.77 us
    pallas_call x1, Pallas kernels, per_device(): call(third_full, [wide, ((EX, PTS, FL), F32)], [VM] * 10, 'full3')  1.74 us
  transfers between devices with their start and end apart: 12, of which 5 were waited for; matrix products, arithmetic and copies ran while one was open for 0% of the time, Pallas kernels for 28%

profile of v4, /device:TPU:1, one launch (start us, length us, event | category | flops | bytes accessed | tf_op | source)
XLA Modules:
  0.0 52.8 jit_solution(726466707282402070)
XLA Ops:
  0.0 2.7 %first.1 = (f32[80,384]{1,0:T(8,128)S(1)}, f32[320,384]{1,0:T(8,128)S(1)}, f32[3,128,16]{2,1,0:T(8,128)S(1)}, f32[128,16]{1,0:T(8,128)S(1)}, bf16[2,128,256]{2,1...) custom-call(f32[1,16,4,8,4,360]{5,4,3,2,1,0:T(4,128)} %u_ref.1, ...), custom_call_target="tpu_custom_call" | custom-call | tf_op jit(solution)/shard_map/first/pallas_call | solution.py:732
  2.8 11.8 %collective-permute-start = (f32[80,384]{1,0:T(8,128)S(1)}, f32[80,384]{1,0:T(8,128)S(1)}, u32[]{:S(2)}, u32[]{:S(2)}) collective-permute-start(f32[80,384]{1,0:T(8,128)S(1)} %get-tuple-element.53), channel_id=1, source_target_pairs={{0,248},{1,249},{2,250},{3,251},{4,252},{5,253},{6,254},{7,255},{8... | collective-permute-start | bytes 368648 | tf_op jit(solution)/shard_map/ppermute | solution.py:715
  14.5 1.2 %other.1 = (f32[80,384]{1,0:T(8,128)S(1)}, f32[320,384]{1,0:T(8,128)S(1)}, f32[16,4,32,384]{3,2,1,0:T(8,128)S(1)}, f32[16,128,128]{2,1,0:T(8,128)S(1)}) custom-call(f32[16,4,8,4,360]{4,3,2,1,0:T(4,128)S(1)} %bitcast.21, f32[3,128,16]{2,1,0:T(8,128)S(1)} %get-tuple-element.54.f_ref, ...), custom_call_target="tpu_custom_call", output_to_operand_aliasing={{2}: (5, {}), {3}: (6, {})} | custom-call | tf_op jit(solution)/shard_map/other/pallas_call | solution.py:740
  15.8 0.1 collective-permute-start.1
  15.9 0.2 rest.1
  16.0 3.3 %collective-permute-start.4 = (f32[488,128]{1,0:T(8,128)S(1)}, f32[488,128]{1,0:T(8,128)S(1)}, u32[]{:S(2)}, u32[]{:S(2)}) collective-permute-start(f32[488,128]{1,0:T(8,128)S(1)} %get-tuple-element.77), channel_id=1, source_target_pairs={{0,248},{1,249},{2,250},{3,251},{4,252},{5,253},{6,254},{7,255},{8... | collective-permute-start | bytes 749576 | tf_op jit(solution)/shard_map/ppermute | solution.py:715
  19.3 0.8 %rows.1 = (f32[16,8,32]{2,1,0:T(8,128)S(1)}, f32[56,384]{1,0:T(8,128)S(1)}, f32[56,384]{1,0:T(8,128)S(1)}) custom-call(f32[16,4,8,4,360]{4,3,2,1,0:T(4,128)S(1)} %bitcast.22, bf16[2,16,64]{2,1,0:T(8,128)(2,1)S(1)} %get-tuple-element.61.rim_ref, f32[2,32,32]{2,1,0:T(8,128)S(1)} %get-tuple-element.62.near_ref, f32[3,128,16]{2,1,0:T(8,128)S(1)} %get-tuple-element.54.f_ref, ...), custom_call_target="tpu_custom_call" | custom-call | tf_op jit(solution)/shard_map/rows/pallas_call | solution.py:749
  20.1 0.0 collective-permute-done.one_ref
  20.2 0.9 %collective-permute-done.1.two_ref = f32[80,384]{1,0:T(8,128)S(1)} collective-permute-done((f32[80,384]{1,0:T(8,128)S(1)}, f32[80,384]{1,0:T(8,128)S(1)}, u32[]{:S(2)}, u32[]{:S(2)}) %collective-permute-start.1) | collective-permute-done | bytes 122912 | tf_op jit(solution)/shard_map/ppermute | solution.py:715
  21.1 3.9 %collective-permute-start.2 = (f32[72,384]{1,0:T(8,128)S(1)}, f32[72,384]{1,0:T(8,128)S(1)}, u32[]{:S(2)}, u32[]{:S(2)}) collective-permute-start(f32[72,384]{1,0:T(8,128)S(1)} %get-tuple-element.70.sent_north_ref), channel_id=1, source_target_pairs={{0,1},{1,2},{2,3},{3,4},{4,5},{5,6},{6,7},{7,0},{8,9},{9,10},{10,1... | collective-permute-start | bytes 331784 | tf_op jit(solution)/shard_map/ppermute | solution.py:707
  25.1 2.8 %own.1 = (f32[16,4,32,384]{3,2,1,0:T(8,128)S(1)}, f32[16,128,128]{2,1,0:T(8,128)S(1)}) custom-call(f32[16,4,8,4,360]{4,3,2,1,0:T(4,128)S(1)} %bitcast.23, f32[72,384]{1,0:T(8,128)S(1)} %get-tuple-element.65.after_ref.sent_south_ref, f32[3,128,16]{2,1,0:T(8,128)S(1)} %get-tuple-element.54.f_ref, ...), custom_call_target="tpu_custom_call", output_to_operand_aliasing={{0}: (6, {}), {1}: (7, {})} | custom-call | tf_op jit(solution)/shard_map/own/pallas_call | solution.py:757
  27.9 1.1 %halo.1 = (f32[6,128,128]{2,1,0:T(8,128)S(1)}, f32[6,8,32]{2,1,0:T(8,128)S(1)}, f32[80,384]{1,0:T(8,128)S(1)}, f32[80,384]{1,0:T(8,128)S(1)}, bf16[6,64,256]{2,1,0:T(8,128)(2,1)S(1)}) custom-call(f32[80,384]{1,0:T(8,128)S(1)} %collective-permute-done.one_ref, f32[80,384]{1,0:T(8,128)S(1)} %collective-permute-done.1.two_ref, ...), custom_call_target="tpu_custom_call" | custom-call | tf_op jit(solution)/shard_map/halo/pallas_call | solution.py:764
  29.1 4.0 %collective-permute-done.3.from_north_ref = f32[72,384]{1,0:T(8,128)S(1)} collective-permute-done((f32[72,384]{1,0:T(8,128)S(1)}, f32[72,384]{1,0:T(8,128)S(1)}, u32[]{:S(2)}, u32[]{:S(2)}) %collective-permute-start.3) | collective-permute-done | bytes 110624 | tf_op jit(solution)/shard_map/ppermute | solution.py:707
  33.1 0.5 edges2.1
  33.6 0.0 copy-start.1
  33.7 0.0 copy-start.2
  33.7 0.1 collective-permute-start.6
  33.8 0.5 collective-permute-start.7
  34.3 1.4 %inner2.1 = (f32[14,4,32,384]{3,2,1,0:T(8,128)S(1)}, bf16[14,128,256]{2,1,0:T(8,128)(2,1)S(1)}, bf16[14,128,128]{2,1,0:T(8,128)(2,1)S(1)}, f32[14,8,32]{2,1,0:T(8,128)S(1)}) custom-call(f32[16,4,32,384]{3,2,1,0:T(8,128)S(1)} %get-tuple-element.68.q_ref, f32[16,8,32]{2,1,0:T(8,128)S(1)} %get-tuple-element.69.e_ref.own_e_ref, ...), custom_call_target="tpu_custom_call" | custom-call | tf_op jit(solution)/shard_map/inner2/pallas_call | solution.py:775
  35.7 1.8 %outer2.1 = (f32[8,4,32,384]{3,2,1,0:T(8,128)S(1)}, f32[2,32,384]{2,1,0:T(8,128)S(1)}, bf16[8,128,256]{2,1,0:T(8,128)(2,1)S(1)}, bf16[8,128,128]{2,1,0:T(8,128)(...) custom-call(f32[16,4,32,384]{3,2,1,0:T(8,128)S(1)} %get-tuple-element.68.q_ref, ...), custom_call_target="tpu_custom_call" | custom-call | tf_op jit(solution)/shard_map/outer2/pallas_call | solution.py:778
  37.5 1.7 %collective-permute-done.7.from_north_ref = f32[64,384]{1,0:T(8,128)S(1)} collective-permute-done((f32[64,384]{1,0:T(8,128)S(1)}, f32[64,384]{1,0:T(8,128)S(1)}, u32[]{:S(2)}, u32[]{:S(2)}) %collective-permute-start.7) | collective-permute-done | bytes 98336 | tf_op jit(solution)/shard_map/ppermute | solution.py:707
  39.2 0.4 edges3.1
  39.6 0.1 collective-permute-start.8
  39.7 0.8 %collective-permute-start.9 = (f32[56,384]{1,0:T(8,128)S(1)}, f32[56,384]{1,0:T(8,128)S(1)}, u32[]{:S(2)}, u32[]{:S(2)}) collective-permute-start(f32[56,384]{1,0:T(8,128)S(1)} %get-tuple-element.94), channel_id=1, source_target_pairs={{0,7},{1,0},{2,1},{3,2},{4,3},{5,4},{6,5},{7,6},{8,15},{9,8},{10,9... | collective-permute-start | bytes 258056 | tf_op jit(solution)/shard_map/ppermute | solution.py:707
  40.5 1.7 %full3.1 = (f32[22,4,32,384]{3,2,1,0:T(8,128)S(1)}, f32[16,128,360]{2,1,0:T(8,128)S(1)}) custom-call(f32[14,4,32,384]{3,2,1,0:T(8,128)S(1)} %get-tuple-element.72.inner_ref, f32[8,4,32,384]{3,2,1,0:T(8,128)S(1)} %get-tuple-element.82.outer_ref, f32[2,32,384]{2,1,0:T(8,128)S(1)} %get-tuple-element.83.joint_ref, ...), custom_call_target="tpu_custom_call" | custom-call | tf_op jit(solution)/shard_map/full3/pallas_call | solution.py:785
  42.3 3.0 %collective-permute-done.9.from_north_ref = f32[56,384]{1,0:T(8,128)S(1)} collective-permute-done((f32[56,384]{1,0:T(8,128)S(1)}, f32[56,384]{1,0:T(8,128)S(1)}, u32[]{:S(2)}, u32[]{:S(2)}) %collective-permute-start.9) | collective-permute-done | bytes 86048 | tf_op jit(solution)/shard_map/ppermute | solution.py:707
  45.3 0.4 edges4.1
  45.7 0.1 collective-permute-start.10
  45.8 0.7 %collective-permute-start.11 = (f32[56,384]{1,0:T(8,128)S(1)}, f32[56,384]{1,0:T(8,128)S(1)}, u32[]{:S(2)}, u32[]{:S(2)}) collective-permute-start(f32[56,384]{1,0:T(8,128)S(1)} %get-tuple-element.100), channel_id=1, source_target_pairs={{0,7},{1,0},{2,1},{3,2},{4,3},{5,4},{6,5},{7,6},{8,15},{9,8},{10,9... | collective-permute-start | bytes 258056 | tf_op jit(solution)/shard_map/ppermute | solution.py:707
  46.5 3.2 %full4.1 = (f32[1,16,4,8,4,360]{5,4,3,2,1,0:T(4,128)}, f32[16,4,4,360]{3,2,1,0:T(4,128)S(1)}, f32[16,4,4,360]{3,2,1,0:T(4,128)S(1)}) custom-call(f32[22,4,32,384]{3,2,1,0:T(8,128)S(1)} %get-tuple-element.91.f_ref, f32[56,384]{1,0:T(8,128)S(1)} %collective-permute-done.8.from_south_ref, f32[56,384]{1,0:T(8,128)S(1)} %collective-permute-done.9.from_north_ref, ...), custom_call_target="tpu_custom_call" | custom-call | tf_op jit(solution)/shard_map/full4/pallas_call | solution.py:792
  49.6 2.0 %collective-permute-done.11.from_north_ref = f32[56,384]{1,0:T(8,128)S(1)} collective-permute-done((f32[56,384]{1,0:T(8,128)S(1)}, f32[56,384]{1,0:T(8,128)S(1)}, u32[]{:S(2)}, u32[]{:S(2)}) %collective-permute-start.11) | collective-permute-done | bytes 86048 | tf_op jit(solution)/shard_map/ppermute | solution.py:707
  51.7 1.0 %patch.1 = f32[1,16,4,8,4,360]{5,4,3,2,1,0:T(4,128)} custom-call(f32[1,16,4,8,4,360]{5,4,3,2,1,0:T(4,128)} %get-tuple-element.96.old_ref, f32[16,4,4,360]{3,2,1,0:T(4,128)S(1)} %get-tuple-element.97.rim_south_ref, f32[16,4,4,360]{3,2,1,0:T(4,128)S(1)} %get-tuple-element.98.rim_north_ref, ...), custom_call_target="tpu_custom_call", output_to_operand_aliasing={{}: (0, {})} | custom-call | tf_op jit(solution)/shard_map/patch/pallas_call | solution.py:799
  (13 shorter events, 0.1 us)
Async XLA Ops:
  0.0 14.5 %copy-start = (f32[1,16,4,8,4,360]{5,4,3,2,1,0:T(4,128)S(1)}, f32[1,16,4,8,4,360]{5,4,3,2,1,0:T(4,128)}, u32[]{:S(2)}) copy-start(f32[1,16,4,8,4,360]{5,4,3,2,1,0:T(4,128)} %u_ref.1) | copy-start | bytes 8847364
  2.8 17.4 %collective-permute-start = (f32[80,384]{1,0:T(8,128)S(1)}, f32[80,384]{1,0:T(8,128)S(1)}, u32[]{:S(2)}, u32[]{:S(2)}) collective-permute-start(f32[80,384]{1,0:T(8,128)S(1)} %get-tuple-element.53), channel_id=1, source_target_pairs={{0,248},{1,249},{2,250},{3,251},{4,252},{5,253},{6,254},{7,255},{8... | collective-permute-start | bytes 368648 | tf_op jit(solution)/shard_map/ppermute | solution.py:715
  15.8 5.3 %collective-permute-start.1 = (f32[80,384]{1,0:T(8,128)S(1)}, f32[80,384]{1,0:T(8,128)S(1)}, u32[]{:S(2)}, u32[]{:S(2)}) collective-permute-start(f32[80,384]{1,0:T(8,128)S(1)} %get-tuple-element.60), channel_id=1, source_target_pairs={{0,8},{1,9},{2,10},{3,11},{4,12},{5,13},{6,14},{7,15},{8,0},{9,1},... | collective-permute-start | bytes 368648 | tf_op jit(solution)/shard_map/ppermute | solution.py:715
  16.0 19.7 %collective-permute-start.4 = (f32[488,128]{1,0:T(8,128)S(1)}, f32[488,128]{1,0:T(8,128)S(1)}, u32[]{:S(2)}, u32[]{:S(2)}) collective-permute-start(f32[488,128]{1,0:T(8,128)S(1)} %get-tuple-element.77), channel_id=1, source_target_pairs={{0,248},{1,249},{2,250},{3,251},{4,252},{5,253},{6,254},{7,255},{8... | collective-permute-start | bytes 749576 | tf_op jit(solution)/shard_map/ppermute | solution.py:715
  19.3 16.4 %collective-permute-start.5 = (f32[488,128]{1,0:T(8,128)S(1)}, f32[488,128]{1,0:T(8,128)S(1)}, u32[]{:S(2)}, u32[]{:S(2)}) collective-permute-start(f32[488,128]{1,0:T(8,128)S(1)} %get-tuple-element.78), channel_id=1, source_target_pairs={{0,8},{1,9},{2,10},{3,11},{4,12},{5,13},{6,14},{7,15},{8,0},{9,1},... | collective-permute-start | bytes 749576 | tf_op jit(solution)/shard_map/ppermute | solution.py:715
  21.1 7.9 %collective-permute-start.2 = (f32[72,384]{1,0:T(8,128)S(1)}, f32[72,384]{1,0:T(8,128)S(1)}, u32[]{:S(2)}, u32[]{:S(2)}) collective-permute-start(f32[72,384]{1,0:T(8,128)S(1)} %get-tuple-element.70.sent_north_ref), channel_id=1, source_target_pairs={{0,1},{1,2},{2,3},{3,4},{4,5},{5,6},{6,7},{7,0},{8,9},{9,10},{10,1... | collective-permute-start | bytes 331784 | tf_op jit(solution)/shard_map/ppermute | solution.py:707
  25.1 8.1 %collective-permute-start.3 = (f32[72,384]{1,0:T(8,128)S(1)}, f32[72,384]{1,0:T(8,128)S(1)}, u32[]{:S(2)}, u32[]{:S(2)}) collective-permute-start(f32[72,384]{1,0:T(8,128)S(1)} %get-tuple-element.65.after_ref.sent_south_ref), channel_id=1, source_target_pairs={{0,7},{1,0},{2,1},{3,2},{4,3},{5,4},{6,5},{7,6},{8,15},{9,8},{10,9... | collective-permute-start | bytes 331784 | tf_op jit(solution)/shard_map/ppermute | solution.py:707
  33.6 2.1 %copy-start.1 = (bf16[320,176]{1,0:T(8,128)(2,1)S(1)}, bf16[320,176]{1,0:T(8,128)(2,1)}, u32[]{:S(2)}) copy-start(bf16[320,176]{1,0:T(8,128)(2,1)} %constant.17.clone.spread_ref) | copy-start | bytes 337924
  33.7 2.1 %copy-start.2 = (bf16[320,80]{1,0:T(8,128)(2,1)S(1)}, bf16[320,80]{1,0:T(8,128)(2,1)}, u32[]{:S(2)}) copy-start(bf16[320,80]{1,0:T(8,128)(2,1)} %constant.16.clone.spread_rim_ref) | copy-start | bytes 153604
  33.7 3.8 %collective-permute-start.6 = (f32[64,384]{1,0:T(8,128)S(1)}, f32[64,384]{1,0:T(8,128)S(1)}, u32[]{:S(2)}, u32[]{:S(2)}) collective-permute-start(f32[64,384]{1,0:T(8,128)S(1)} %get-tuple-element.85), channel_id=1, source_target_pairs={{0,1},{1,2},{2,3},{3,4},{4,5},{5,6},{6,7},{7,0},{8,9},{9,10},{10,1... | collective-permute-start | bytes 294920 | tf_op jit(solution)/shard_map/ppermute | solution.py:707
  33.8 5.4 %collective-permute-start.7 = (f32[64,384]{1,0:T(8,128)S(1)}, f32[64,384]{1,0:T(8,128)S(1)}, u32[]{:S(2)}, u32[]{:S(2)}) collective-permute-start(f32[64,384]{1,0:T(8,128)S(1)} %get-tuple-element.86), channel_id=1, source_target_pairs={{0,7},{1,0},{2,1},{3,2},{4,3},{5,4},{6,5},{7,6},{8,15},{9,8},{10,9... | collective-permute-start | bytes 294920 | tf_op jit(solution)/shard_map/ppermute | solution.py:707
  39.6 2.6 %collective-permute-start.8 = (f32[56,384]{1,0:T(8,128)S(1)}, f32[56,384]{1,0:T(8,128)S(1)}, u32[]{:S(2)}, u32[]{:S(2)}) collective-permute-start(f32[56,384]{1,0:T(8,128)S(1)} %get-tuple-element.93), channel_id=1, source_target_pairs={{0,1},{1,2},{2,3},{3,4},{4,5},{5,6},{6,7},{7,0},{8,9},{9,10},{10,1... | collective-permute-start | bytes 258056 | tf_op jit(solution)/shard_map/ppermute | solution.py:707
  39.7 5.6 %collective-permute-start.9 = (f32[56,384]{1,0:T(8,128)S(1)}, f32[56,384]{1,0:T(8,128)S(1)}, u32[]{:S(2)}, u32[]{:S(2)}) collective-permute-start(f32[56,384]{1,0:T(8,128)S(1)} %get-tuple-element.94), channel_id=1, source_target_pairs={{0,7},{1,0},{2,1},{3,2},{4,3},{5,4},{6,5},{7,6},{8,15},{9,8},{10,9... | collective-permute-start | bytes 258056 | tf_op jit(solution)/shard_map/ppermute | solution.py:707
  45.7 4.0 %collective-permute-start.10 = (f32[56,384]{1,0:T(8,128)S(1)}, f32[56,384]{1,0:T(8,128)S(1)}, u32[]{:S(2)}, u32[]{:S(2)}) collective-permute-start(f32[56,384]{1,0:T(8,128)S(1)} %get-tuple-element.99), channel_id=1, source_target_pairs={{0,1},{1,2},{2,3},{3,4},{4,5},{5,6},{6,7},{7,0},{8,9},{9,10},{10,1... | collective-permute-start | bytes 258056 | tf_op jit(solution)/shard_map/ppermute | solution.py:707
  45.8 5.9 %collective-permute-start.11 = (f32[56,384]{1,0:T(8,128)S(1)}, f32[56,384]{1,0:T(8,128)S(1)}, u32[]{:S(2)}, u32[]{:S(2)}) collective-permute-start(f32[56,384]{1,0:T(8,128)S(1)} %get-tuple-element.100), channel_id=1, source_target_pairs={{0,7},{1,0},{2,1},{3,2},{4,3},{5,4},{6,5},{7,6},{8,15},{9,8},{10,9... | collective-permute-start | bytes 258056 | tf_op jit(solution)/shard_map/ppermute | solution.py:707
